TPU v7x, 32 devices: a whole 2x2x4 slice. The times are simulated.
32 devices in a mesh: dp: 4 (over z), ctx: 8 (over y, x, core).
Axes of the slice: x: 2, y: 2, z: 4, core: 2. Of those that a mesh axis runs over, the one named last changes fastest.
Arguments:
- tokens: bfloat16 [4, 1024, 2048], P('dp', 'ctx'), may hold values from -6 to 6
- cotangent: bfloat16 [4, 1024, 2048], P('dp', 'ctx'), may hold values from -6 to 6
- block_ids: int32 [16], replicated, may hold values from 0 to 15, as said below
- attn_weight: float32 [2048, 8192], P(('dp', 'ctx')), may hold values from -1.06066017 to 1.06066017
- gate_up: float32 [2048, 16384], P(('dp', 'ctx')), may hold values from -0.125 to 0.125
- down_weight: float32 [8192, 2048], P(('dp', 'ctx')), may hold values from -0.0625 to 0.0625
- norm_gains: float32 [2, 2048], P(None, ('dp', 'ctx')), may hold values from 0.25 to 1.75
- attn_first: float32 [2048, 8192], P(('dp', 'ctx')), may hold values from -25.6 to 25.6
- attn_second: float32 [2048, 8192], P(('dp', 'ctx')), may hold values from 2.048 to 311.296
- gate_first: float32 [2048, 16384], P(('dp', 'ctx')), may hold values from -12.8 to 12.8
- gate_second: float32 [2048, 16384], P(('dp', 'ctx')), may hold values from 19.6608 to 77.824
- down_first: float32 [8192, 2048], P(('dp', 'ctx')), may hold values from -25.6 to 25.6
- down_second: float32 [8192, 2048], P(('dp', 'ctx')), may hold values from 77.824 to 311.296
- gain_first: float32 [2, 2048], P(None, ('dp', 'ctx')), may hold values from -42.24 to 42.24
- gain_second: float32 [2, 2048], P(None, ('dp', 'ctx')), may hold values from 217.088 to 860.16
Outputs:
- activations: bfloat16 [4, 1024, 2048], P('dp', 'ctx')
- input_grad: bfloat16 [4, 1024, 2048], P('dp', 'ctx')
- attn_grad: float32 [2048, 8192], P(('dp', 'ctx'))
- gate_grad: float32 [2048, 16384], P(('dp', 'ctx'))
- down_grad: float32 [8192, 2048], P(('dp', 'ctx'))
- gain_grad: float32 [2, 2048], P(None, ('dp', 'ctx'))
- attn_new: float32 [2048, 8192], P(('dp', 'ctx'))
- gate_new: float32 [2048, 16384], P(('dp', 'ctx'))
- down_new: float32 [8192, 2048], P(('dp', 'ctx'))
- gain_new: float32 [2, 2048], P(None, ('dp', 'ctx'))
- attn_moment: float32 [2048, 8192], P(('dp', 'ctx'))
- gate_moment: float32 [2048, 16384], P(('dp', 'ctx'))
- down_moment: float32 [8192, 2048], P(('dp', 'ctx'))
- gain_moment: float32 [2, 2048], P(None, ('dp', 'ctx'))
- attn_square: float32 [2048, 8192], P(('dp', 'ctx'))
- gate_square: float32 [2048, 16384], P(('dp', 'ctx'))
- down_square: float32 [8192, 2048], P(('dp', 'ctx'))
- gain_square: float32 [2, 2048], P(None, ('dp', 'ctx'))
Inputs may be any that keep to these rules, and one draw needn't show every extreme that they name: `block_ids`: slots 2c and 2c + 1 (the rows of device c of ctx) hold a block b and the block 15 - b; every block of a sequence appears once, the same for all sequences.
All inputs are finite; a program needn't handle non-finite values.
Results may differ from a plain program's by a relative error of at most 0.015.
Values may be sent and summed in bfloat16 or wider, within the bound.
No kernel may reach another device: no remote copies, remote signals or barrier semaphores. Data moves between devices by JAX's collectives and lax.ppermute only.
A program may use at most 704 MiB of HBM per device.

v0:
```python
import math

import jax
import jax.numpy as jnp
from jax import lax
from jax.sharding import PartitionSpec as P

D = 2048
HEADS = 32
HEAD = 64
FF = 8192
STEP = 5


norm_eps = 1e-05
rope_base = 130000.0
beta_one = 0.9
beta_two = 0.95
adam_eps = 1e-08
decay_rate = 0.1
gain_rate = 0.4
masked = -1e30


def rms_scale(values):
    return lax.rsqrt(jnp.mean(values * values, axis=-1, keepdims=True) + norm_eps)


def angles(positions):
    index = jnp.arange(HEAD // 2, dtype=jnp.float32)
    freqs = jnp.power(jnp.float32(rope_base), -2.0 * index / HEAD)
    phase = positions.astype(jnp.float32)[:, None] * freqs[None, :]
    phase = jnp.concatenate([phase, phase], axis=-1)
    return (jnp.cos(phase)[:, None, :], jnp.sin(phase)[:, None, :])


def rotate(values, cosine, sine):
    middle = values.shape[-1] // 2
    turned = jnp.concatenate([-values[..., middle:], values[..., :middle]], axis=-1)
    return values * cosine + turned * sine


def unrotate(values, cosine, sine):
    middle = values.shape[-1] // 2
    sined = values * sine
    turned = jnp.concatenate([sined[..., middle:], -sined[..., :middle]], axis=-1)
    return values * cosine + turned


def contract_last(first, second):
    return lax.dot_general(
        first, second, (((1,), (1,)), ((), ())), preferred_element_type=jnp.float32
    )


def contract_first(first, second):
    return lax.dot_general(
        first, second, (((0,), (0,)), ((), ())), preferred_element_type=jnp.float32
    )


def adam_step(weight, grad, first, second, rate, decay):
    first = beta_one * first + (1.0 - beta_one) * grad
    second = beta_two * second + (1.0 - beta_two) * grad * grad
    corrected_first = first / (1.0 - beta_one**STEP)
    corrected_second = second / (1.0 - beta_two**STEP)
    fresh = weight - rate * (
        corrected_first / (jnp.sqrt(corrected_second) + adam_eps) + decay * weight
    )
    return (fresh, first, second)


def body(
    tokens,
    cotangent,
    block_ids,
    attn_weight,
    gate_up,
    down_weight,
    norm_gains,
    attn_first,
    attn_second,
    gate_first,
    gate_second,
    down_first,
    down_second,
    gain_first,
    gain_second,
):
    width = attn_weight.shape[1] // 4
    hidden_width = gate_up.shape[1] // 2
    context_size = lax.axis_size("ctx")
    rows = tokens.shape[1]
    half = rows // 2
    seq_len = rows * context_size
    scale = HEAD ** (-0.5)
    all_pos = (block_ids[:, None] * half + jnp.arange(half, dtype=jnp.int32)[None, :]).reshape(-1)
    own_pos = lax.dynamic_slice_in_dim(all_pos, lax.axis_index("ctx") * rows, rows)
    group = 4
    span = group * rows
    blocks = seq_len // span
    key_pos = all_pos.reshape(blocks, span)
    cosine, sine = angles(own_pos)
    inputs = tokens[0].astype(jnp.float32)
    attn_full, gains_low = (
        lax.all_gather(attn_weight.astype(jnp.bfloat16), ("dp", "ctx"), axis=0, tiled=True),
        lax.all_gather(norm_gains.astype(jnp.bfloat16), ("dp", "ctx"), axis=1, tiled=True),
    )
    gain_one = gains_low[0].astype(jnp.float32)
    gain_two = gains_low[1].astype(jnp.float32)
    inv_one = rms_scale(inputs)
    normed_one = inputs * inv_one
    hidden_one = (normed_one * gain_one).astype(jnp.bfloat16)
    projected = jnp.dot(hidden_one, attn_full[:, : 3 * width], preferred_element_type=jnp.float32)
    queries = rotate(projected[:, :width].reshape(rows, HEADS, HEAD), cosine, sine).astype(
        jnp.bfloat16
    )
    keys_own = (
        rotate(projected[:, width : 2 * width].reshape(rows, HEADS, HEAD), cosine, sine)
        .astype(jnp.bfloat16)
        .reshape(rows, width)
    )
    values_own = projected[:, 2 * width :].astype(jnp.bfloat16)
    keys_all, values_all = (
        lax.all_gather(keys_own, "ctx", axis=0, tiled=True),
        lax.all_gather(values_own, "ctx", axis=0, tiled=True),
    )
    key_blocks = keys_all.reshape(blocks, span, HEADS, HEAD)
    value_blocks = values_all.reshape(blocks, span, HEADS, HEAD)

    def block_scores(key_block, position_block):
        scores = (
            jnp.einsum("qhd,khd->hqk", queries, key_block, preferred_element_type=jnp.float32)
            * scale
        )
        return jnp.where((position_block[None, :] <= own_pos[:, None])[None], scores, masked)

    def stat_step(carry, piece):
        run_max, run_sum = carry
        key_block, position_block = piece
        scores = block_scores(key_block, position_block)
        new_max = jnp.maximum(run_max, jnp.max(scores, axis=-1))
        run_sum = run_sum * jnp.exp(run_max - new_max) + jnp.sum(
            jnp.exp(scores - new_max[..., None]), axis=-1
        )
        return ((new_max, run_sum), None)

    start_stats = (
        jnp.full((HEADS, rows), masked, jnp.float32),
        jnp.zeros((HEADS, rows), jnp.float32),
    )
    (run_max, run_sum), _ = lax.scan(stat_step, start_stats, (key_blocks, key_pos))
    log_total = run_max + jnp.log(run_sum)

    def mix_step(total, piece):
        key_block, value_block, position_block = piece
        weights = jnp.exp(block_scores(key_block, position_block) - log_total[..., None]).astype(
            jnp.bfloat16
        )
        return (
            total
            + jnp.einsum("hqk,khd->qhd", weights, value_block, preferred_element_type=jnp.float32),
            None,
        )

    mixed, _ = lax.scan(
        mix_step, jnp.zeros((rows, HEADS, HEAD), jnp.float32), (key_blocks, value_blocks, key_pos)
    )
    mixed_low = mixed.reshape(rows, width).astype(jnp.bfloat16)
    after = inputs + jnp.dot(
        mixed_low, attn_full[:, 3 * width :], preferred_element_type=jnp.float32
    )
    gate_full, down_full = (
        lax.all_gather(gate_up.astype(jnp.bfloat16), ("dp", "ctx"), axis=0, tiled=True),
        lax.all_gather(down_weight.astype(jnp.bfloat16), ("dp", "ctx"), axis=0, tiled=True),
    )
    inv_two = rms_scale(after)
    normed_two = after * inv_two
    hidden_two = (normed_two * gain_two).astype(jnp.bfloat16)
    gate_both = jnp.dot(hidden_two, gate_full, preferred_element_type=jnp.float32)
    gate_part = gate_both[:, :hidden_width]
    up_part = gate_both[:, hidden_width:]
    gate_sigmoid = jax.nn.sigmoid(gate_part)
    gate_act = gate_part * gate_sigmoid
    activation = (gate_act * up_part).astype(jnp.bfloat16)
    outputs = after + jnp.dot(activation, down_full, preferred_element_type=jnp.float32)
    grad_out = cotangent[0]
    grad_f32 = grad_out.astype(jnp.float32)
    gate_back, down_back = (
        lax.all_gather(gate_up.astype(jnp.bfloat16), ("dp", "ctx"), axis=0, tiled=True),
        lax.all_gather(down_weight.astype(jnp.bfloat16), ("dp", "ctx"), axis=0, tiled=True),
    )
    grad_act = contract_last(grad_out, down_back)
    grad_gate = (
        grad_act * up_part * gate_sigmoid * (1.0 + gate_part * (1.0 - gate_sigmoid))
    ).astype(jnp.bfloat16)
    grad_up = (grad_act * gate_act).astype(jnp.bfloat16)
    grad_both = jnp.concatenate([grad_gate, grad_up], axis=1)
    grad_two = contract_last(grad_both, gate_back)
    gate_grad = lax.psum_scatter(
        contract_first(hidden_two, grad_both), ("dp", "ctx"), scatter_dimension=0, tiled=True
    )
    reduced_two = grad_two * gain_two
    grad_gain_two = jnp.sum(grad_two * normed_two, axis=0)
    grad_after = grad_f32 + inv_two * (
        reduced_two - normed_two * jnp.mean(reduced_two * normed_two, axis=-1, keepdims=True)
    )
    attn_back = lax.all_gather(attn_weight.astype(jnp.bfloat16), ("dp", "ctx"), axis=0, tiled=True)
    after_low = grad_after.astype(jnp.bfloat16)
    grad_mixed = (
        contract_last(after_low, attn_back[:, 3 * width :])
        .astype(jnp.bfloat16)
        .reshape(rows, HEADS, HEAD)
    )
    keys_again, values_again = (
        lax.all_gather(keys_own, "ctx", axis=0, tiled=True),
        lax.all_gather(values_own, "ctx", axis=0, tiled=True),
    )
    back_keys = keys_again.reshape(blocks, span, HEADS, HEAD)
    back_values = values_again.reshape(blocks, span, HEADS, HEAD)

    def delta_step(total, piece):
        key_block, value_block, position_block = piece
        probs = jnp.exp(block_scores(key_block, position_block) - log_total[..., None])
        grad_probs = jnp.einsum(
            "qhd,khd->hqk", grad_mixed, value_block, preferred_element_type=jnp.float32
        )
        return (total + jnp.sum(probs * grad_probs, axis=-1), None)

    delta, _ = lax.scan(
        delta_step, jnp.zeros((HEADS, rows), jnp.float32), (back_keys, back_values, key_pos)
    )

    def grad_step(grad_query, piece):
        key_block, value_block, position_block = piece
        probs = jnp.exp(block_scores(key_block, position_block) - log_total[..., None])
        grad_probs = jnp.einsum(
            "qhd,khd->hqk", grad_mixed, value_block, preferred_element_type=jnp.float32
        )
        grad_scores = (probs * (grad_probs - delta[..., None])).astype(jnp.bfloat16)
        grad_query = grad_query + jnp.einsum(
            "hqk,khd->qhd", grad_scores, key_block, preferred_element_type=jnp.float32
        )
        grad_keys = jnp.einsum(
            "hqk,qhd->khd", grad_scores, queries, preferred_element_type=jnp.float32
        )
        grad_values = jnp.einsum(
            "hqk,qhd->khd",
            probs.astype(jnp.bfloat16),
            grad_mixed,
            preferred_element_type=jnp.float32,
        )
        return (grad_query, (grad_keys, grad_values))

    grad_query, (grad_keys, grad_values) = lax.scan(
        grad_step, jnp.zeros((rows, HEADS, HEAD), jnp.float32), (back_keys, back_values, key_pos)
    )
    keys_sum, values_sum = (
        lax.psum_scatter(
            grad_keys.reshape(seq_len, width).astype(jnp.bfloat16),
            "ctx",
            scatter_dimension=0,
            tiled=True,
        ).astype(jnp.float32),
        lax.psum_scatter(
            grad_values.reshape(seq_len, width).astype(jnp.bfloat16),
            "ctx",
            scatter_dimension=0,
            tiled=True,
        ).astype(jnp.float32),
    )
    query_low = unrotate(grad_query * scale, cosine, sine).reshape(rows, width).astype(jnp.bfloat16)
    key_low = (
        unrotate((keys_sum * scale).reshape(rows, HEADS, HEAD), cosine, sine)
        .reshape(rows, width)
        .astype(jnp.bfloat16)
    )
    value_low = values_sum.astype(jnp.bfloat16)
    grad_proj = jnp.concatenate([query_low, key_low, value_low], axis=1)
    grad_one = contract_last(grad_proj, attn_back[:, : 3 * width])
    reduced_one = grad_one * gain_one
    grad_gain_one = jnp.sum(grad_one * normed_one, axis=0)
    grad_input = grad_after + inv_one * (
        reduced_one - normed_one * jnp.mean(reduced_one * normed_one, axis=-1, keepdims=True)
    )
    attn_term = jnp.concatenate(
        [contract_first(hidden_one, grad_proj), contract_first(mixed_low, after_low)], axis=1
    )
    down_term = contract_first(activation, grad_out)
    gain_term = jnp.stack([grad_gain_one, grad_gain_two])
    attn_grad, down_grad, gain_grad = (
        lax.psum_scatter(attn_term, ("dp", "ctx"), scatter_dimension=0, tiled=True),
        lax.psum_scatter(down_term, ("dp", "ctx"), scatter_dimension=0, tiled=True),
        lax.psum_scatter(gain_term, ("dp", "ctx"), scatter_dimension=1, tiled=True),
    )
    attn_new, attn_moment, attn_square = adam_step(
        attn_weight, attn_grad, attn_first, attn_second, 3.0 / math.sqrt(D), decay_rate
    )
    gate_new, gate_moment, gate_square = adam_step(
        gate_up, gate_grad, gate_first, gate_second, 3.0 / math.sqrt(D), decay_rate
    )
    down_new, down_moment, down_square = adam_step(
        down_weight, down_grad, down_first, down_second, 3.0 / math.sqrt(FF), decay_rate
    )
    gain_new, gain_moment, gain_square = adam_step(
        norm_gains, gain_grad, gain_first, gain_second, gain_rate, 0.0
    )
    return (
        outputs.astype(jnp.bfloat16)[None],
        grad_input.astype(jnp.bfloat16)[None],
        attn_grad,
        gate_grad,
        down_grad,
        gain_grad,
        attn_new,
        gate_new,
        down_new,
        gain_new,
        attn_moment,
        gate_moment,
        down_moment,
        gain_moment,
        attn_square,
        gate_square,
        down_square,
        gain_square,
    )


def solution(mesh):
    placed = (
        P("dp", "ctx", None),
        P("dp", "ctx", None),
        P(),
        P(("dp", "ctx"), None),
        P(("dp", "ctx"), None),
        P(("dp", "ctx"), None),
        P(None, ("dp", "ctx")),
        P(("dp", "ctx"), None),
        P(("dp", "ctx"), None),
        P(("dp", "ctx"), None),
        P(("dp", "ctx"), None),
        P(("dp", "ctx"), None),
        P(("dp", "ctx"), None),
        P(None, ("dp", "ctx")),
        P(None, ("dp", "ctx")),
    )
    return jax.shard_map(
        body,
        mesh=mesh,
        in_specs=placed,
        out_specs=(
            P("dp", "ctx", None),
            P("dp", "ctx", None),
            P(("dp", "ctx"), None),
            P(("dp", "ctx"), None),
            P(("dp", "ctx"), None),
            P(None, ("dp", "ctx")),
            P(("dp", "ctx"), None),
            P(("dp", "ctx"), None),
            P(("dp", "ctx"), None),
            P(None, ("dp", "ctx")),
            P(("dp", "ctx"), None),
            P(("dp", "ctx"), None),
            P(("dp", "ctx"), None),
            P(None, ("dp", "ctx")),
            P(("dp", "ctx"), None),
            P(("dp", "ctx"), None),
            P(("dp", "ctx"), None),
            P(None, ("dp", "ctx")),
        ),
        check_vma=False,
    )
```

profile of v0, /device:TPU:0, one launch (start us, length us, event | category | flops | bytes accessed | tf_op | source)
XLA Modules:
  0.0 4094.7 jit_solution(10261999250331426745)
XLA Ops:
  10.1 43.6 %all-gather = bf16[32,64,2]{1,2,0:T(2,128)(2,1)S(1)} all-gather(bf16[1,64,2]{1,2,0:T(2,128)(2,1)S(1)} %convert_bitcast_fusion), channel_id=1, replica_groups=mesh['dp'=4,'ctx'=8] {'dp','ctx'}, dimensions={0}, use_global_device_ids=true | all-gather | bytes 8448 | tf_op jit(solution)/shard_map/all_gather | solution.py:107
  54.0 155.1 %all-gather.7.cloned.1.call-done = bf16[2048,8192]{1,0:T(8,128)(2,1)} async-done(((bf16[64,8192]{1,0:T(8,128)(2,1)}), bf16[2048,8192]{1,0:T(8,128)(2,1)}) %all-gather.7.cloned.1.call-update) | async-done | bytes 33554448 | tf_op jit(solution)/shard_map/all_gather | solution.py:106
  237.2 19.6 all-gather.9.cloned.1.call-done
  256.8 12.9 reshape.297
  279.4 16.6 all-gather.11.cloned.1.call-done
  296.0 12.9 reshape.298
  308.9 10.1 copy.93
  319.0 24.3 while.50
  343.3 11.5 while.51
  362.1 293.5 %all-gather.13.cloned.1.call-done = bf16[2048,16384]{1,0:T(8,128)(2,1)} async-done(((bf16[64,16384]{1,0:T(8,128)(2,1)}), bf16[2048,16384]{1,0:T(8,128)(2,1)}) %all-gather.13.cloned.1.call-update) | async-done | bytes 67108880 | tf_op jit(solution)/shard_map/all_gather | solution.py:174
  655.6 27.4 fusion.138
  682.9 168.9 %all-gather.15.cloned.1.call-done = bf16[8192,2048]{1,0:T(8,128)(2,1)} async-done(((bf16[256,2048]{1,0:T(8,128)(2,1)}), bf16[8192,2048]{1,0:T(8,128)(2,1)}) %all-gather.15.cloned.1.call-update) | async-done | bytes 33554448 | tf_op jit(solution)/shard_map/all_gather | solution.py:175
  851.8 21.0 multiply_convert_fusion.1
  872.8 30.6 multiply_reduce_fusion
  911.4 13.3 while.52
  924.7 43.8 %while.53 = (s32[]{:T(128)}, f32[128,32,64]{0,2,1:T(8,128)S(1)}, bf16[2,512,32,64]{1,3,2,0:T(8,128)(2,1)}, bf16[2,512,32,64]{1,3,2,0:T(8,128)(2,1)}, bf16[2,512,...) while((s32[]{:T(128)}, f32[128,32,64]{0,2,1:T(8,128)S(1)}, ...), condition=%wide.region_13.14_spmd.clone, body=%wide.region_12.13_spmd.clone.sunk | while | flops 1363738624 | bytes 191093600 | solution.py:255
  968.5 13.0 copy.117
  981.5 12.5 reshape.291
  994.0 13.2 copy.118
  1007.2 12.4 reshape.293
  1021.5 22.1 reduce-scatter.20.cloned.1.call-done
  1046.7 52.6 %reduce-scatter.22.cloned.1.call-done = bf16[128,2048]{1,0:T(8,128)(2,1)} async-done(((bf16[1024,2048]{1,0:T(8,128)(2,1)}), bf16[128,2048]{1,0:T(8,128)(2,1)}) %reduce-scatter.22.cloned.1.call-update) | async-done | bytes 524304
  1100.7 14.9 fusion.114
  1117.1 24.3 fusion.122
  1150.8 20.6 fusion.120
  1171.3 43.4 %pad_maximum_fusion = f32[2048,8192]{1,0:T(8,128)} fusion(f32[2048,2048]{1,0:T(8,128)} %fusion.126, f32[2048,6144]{1,0:T(8,128)} %fusion.120), kind=kLoop, calls=%fused_computation.78 | loop fusion | flops 16777216 | bytes 134217728 | tf_op jit(solution)/shard_map/concatenate | solution.py:286
  1216.7 45.9 %fusion.92 = f32[2048,16384]{1,0:T(8,128)} fusion(bf16[128,8192]{1,0:T(8,128)(2,1)} %get-tuple-element.537, bf16[128,8192]{1,0:T(8,128)(2,1)S(1)} %copy-done.11, f32[128,2048]{1,0:T(8,128)S(1)} %copy-done.5, f32[2048]{0:T(1024)S(1)} %bitcast.256, f32[128]{0:T(128)S(1)} %copy-done.37), kind=kOutput, calls=%fused_computation.99 | convolution fusion | flops 8599109632 | bytes 139469312 | tf_op jit(solution)/shard_map/dot_general | solution.py:57
  1264.2 14.6 fusion.101
  1281.4 672.1 %reduce-scatter.18.cloned.1.call-done = f32[256,2048]{1,0:T(8,128)} async-done(((f32[8192,2048]{1,0:T(8,128)}), f32[256,2048]{1,0:T(8,128)}) %reduce-scatter.18.cloned.1.call-update) | async-done | bytes 2097168 | tf_op jit(solution)/shard_map/reduce_scatter | solution.py:293
  1960.4 706.3 %reduce-scatter.16.cloned.1.call-done = f32[64,8192]{1,0:T(8,128)} async-done(((f32[2048,8192]{1,0:T(8,128)}), f32[64,8192]{1,0:T(8,128)}) %reduce-scatter.16.cloned.1.call-update) | async-done | bytes 2097168 | tf_op jit(solution)/shard_map/reduce_scatter | solution.py:292
  2673.8 1402.7 %reduce-scatter.26.cloned.1.call-done = f32[64,16384]{1,0:T(8,128)} async-done(((f32[2048,16384]{1,0:T(8,128)}), f32[64,16384]{1,0:T(8,128)}) %reduce-scatter.26.cloned.1.call-update) | async-done | bytes 4194320
  4076.6 11.4 multiply_subtract_fusion
  (256 shorter events, 185.0 us)
Async XLA Ops:
  7.2 46.5 %copy-start.14 = (bf16[1,128,2048]{2,1,0:T(8,128)(2,1)S(1)}, bf16[1,128,2048]{2,1,0:T(8,128)(2,1)}, u32[]{:S(2)}) copy-start(bf16[1,128,2048]{2,1,0:T(8,128)(2,1)} %param.23) | copy-start | bytes 1572868
  7.2 201.8 %all-gather.7.cloned.1.call-start = ((), (), s32[]{:S(2)}) async-start(), calls=%async_computation.6 | async-start | bytes 34603008 | tf_op jit(solution)/shard_map/all_gather | solution.py:106
  10.0 246.8 %all-gather.9.cloned.1.call-start = ((), (), s32[]{:S(2)}) async-start(), calls=%async_computation.7 | async-start | bytes 4718592 | tf_op jit(solution)/shard_map/all_gather | solution.py:126
  53.9 165.2 %copy-start.43 = (f32[128]{0:T(128)}, f32[128]{0:T(128)S(1)}, u32[]{:S(2)}) copy-start(f32[128]{0:T(128)S(1)} %add_rsqrt_fusion.1) | copy-start | bytes 1540
  54.0 165.2 %copy-start.38 = (f32[1,2048]{1,0:T(1,128)}, f32[1,2048]{1,0:T(1,128)S(1)}, u32[]{:S(2)}) copy-start(f32[1,2048]{1,0:T(1,128)S(1)} %get-tuple-element.554) | copy-start | bytes 24580
  54.0 849.5 %copy-start.23 = (f32[1,2048]{1,0:T(1,128)}, f32[1,2048]{1,0:T(1,128)S(1)}, u32[]{:S(2)}) copy-start(f32[1,2048]{1,0:T(1,128)S(1)} %get-tuple-element.553) | copy-start | bytes 24580
  221.7 74.3 %all-gather.11.cloned.1.call-start = ((), (), s32[]{:S(2)}) async-start(), calls=%async_computation.8 | async-start | bytes 4718592 | tf_op jit(solution)/shard_map/all_gather | solution.py:125
  229.6 426.0 %all-gather.13.cloned.1.call-start = ((), (), s32[]{:S(2)}) async-start(), calls=%async_computation.9 | async-start | bytes 69206016 | tf_op jit(solution)/shard_map/all_gather | solution.py:174
  233.6 618.3 %all-gather.15.cloned.1.call-start = ((), (), s32[]{:S(2)}) async-start(), calls=%async_computation.10 | async-start | bytes 34603008 | tf_op jit(solution)/shard_map/all_gather | solution.py:175
  234.8 808.9 %reduce-scatter.20.cloned.1.call-start = ((), (), s32[]{:S(2)}) async-start(), calls=%async_computation.13 | async-start | bytes 4718592
  319.0 24.3 copy-start.29
  362.1 541.4 %copy-start.4 = (f32[128,2048]{1,0:T(8,128)}, f32[128,2048]{1,0:T(8,128)S(1)}, u32[]{:S(2)}) copy-start(f32[128,2048]{1,0:T(8,128)S(1)} %get-tuple-element.556) | copy-start | bytes 3145732
  362.1 541.4 %copy-start.36 = (f32[128]{0:T(128)}, f32[128]{0:T(128)S(1)}, u32[]{:S(2)}) copy-start(f32[128]{0:T(128)S(1)} %add_rsqrt_fusion) | copy-start | bytes 1540
  655.6 196.3 %copy-start.27 = (bf16[1,128,2048]{2,1,0:T(8,128)(2,1)S(1)}, bf16[1,128,2048]{2,1,0:T(8,128)(2,1)}, u32[]{:S(2)}) copy-start(bf16[1,128,2048]{2,1,0:T(8,128)(2,1)} %param.24) | copy-start | bytes 1572868
  994.0 105.3 %reduce-scatter.22.cloned.1.call-start = ((), (), s32[]{:S(2)}) async-start(), calls=%async_computation.14 | async-start | bytes 4718592
  1019.6 260.3 %reduce-scatter.24.cloned.1.call-start = ((), (), s32[]{:S(2)}) async-start(), calls=%async_computation.15 | async-start | bytes 1081344
  1020.4 24.6 copy-start.33
  1045.2 55.5 %copy-start.15 = (bf16[1,128,2048]{2,1,0:T(8,128)(2,1)S(1)}, bf16[1,128,2048]{2,1,0:T(8,128)(2,1)}, u32[]{:S(2)}) copy-start(bf16[1,128,2048]{2,1,0:T(8,128)(2,1)} %param.23) | copy-start | bytes 1572868
  1045.2 55.5 %copy-start.39 = (f32[1,2048]{1,0:T(1,128)S(1)}, f32[1,2048]{1,0:T(1,128)}, u32[]{:S(2)}) copy-start(f32[1,2048]{1,0:T(1,128)} %copy-done.38) | copy-start | bytes 24580
  1045.2 55.5 %copy-start.44 = (f32[128]{0:T(128)S(1)}, f32[128]{0:T(128)}, u32[]{:S(2)}) copy-start(f32[128]{0:T(128)} %copy-done.43) | copy-start | bytes 1540
  1100.7 14.9 copy-start.42
  1100.7 16.4 copy-start.6
  1117.0 836.5 %reduce-scatter.18.cloned.1.call-start = ((), (), s32[]{:S(2)}) async-start(), calls=%async_computation.12 | async-start | bytes 69206016 | tf_op jit(solution)/shard_map/reduce_scatter | solution.py:293
  1141.4 1525.3 %reduce-scatter.16.cloned.1.call-start = ((), (), s32[]{:S(2)}) async-start(), calls=%async_computation.11 | async-start | bytes 69206016 | tf_op jit(solution)/shard_map/reduce_scatter | solution.py:292
  1214.8 2861.8 %reduce-scatter.26.cloned.1.call-start = ((), (), s32[]{:S(2)}) async-start(), calls=%async_computation.16 | async-start | bytes 138412032
  1264.1 14.6 copy-start.16
  1264.1 14.6 copy-start.31
  1264.1 16.7 copy-start.47
  1264.1 16.6 copy-start.48
  1264.2 16.6 copy-start.49
  1278.7 674.8 %copy-start.13 = (f32[256,2048]{1,0:T(8,128)S(1)}, f32[256,2048]{1,0:T(8,128)}, u32[]{:S(2)}) copy-start(f32[256,2048]{1,0:T(8,128)} %param.28) | copy-start | bytes 6291460
  1280.8 679.6 %copy-start.45 = (f32[2,64]{1,0:T(2,128)}, f32[2,64]{1,0:T(2,128)S(1)}, u32[]{:S(2)}) copy-start(f32[2,64]{1,0:T(2,128)S(1)} %copy.112) | copy-start | bytes 1540
  (39 other events, 191.8 us)
Sparse Core Ops, SparseCore 0:
  11.5 197.5 all-gather.6
  221.9 34.8 all-gather.8
  259.2 36.7 all-gather.10
  299.3 356.2 all-gather.12
  658.9 192.9 all-gather.14
  994.1 49.4 reduce-scatter.19
  1048.0 51.3 reduce-scatter.21
  1117.1 134.7 reduce-scatter.23
  1255.0 698.4 reduce-scatter.17
  1956.4 710.2 reduce-scatter.15
  2669.7 1406.8 reduce-scatter.25
where the time goes:
time: 4110 us; the launch traced here: 4090 us
  waiting for transfers between devices  3510 us (85%)
  matrix products  300 us (7%)
  local copies, waits for them, and re-layouts  126 us (3%)
  other arithmetic  99.2 us (2%)
  blocking collectives  43.6 us (1%)
    unnamed x15, waiting for transfers between devices  1480 us
    reduce_scatter x1, waiting for transfers between devices, body(): lax.psum_scatter(attn_term, ('dp', 'ctx'), scatter_dimension=0, tiled=True)  706 us
    reduce_scatter x1, waiting for transfers between devices, body(): lax.psum_scatter(down_term, ('dp', 'ctx'), scatter_dimension=0, tiled=True)  672 us
    all_gather x1, waiting for transfers between devices, body(): lax.all_gather(gate_up.astype(jnp.bfloat16), ('dp', 'ctx'), axis=0, tiled...  293 us
    all_gather x1, waiting for transfers between devices, body(): lax.all_gather(down_weight.astype(jnp.bfloat16), ('dp', 'ctx'), axis=0, t...  169 us
    all_gather x1, waiting for transfers between devices, body(): lax.all_gather(attn_weight.astype(jnp.bfloat16), ('dp', 'ctx'), axis=0, t...  155 us
    dot_general x4, matrix products, contract_first(): lax.dot_general(first, second, (((0,), (0,)), ((), ())), preferred_elemen...  98.8 us
    unnamed x101, local copies, waits for them, and re-layouts  85 us
  transfers between devices with their start and end apart: 11, of which 10 were waited for; matrix products, arithmetic and copies ran while one was open for 8% of the time, Pallas kernels for 0%

commit v1 on v0

v1 whole, which is shorter than its diff:
```python
import math

import jax
import jax.numpy as jnp
from jax import lax
from jax.sharding import PartitionSpec as P

D = 2048
HEADS = 32
HEAD = 64
FF = 8192
STEP = 5

norm_eps = 1e-05
rope_base = 130000.0
beta_one = 0.9
beta_two = 0.95
adam_eps = 1e-08
decay_rate = 0.1
gain_rate = 0.4
masked = -1e30

bf16 = jnp.bfloat16
f32 = jnp.float32


def rms_scale(values):
    return lax.rsqrt(jnp.mean(values * values, axis=-1, keepdims=True) + norm_eps)


def angles(positions):
    index = jnp.arange(HEAD // 2, dtype=f32)
    freqs = jnp.power(f32(rope_base), -2.0 * index / HEAD)
    phase = positions.astype(f32)[:, None] * freqs[None, :]
    phase = jnp.concatenate([phase, phase], axis=-1)
    return (jnp.cos(phase)[:, None, :], jnp.sin(phase)[:, None, :])


def rotate(values, cosine, sine):
    middle = values.shape[-1] // 2
    turned = jnp.concatenate([-values[..., middle:], values[..., :middle]], axis=-1)
    return values * cosine + turned * sine


def unrotate(values, cosine, sine):
    middle = values.shape[-1] // 2
    sined = values * sine
    turned = jnp.concatenate([sined[..., middle:], -sined[..., :middle]], axis=-1)
    return values * cosine + turned


def dot(first, second):
    return jnp.dot(first, second, preferred_element_type=f32)


def contract_last(first, second):
    return lax.dot_general(first, second, (((1,), (1,)), ((), ())), preferred_element_type=f32)


def contract_first(first, second):
    return lax.dot_general(first, second, (((0,), (0,)), ((), ())), preferred_element_type=f32)


def adam_step(weight, grad, first, second, rate, decay):
    first = beta_one * first + (1.0 - beta_one) * grad
    second = beta_two * second + (1.0 - beta_two) * grad * grad
    corrected_first = first / (1.0 - beta_one**STEP)
    corrected_second = second / (1.0 - beta_two**STEP)
    fresh = weight - rate * (
        corrected_first / (jnp.sqrt(corrected_second) + adam_eps) + decay * weight
    )
    return (fresh, first, second)


def gather(values, axis):
    return lax.all_gather(values, axis, axis=0, tiled=True)


def scatter(values, axis):
    return lax.psum_scatter(values, axis, scatter_dimension=0, tiled=True)


def exchange(pieces):
    return lax.all_to_all(pieces, "ctx", split_axis=0, concat_axis=0, tiled=True)


def attention_forward(queries, keys, values, positions, scale):
    scores = jnp.einsum("qhd,khd->hqk", queries, keys, preferred_element_type=f32) * scale
    allowed = positions[None, :] <= positions[:, None]
    scores = jnp.where(allowed[None], scores, masked)
    peak = jnp.max(scores, axis=-1, keepdims=True)
    weights = jnp.exp(scores - peak)
    total = jnp.sum(weights, axis=-1, keepdims=True)
    mixed = jnp.einsum(
        "hqk,khd->qhd", (weights / total).astype(bf16), values, preferred_element_type=f32
    )
    return mixed, peak + jnp.log(total)


def attention_backward(queries, keys, values, positions, scale, log_total, grad_mixed):
    scores = jnp.einsum("qhd,khd->hqk", queries, keys, preferred_element_type=f32) * scale
    allowed = positions[None, :] <= positions[:, None]
    probs = jnp.where(allowed[None], jnp.exp(scores - log_total), 0.0)
    grad_probs = jnp.einsum("qhd,khd->hqk", grad_mixed, values, preferred_element_type=f32)
    delta = jnp.sum(probs * grad_probs, axis=-1, keepdims=True)
    grad_scores = (probs * (grad_probs - delta)).astype(bf16)
    grad_query = jnp.einsum("hqk,khd->qhd", grad_scores, keys, preferred_element_type=f32) * scale
    grad_keys = jnp.einsum("hqk,qhd->khd", grad_scores, queries, preferred_element_type=f32) * scale
    grad_values = jnp.einsum(
        "hqk,qhd->khd", probs.astype(bf16), grad_mixed, preferred_element_type=f32
    )
    return grad_query, grad_keys, grad_values


def body(
    tokens,
    cotangent,
    block_ids,
    attn_weight,
    gate_up,
    down_weight,
    norm_gains,
    attn_first,
    attn_second,
    gate_first,
    gate_second,
    down_first,
    down_second,
    gain_first,
    gain_second,
):
    every = ("dp", "ctx")
    width = attn_weight.shape[1] // 4
    planes = lax.axis_size("dp")
    ranks = lax.axis_size("ctx")
    own_rows = attn_weight.shape[0]
    units = down_weight.shape[0]
    rows = tokens.shape[1]
    half = rows // 2
    seq_len = rows * ranks
    local_heads = HEADS // ranks
    local_width = local_heads * HEAD
    aligned = local_heads == planes
    rank = lax.axis_index("ctx")
    scale = HEAD ** (-0.5)
    positions = (
        block_ids[:, None] * half + jnp.arange(half, dtype=jnp.int32)[None, :]
    ).reshape(-1)
    cosine, sine = angles(positions)

    attn_low = attn_weight.astype(bf16)
    qkv_pieces = (
        attn_low[:, : 3 * width]
        .reshape(own_rows, 3, local_heads, ranks, HEAD)
        .transpose(3, 0, 1, 2, 4)
        .reshape(ranks, own_rows, 3 * local_width)
    )
    qkv = gather(exchange(qkv_pieces).reshape(ranks * own_rows, 3 * local_width), "dp")
    out_low = attn_low[:, 3 * width :]
    if aligned:
        out_proj = gather(out_low, "dp")
    else:
        out_all = gather(out_low, every).reshape(local_heads, ranks, HEAD, width)
        out_proj = lax.dynamic_index_in_dim(out_all, rank, 1, keepdims=False).reshape(
            local_width, width
        )
    gate_pieces = (
        gate_up.astype(bf16)
        .reshape(own_rows, 2, planes, ranks, units)
        .transpose(3, 0, 1, 2, 4)
        .reshape(ranks, own_rows, 2 * planes * units)
    )
    hidden = planes * units
    gate = gather(exchange(gate_pieces).reshape(ranks * own_rows, 2 * hidden), "dp")
    down = gather(down_weight.astype(bf16), "dp")

    gains_low = lax.all_gather(norm_gains.astype(bf16), every, axis=1, tiled=True)
    gain_one = gains_low[0].astype(f32)
    gain_two = gains_low[1].astype(f32)
    inputs_all = gather(tokens[0], "ctx").astype(f32)
    grad_out_all = gather(cotangent[0], "ctx")

    normed_all = inputs_all * rms_scale(inputs_all)
    hidden_one = (normed_all * gain_one).astype(bf16)
    projected = dot(hidden_one, qkv)
    by_head = projected.reshape(seq_len, 3, local_heads, HEAD)
    queries = rotate(by_head[:, 0], cosine, sine).astype(bf16)
    keys = rotate(by_head[:, 1], cosine, sine).astype(bf16)
    values = by_head[:, 2].astype(bf16)
    mixed, log_total = attention_forward(queries, keys, values, positions, scale)
    mixed_low = mixed.reshape(seq_len, local_width).astype(bf16)

    inputs = tokens[0].astype(f32)
    after = inputs + scatter(dot(mixed_low, out_proj).astype(bf16), "ctx").astype(f32)
    inv_two = rms_scale(after)
    normed_two = after * inv_two
    hidden_two = gather((normed_two * gain_two).astype(bf16), "ctx")
    gate_both = dot(hidden_two, gate)
    gate_part = gate_both[:, :hidden]
    up_part = gate_both[:, hidden:]
    gate_sigmoid = jax.nn.sigmoid(gate_part)
    gate_act = gate_part * gate_sigmoid
    activation = (gate_act * up_part).astype(bf16)
    outputs = after + scatter(dot(activation, down).astype(bf16), "ctx").astype(f32)

    grad_act = contract_last(grad_out_all, down)
    grad_gate = (
        grad_act * up_part * gate_sigmoid * (1.0 + gate_part * (1.0 - gate_sigmoid))
    ).astype(bf16)
    grad_up = (grad_act * gate_act).astype(bf16)
    grad_both = jnp.concatenate([grad_gate, grad_up], axis=1)
    grad_two = scatter(contract_last(grad_both, gate).astype(bf16), "ctx").astype(f32)
    down_grad = scatter(contract_first(activation, grad_out_all).astype(bf16), "dp").astype(f32)
    gate_term = scatter(contract_first(hidden_two, grad_both).astype(bf16), "dp")
    gate_grad = (
        exchange(gate_term.reshape(ranks, own_rows, 2 * hidden))
        .reshape(ranks, own_rows, 2, planes, units)
        .transpose(1, 2, 3, 0, 4)
        .reshape(own_rows, gate_up.shape[1])
        .astype(f32)
    )

    reduced_two = grad_two * gain_two
    grad_gain_two = jnp.sum(grad_two * normed_two, axis=0)
    grad_after = cotangent[0].astype(f32) + inv_two * (
        reduced_two - normed_two * jnp.mean(reduced_two * normed_two, axis=-1, keepdims=True)
    )
    after_low = gather(grad_after.astype(bf16), "ctx")
    grad_mixed = (
        contract_last(after_low, out_proj).astype(bf16).reshape(seq_len, local_heads, HEAD)
    )
    grad_query, grad_keys, grad_values = attention_backward(
        queries, keys, values, positions, scale, log_total, grad_mixed
    )
    grad_proj = jnp.concatenate(
        [
            unrotate(grad_query, cosine, sine).reshape(seq_len, local_width),
            unrotate(grad_keys, cosine, sine).reshape(seq_len, local_width),
            grad_values.reshape(seq_len, local_width),
        ],
        axis=1,
    ).astype(bf16)
    grad_one_part = contract_last(grad_proj, qkv)
    grad_gain_one = jnp.sum(grad_one_part * normed_all, axis=0)
    grad_one = scatter(grad_one_part.astype(bf16), "ctx").astype(f32)
    inv_one = rms_scale(inputs)
    normed_one = inputs * inv_one
    reduced_one = grad_one * gain_one
    grad_input = grad_after + inv_one * (
        reduced_one - normed_one * jnp.mean(reduced_one * normed_one, axis=-1, keepdims=True)
    )

    out_term = contract_first(mixed_low, after_low).astype(bf16)
    if aligned:
        out_grad = scatter(out_term, "dp").astype(f32)
    else:
        spread = jnp.zeros((local_heads, ranks, HEAD, width), bf16)
        spread = lax.dynamic_update_index_in_dim(
            spread, out_term.reshape(local_heads, 1, HEAD, width), rank, 1
        )
        out_grad = scatter(spread.reshape(HEADS * HEAD, width), every).astype(f32)
    qkv_term = scatter(contract_first(hidden_one, grad_proj).astype(bf16), "dp")
    qkv_grad = (
        exchange(qkv_term.reshape(ranks, own_rows, 3 * local_width))
        .reshape(ranks, own_rows, 3, local_heads, HEAD)
        .transpose(1, 2, 3, 0, 4)
        .reshape(own_rows, 3 * width)
        .astype(f32)
    )
    attn_grad = jnp.concatenate([qkv_grad, out_grad], axis=1)
    gain_grad = lax.psum_scatter(
        jnp.stack([grad_gain_one, grad_gain_two]), every, scatter_dimension=1, tiled=True
    )

    attn_new, attn_moment, attn_square = adam_step(
        attn_weight, attn_grad, attn_first, attn_second, 3.0 / math.sqrt(D), decay_rate
    )
    gate_new, gate_moment, gate_square = adam_step(
        gate_up, gate_grad, gate_first, gate_second, 3.0 / math.sqrt(D), decay_rate
    )
    down_new, down_moment, down_square = adam_step(
        down_weight, down_grad, down_first, down_second, 3.0 / math.sqrt(FF), decay_rate
    )
    gain_new, gain_moment, gain_square = adam_step(
        norm_gains, gain_grad, gain_first, gain_second, gain_rate, 0.0
    )
    return (
        outputs.astype(bf16)[None],
        grad_input.astype(bf16)[None],
        attn_grad,
        gate_grad,
        down_grad,
        gain_grad,
        attn_new,
        gate_new,
        down_new,
        gain_new,
        attn_moment,
        gate_moment,
        down_moment,
        gain_moment,
        attn_square,
        gate_square,
        down_square,
        gain_square,
    )


def solution(mesh):
    acts = P("dp", "ctx", None)
    weight = P(("dp", "ctx"), None)
    gains = P(None, ("dp", "ctx"))
    four = (weight, weight, weight, gains)
    return jax.shard_map(
        body,
        mesh=mesh,
        in_specs=(acts, acts, P()) + four + (weight,) * 6 + (gains,) * 2,
        out_specs=(acts, acts) + four * 4,
        check_vma=False,
    )
```

time: 4110 us -> 1230 us (0.30)
  waiting for transfers between devices: 3510 us -> 857 us
  matrix products: 300 us -> 137 us
  local copies, waits for them, and re-layouts: 126 us -> 39.7 us
  blocking collectives: 43.6 us -> 106 us
    unnamed x15 -> x18, waiting for transfers between devices: 1480 us -> 131 us
    reduce_scatter x2 -> x8, waiting for transfers between devices: 1380 us -> 381 us  [scatter(): return lax.psum_scatter(values, axis, scatter_dimension=0, tiled=True)]
    all_gather x5 -> x8, waiting for transfers between devices: 654 us -> 345 us  [gather(): return lax.all_gather(values, axis, axis=0, tiled=True)]
    unnamed x101 -> x67, local copies, waits for them, and re-layouts: 85 us -> 13.2 us
    all_to_all x0 -> x2, blocking collectives: none -> 65.6 us  [exchange(): lax.all_to_all(pieces, 'ctx', split_axis=0, concat_axis=0, tiled=True)]
    dot_general x4, matrix products: 98.8 us -> 33.5 us  [contract_first(): lax.dot_general(first, second, (((0,), (0,)), ((), ())), preferred_elemen...]
    dot_general x22 -> x10, matrix products: 128 us -> 68.2 us  [the longest x4 35 us: dot(): return jnp.dot(first, second, preferred_element_type=f32)]
    concatenate x2 -> x0, other arithmetic: 43.5 us -> none  [the longest x1 43.4 us: body(): jnp.concatenate([contract_first(hidden_one, grad_proj), contract_first(mi...]
  transfers between devices with their start and end apart: 11 -> 19, of which waited for: 10 -> 16; matrix products, arithmetic and copies ran while one was open for 8% -> 15% of each run, Pallas kernels for 0% -> 0%
where the time goes in v1:
time: 1230 us
  waiting for transfers between devices  857 us (70%)
  matrix products  137 us (11%)
  blocking collectives  106 us (9%)
  other arithmetic  61.8 us (5%)
  local copies, waits for them, and re-layouts  39.7 us (3%)
  between operations  14.7 us (1%)
    reduce_scatter x8, waiting for transfers between devices, scatter(): return lax.psum_scatter(values, axis, scatter_dimension=0, tiled=True)  381 us
    all_gather x8, waiting for transfers between devices, gather(): return lax.all_gather(values, axis, axis=0, tiled=True)  345 us
    unnamed x18, waiting for transfers between devices  131 us
    all_to_all x2, blocking collectives, exchange(): lax.all_to_all(pieces, 'ctx', split_axis=0, concat_axis=0, tiled=True)  65.6 us
    all_gather x1, blocking collectives, body(): lax.all_gather(norm_gains.astype(bf16), every, axis=1, tiled=True)  40 us
    dot_general x4, matrix products, contract_last(): lax.dot_general(first, second, (((1,), (1,)), ((), ())), preferred_elemen...  35.6 us
    dot_general x4, matrix products, dot(): return jnp.dot(first, second, preferred_element_type=f32)  35 us
    dot_general x4, matrix products, contract_first(): lax.dot_general(first, second, (((0,), (0,)), ((), ())), preferred_elemen...  33.5 us
  transfers between devices with their start and end apart: 19, of which 16 were waited for; matrix products, arithmetic and copies ran while one was open for 15% of the time, Pallas kernels for 0%

profile of v1, /device:TPU:0, one launch (start us, length us, event | category | flops | bytes accessed | tf_op | source)
XLA Modules:
  0.0 1226.5 jit_solution(10724186730532925747)
XLA Ops:
  13.9 23.2 %all_to_all.20 = bf16[8,64,768]{2,1,0:T(8,128)(2,1)} all-to-all(bf16[8,64,768]{2,1,0:T(8,128)(2,1)S(1)} %reshape.258), channel_id=1, replica_groups=mesh['dp'=4,'ctx'=8] {'ctx'}, dimensions={0} | all-to-all | bytes 1572864 | tf_op jit(solution)/shard_map/all_to_all | solution.py:84
  39.9 40.0 %all-gather.2 = bf16[32,64,2]{1,2,0:T(2,128)(2,1)S(1)} all-gather(bf16[1,64,2]{1,2,0:T(2,128)(2,1)S(1)} %convert_bitcast_fusion), channel_id=1, replica_groups=mesh['dp'=4,'ctx'=8] {'dp','ctx'}, dimensions={0}, use_global_device_ids=true | all-gather | bytes 8448 | tf_op jit(solution)/shard_map/all_gather | solution.py:177
  84.9 37.3 %all-gather.12.cloned.1.call-done = bf16[2048,768]{1,0:T(8,128)(2,1)} async-done(((bf16[512,768]{1,0:T(8,128)(2,1)}), bf16[2048,768]{1,0:T(8,128)(2,1)}) %all-gather.12.cloned.1.call-update) | async-done | bytes 3145744 | tf_op jit(solution)/shard_map/all_gather | solution.py:76
  122.2 6.6 fusion.31
  143.9 7.1 all-gather.14.cloned.1.call-done
  165.1 42.3 %all_to_all.21 = bf16[8,64,2048]{2,1,0:T(8,128)(2,1)} all-to-all(bf16[8,64,2048]{2,1,0:T(8,128)(2,1)} %reshape.262), channel_id=1, replica_groups=mesh['dp'=4,'ctx'=8] {'ctx'}, dimensions={0} | all-to-all | bytes 4194304 | tf_op jit(solution)/shard_map/all_to_all | solution.py:84
  207.8 13.1 %reduce-scatter.12.cloned.1.call-done = bf16[128,2048]{1,0:T(8,128)(2,1)} async-done(((bf16[1024,2048]{1,0:T(8,128)(2,1)}), bf16[128,2048]{1,0:T(8,128)(2,1)}) %reduce-scatter.12.cloned.1.call-update) | async-done | bytes 524304 | tf_op jit(solution)/shard_map/reduce_scatter | solution.py:80
  227.8 144.2 %all-gather.18.cloned.1.call-done = bf16[2048,2048]{1,0:T(8,128)(2,1)} async-done(((bf16[512,2048]{1,0:T(8,128)(2,1)}), bf16[2048,2048]{1,0:T(8,128)(2,1)}) %all-gather.18.cloned.1.call-update) | async-done | bytes 8388624 | tf_op jit(solution)/shard_map/all_gather | solution.py:76
  372.0 37.5 %all-gather.16.cloned.1.call-done = bf16[1024,2048]{1,0:T(8,128)(2,1)} async-done(((bf16[128,2048]{1,0:T(8,128)(2,1)}), bf16[1024,2048]{1,0:T(8,128)(2,1)}) %all-gather.16.cloned.1.call-update) | async-done | bytes 4194320 | tf_op jit(solution)/shard_map/all_gather | solution.py:76
  409.5 14.5 %fusion.75 = f32[1024,2048]{1,0:T(8,128)} fusion(bf16[1024,2048]{1,0:T(8,128)(2,1)} %all-gather.16.cloned.1.call-done, bf16[2048,2048]{1,0:T(8,128)(2,1)} %all-gather.18.cloned.1.call-done), kind=kOutput, calls=%fused_computation.141 | convolution fusion | flops 8589934592 | bytes 20971520 | tf_op jit(solution)/shard_map/dot_general | solution.py:53
  424.0 68.5 %all-gather.20.cloned.1.call-done = bf16[1024,2048]{1,0:T(8,128)(2,1)} async-done(((bf16[256,2048]{1,0:T(8,128)(2,1)}), bf16[1024,2048]{1,0:T(8,128)(2,1)}) %all-gather.20.cloned.1.call-update) | async-done | bytes 4194320 | tf_op jit(solution)/shard_map/all_gather | solution.py:76
  492.5 37.3 %all-gather.26.cloned.1.call-done = bf16[1,1024,2048]{2,1,0:T(8,128)(2,1)} async-done(((bf16[1,128,2048]{2,1,0:T(8,128)(2,1)}), bf16[1,1024,2048]{2,1,0:T(8,128)(2,1)}) %all-gather.26.cloned.1.call-update) | async-done | bytes 4194320 | tf_op jit(solution)/shard_map/all_gather | solution.py:76
  529.8 13.1 %multiply_convert_fusion.2 = (bf16[1024,1024]{1,0:T(8,128)(2,1)S(1)}, bf16[1024,1024]{1,0:T(8,128)(2,1)S(1)}, bf16[1024,1024]{1,0:T(8,128)(2,1)}) fusion(f32[1024,2048]{1,0:T(8,128)} %fusion.75, bf16[1024,2048]{1,0:T(8,128)(2,1)} %all-gather.20.cloned.1.call-done, bf16[1,1024,2048]{2,1,0:T(8,128)(2,1)} %all-gather.26.cloned.1.call-done), kind=kOutput, calls=%fused_computation.29 | convolution fusion | flops 4310695936 | bytes 23068672 | tf_op jit(solution)/shard_map/dot_general | solution.py:57
  545.0 12.6 %convolution_convert_fusion.1 = bf16[1024,2048]{1,0:T(8,128)(2,1)} fusion(bf16[2048,2048]{1,0:T(8,128)(2,1)} %all-gather.18.cloned.1.call-done, bf16[1024,1024]{1,0:T(8,128)(2,1)S(1)} %get-tuple-element.36, bf16[1024,1024]{1,0:T(8,128)(2,1)S(1)} %get-tuple-element.35), kind=kOutput, calls=%fused_computation.33 | convolution fusion | flops 8600420352 | bytes 16777216 | tf_op jit(solution)/shard_map/dot_general | solution.py:57
  558.0 51.0 %reduce-scatter.16.cloned.1.call-done = bf16[128,2048]{1,0:T(8,128)(2,1)} async-done(((bf16[1024,2048]{1,0:T(8,128)(2,1)}), bf16[128,2048]{1,0:T(8,128)(2,1)}) %reduce-scatter.16.cloned.1.call-update) | async-done | bytes 524304 | tf_op jit(solution)/shard_map/reduce_scatter | solution.py:80
  613.1 14.0 %convolution_convert_fusion = bf16[2048,2048]{1,0:T(8,128)(2,1)} fusion(bf16[1024,2048]{1,0:T(8,128)(2,1)} %all-gather.16.cloned.1.call-done, bf16[1024,1024]{1,0:T(8,128)(2,1)} %copy-done.30, bf16[1024,1024]{1,0:T(8,128)(2,1)} %copy-done.29), kind=kOutput, calls=%fused_computation.18 | convolution fusion | flops 8602517504 | bytes 16777216 | tf_op jit(solution)/shard_map/dot_general | solution.py:61
  627.3 9.4 fusion.17
  636.8 13.2 %all-gather.22.cloned.1.call-done = bf16[1024,2048]{1,0:T(8,128)(2,1)} async-done(((bf16[128,2048]{1,0:T(8,128)(2,1)}), bf16[1024,2048]{1,0:T(8,128)(2,1)}) %all-gather.22.cloned.1.call-update) | async-done | bytes 4194320 | tf_op jit(solution)/shard_map/all_gather | solution.py:76
  653.7 12.8 %multiply_reduce_fusion = (f32[4,1024]{1,0:T(4,128)S(1)}, f32[4,1024,1024]{1,2,0:T(8,128)}) fusion(f32[4,1024,1024]{1,2,0:T(8,128)} %copy-done, f32[4,1024]{1,0:T(4,128)S(1)} %log_add_fusion, pred[1024,1024]{0,1:T(8,128)(4,1)S(1)} %broadcast_compare_fusion, bf16[1024,4,64]{0,2,1:T(8,128)(2,1)S(1)} %bitcast.148, f32[1024,3,4,64]{0,3,2,1:T(8,128)} %bitcast.135), kind=kOutput, calls=%fused_computation.1 | convolution fusion | flops 557838336 | bytes 35684352 | tf_op jit(solution)/shard_map/qhd,khd->hqk/dot_general | solution.py:104
  666.5 12.3 multiply_convert_fusion
  684.6 8.0 fusion.22
  700.5 7.8 convolution_convert_fusion.4
  709.0 9.3 convolution_convert_fusion.3
  718.3 78.5 %reduce-scatter.24.cloned.1.call-done = bf16[512,2048]{1,0:T(8,128)(2,1)} async-done(((bf16[2048,2048]{1,0:T(8,128)(2,1)}), bf16[512,2048]{1,0:T(8,128)(2,1)}) %reduce-scatter.24.cloned.1.call-update) | async-done | bytes 2097168 | tf_op jit(solution)/shard_map/reduce_scatter | solution.py:80
  801.7 75.4 %reduce-scatter.26.cloned.1.call-done = bf16[256,2048]{1,0:T(8,128)(2,1)} async-done(((bf16[1024,2048]{1,0:T(8,128)(2,1)}), bf16[256,2048]{1,0:T(8,128)(2,1)}) %reduce-scatter.26.cloned.1.call-update) | async-done | bytes 1048592 | tf_op jit(solution)/shard_map/reduce_scatter | solution.py:80
  877.0 7.3 multiply_subtract_fusion.1
  886.6 128.7 %reduce-scatter.28.cloned.1.call-done = f32[64,2]{1,0:T(8,128)} async-done(((f32[2048,2]{1,0:T(8,128)}), f32[64,2]{1,0:T(8,128)}) %reduce-scatter.28.cloned.1.call-update) | async-done | bytes 528
  1037.6 36.0 %reduce-scatter.20.cloned.1.call-done = bf16[512,768]{1,0:T(8,128)(2,1)} async-done(((bf16[2048,768]{1,0:T(8,128)(2,1)}), bf16[512,768]{1,0:T(8,128)(2,1)}) %reduce-scatter.20.cloned.1.call-update) | async-done | bytes 786448 | tf_op jit(solution)/shard_map/reduce_scatter | solution.py:80
  1077.5 50.8 %reduce-scatter.18.cloned.1.call-done = bf16[128,2048]{1,0:T(8,128)(2,1)} async-done(((bf16[1024,2048]{1,0:T(8,128)(2,1)}), bf16[128,2048]{1,0:T(8,128)(2,1)}) %reduce-scatter.18.cloned.1.call-update) | async-done | bytes 524304 | tf_op jit(solution)/shard_map/reduce_scatter | solution.py:80
  1129.6 53.6 %reduce-scatter.14.cloned.1.call-done = bf16[128,2048]{1,0:T(8,128)(2,1)} async-done(((bf16[1024,2048]{1,0:T(8,128)(2,1)}), bf16[128,2048]{1,0:T(8,128)(2,1)}) %reduce-scatter.14.cloned.1.call-update) | async-done | bytes 524304 | tf_op jit(solution)/shard_map/reduce_scatter | solution.py:80
  1190.2 22.8 %reduce-scatter.22.cloned.1.call-done = bf16[64,2048]{1,0:T(8,128)(2,1)} async-done(((bf16[256,2048]{1,0:T(8,128)(2,1)}), bf16[64,2048]{1,0:T(8,128)(2,1)}) %reduce-scatter.22.cloned.1.call-update) | async-done | bytes 262160 | tf_op jit(solution)/shard_map/reduce_scatter | solution.py:80
  1213.1 6.7 multiply_subtract_fusion.2
  (163 shorter events, 116.8 us)
Async XLA Ops:
  7.2 74.6 %all-gather.24.cloned.1.call-start = ((), (), s32[]{:S(2)}) async-start(), calls=%async_computation.27 | async-start | bytes 4718592 | tf_op jit(solution)/shard_map/all_gather | solution.py:76
  7.9 114.3 %all-gather.12.cloned.1.call-start = ((), (), s32[]{:S(2)}) async-start(), calls=%async_computation.13 | async-start | bytes 3932160 | tf_op jit(solution)/shard_map/all_gather | solution.py:76
  12.3 26.7 %copy-start.27 = (s32[16]{0:T(128)S(1)}, s32[16]{0:T(128)}, u32[]{:S(2)}) copy-start(s32[16]{0:T(128)} %param.17) | copy-start | bytes 196
  12.4 27.5 %copy-start.21 = (f32[2,64]{1,0:T(2,128)S(1)}, f32[2,64]{1,0:T(2,128)}, u32[]{:S(2)}) copy-start(f32[2,64]{1,0:T(2,128)} %param.21) | copy-start | bytes 1540
  37.2 113.8 %all-gather.14.cloned.1.call-start = ((), (), s32[]{:S(2)}) async-start(), calls=%async_computation.14 | async-start | bytes 1310720 | tf_op jit(solution)/shard_map/all_gather | solution.py:76
  39.0 181.9 %reduce-scatter.12.cloned.1.call-start = ((), (), s32[]{:S(2)}) async-start(), calls=%async_computation.15 | async-start | bytes 4718592 | tf_op jit(solution)/shard_map/reduce_scatter | solution.py:80
  80.0 48.9 %copy-start.16 = (f32[1,2048]{1,0:T(1,128)}, f32[1,2048]{1,0:T(1,128)S(1)}, u32[]{:S(2)}) copy-start(f32[1,2048]{1,0:T(1,128)S(1)} %get-tuple-element.63) | copy-start | bytes 24580
  84.9 44.0 %copy-start.19 = (f32[1024]{0:T(1024)}, f32[1024]{0:T(1024)S(1)}, u32[]{:S(2)}) copy-start(f32[1024]{0:T(1024)S(1)} %add_rsqrt_fusion) | copy-start | bytes 12292
  143.8 11.7 copy-start.13
  155.5 216.5 %all-gather.18.cloned.1.call-start = ((), (), s32[]{:S(2)}) async-start(), calls=%async_computation.17 | async-start | bytes 10485760 | tf_op jit(solution)/shard_map/all_gather | solution.py:76
  165.1 55.7 %copy-start.1 = (bf16[1,128,2048]{2,1,0:T(8,128)(2,1)S(1)}, bf16[1,128,2048]{2,1,0:T(8,128)(2,1)}, u32[]{:S(2)}) copy-start(bf16[1,128,2048]{2,1,0:T(8,128)(2,1)} %param.15) | copy-start | bytes 1572868
  207.5 202.0 %all-gather.16.cloned.1.call-start = ((), (), s32[]{:S(2)}) async-start(), calls=%async_computation.16 | async-start | bytes 4718592 | tf_op jit(solution)/shard_map/all_gather | solution.py:76
  224.2 268.3 %all-gather.20.cloned.1.call-start = ((), (), s32[]{:S(2)}) async-start(), calls=%async_computation.18 | async-start | bytes 5242880 | tf_op jit(solution)/shard_map/all_gather | solution.py:76
  227.0 302.8 %all-gather.26.cloned.1.call-start = ((), (), s32[]{:S(2)}) async-start(), calls=%async_computation.28 | async-start | bytes 4718592 | tf_op jit(solution)/shard_map/all_gather | solution.py:76
  227.8 381.3 %reduce-scatter.16.cloned.1.call-start = ((), (), s32[]{:S(2)}) async-start(), calls=%async_computation.20 | async-start | bytes 4718592 | tf_op jit(solution)/shard_map/reduce_scatter | solution.py:80
  557.5 51.5 %copy-start.4 = (bf16[128,2048]{1,0:T(8,128)(2,1)S(1)}, bf16[128,2048]{1,0:T(8,128)(2,1)}, u32[]{:S(2)}) copy-start(bf16[128,2048]{1,0:T(8,128)(2,1)} %reduce-scatter.12.cloned.1.call-done) | copy-start | bytes 1572868
  557.6 92.4 %all-gather.22.cloned.1.call-start = ((), (), s32[]{:S(2)}) async-start(), calls=%async_computation.21 | async-start | bytes 4718592 | tf_op jit(solution)/shard_map/all_gather | solution.py:76
  613.1 183.7 %reduce-scatter.24.cloned.1.call-start = ((), (), s32[]{:S(2)}) async-start(), calls=%async_computation.25 | async-start | bytes 10485760 | tf_op jit(solution)/shard_map/reduce_scatter | solution.py:80
  627.2 249.8 %reduce-scatter.26.cloned.1.call-start = ((), (), s32[]{:S(2)}) async-start(), calls=%async_computation.26 | async-start | bytes 5242880 | tf_op jit(solution)/shard_map/reduce_scatter | solution.py:80
  636.7 378.6 %reduce-scatter.28.cloned.1.call-start = ((), (), s32[]{:S(2)}) async-start(), calls=%async_computation.29 | async-start | bytes 1081344
  700.2 373.5 %reduce-scatter.20.cloned.1.call-start = ((), (), s32[]{:S(2)}) async-start(), calls=%async_computation.23 | async-start | bytes 3932160 | tf_op jit(solution)/shard_map/reduce_scatter | solution.py:80
  708.3 419.9 %reduce-scatter.18.cloned.1.call-start = ((), (), s32[]{:S(2)}) async-start(), calls=%async_computation.22 | async-start | bytes 4718592 | tf_op jit(solution)/shard_map/reduce_scatter | solution.py:80
  708.9 474.3 %reduce-scatter.14.cloned.1.call-start = ((), (), s32[]{:S(2)}) async-start(), calls=%async_computation.19 | async-start | bytes 4718592 | tf_op jit(solution)/shard_map/reduce_scatter | solution.py:80
  796.8 219.9 %all-to-all-start.3 = ((bf16[8,64,2048]{2,1,0:T(8,128)(2,1)}), bf16[8,64,2048]{2,1,0:T(8,128)(2,1)}, u32[]{:S(2)}, u32[]{:S(2)}) async-start(bf16[8,64,2048]{2,1,0:T(8,128)(2,1)} %bitcast.144), calls=%async_computation.10 | async-start | bytes 4194304 | tf_op jit(solution)/shard_map/all_to_all | solution.py:84
  801.2 411.9 %reduce-scatter.22.cloned.1.call-start = ((), (), s32[]{:S(2)}) async-start(), calls=%async_computation.24 | async-start | bytes 1310720 | tf_op jit(solution)/shard_map/reduce_scatter | solution.py:80
  801.7 82.7 %copy-start.14 = (bf16[4,64,1024]{2,1,0:T(8,128)(2,1)S(1)}, bf16[4,64,1024]{2,1,0:T(8,128)(2,1)}, u32[]{:S(2)}) copy-start(bf16[4,64,1024]{2,1,0:T(8,128)(2,1)} %copy-done.13) | copy-start | bytes 1572868
  884.3 131.8 %copy-start.22 = (f32[2,64]{1,0:T(2,128)S(1)}, f32[2,64]{1,0:T(2,128)}, u32[]{:S(2)}) copy-start(f32[2,64]{1,0:T(2,128)} %param.21) | copy-start | bytes 1540
  884.3 131.8 %copy-start.23 = (f32[2,64]{1,0:T(2,128)S(1)}, f32[2,64]{1,0:T(2,128)}, u32[]{:S(2)}) copy-start(f32[2,64]{1,0:T(2,128)} %param.28) | copy-start | bytes 1540
  884.4 131.8 %copy-start.24 = (f32[2,64]{1,0:T(2,128)S(1)}, f32[2,64]{1,0:T(2,128)}, u32[]{:S(2)}) copy-start(f32[2,64]{1,0:T(2,128)} %param.29) | copy-start | bytes 1540
  1032.0 151.2 %copy-start.6 = (bf16[128,2048]{1,0:T(8,128)(2,1)S(1)}, bf16[128,2048]{1,0:T(8,128)(2,1)}, u32[]{:S(2)}) copy-start(bf16[128,2048]{1,0:T(8,128)(2,1)} %reduce-scatter.16.cloned.1.call-done) | copy-start | bytes 1572868
  1032.0 151.2 %copy-start.7 = (bf16[1,128,2048]{2,1,0:T(8,128)(2,1)S(1)}, bf16[1,128,2048]{2,1,0:T(8,128)(2,1)}, u32[]{:S(2)}) copy-start(bf16[1,128,2048]{2,1,0:T(8,128)(2,1)} %param.16) | copy-start | bytes 1572868
  1073.6 112.6 %all-to-all-start.2 = ((bf16[8,64,768]{2,1,0:T(8,128)(2,1)}), bf16[8,64,768]{2,1,0:T(8,128)(2,1)S(1)}, u32[]{:S(2)}, u32[]{:S(2)}) async-start(bf16[8,64,768]{2,1,0:T(8,128)(2,1)} %bitcast.147), calls=%async_computation.7 | async-start | bytes 1572864 | tf_op jit(solution)/shard_map/all_to_all | solution.py:84
  (18 other events, 98.5 us)
Sparse Core Ops, SparseCore 0:
  9.9 47.1 all-gather.23
  58.7 63.5 all-gather.11
  124.3 26.5 all-gather.13
  155.7 65.1 reduce-scatter.11
  222.4 149.6 all-gather.17
  374.5 34.9 all-gather.15
  411.7 80.7 all-gather.19
  494.6 35.2 all-gather.25
  557.7 51.3 reduce-scatter.15
  613.2 36.6 all-gather.21
  652.3 144.4 reduce-scatter.23
  799.5 77.4 reduce-scatter.25
  879.9 135.3 reduce-scatter.27
  1017.4 56.1 reduce-scatter.19
  1076.9 51.3 reduce-scatter.17
  1131.8 51.3 reduce-scatter.13
  1185.9 27.1 reduce-scatter.21

commit v2 on v1

v2 whole, which is shorter than its diff:
```python
import math

import jax
import jax.numpy as jnp
from jax import lax
from jax.experimental import pallas as pl
from jax.experimental.pallas import tpu as pltpu
from jax.sharding import PartitionSpec as P

D = 2048
HEADS = 32
HEAD = 64
FF = 8192
STEP = 5

norm_eps = 1e-05
rope_base = 130000.0
beta_one = 0.9
beta_two = 0.95
adam_eps = 1e-08
decay_rate = 0.1
gain_rate = 0.4
masked = -1e30
score_scale = HEAD ** (-0.5)
pair_width = 2 * HEAD
query_block = 256

bf16 = jnp.bfloat16
f32 = jnp.float32


def rms_scale(values):
    return lax.rsqrt(jnp.mean(values * values, axis=-1, keepdims=True) + norm_eps)


def angle_tables(positions):
    index = jnp.arange(HEAD // 2, dtype=f32)
    freqs = jnp.power(f32(rope_base), -2.0 * index / HEAD)
    phase = positions.astype(f32)[:, None] * freqs[None, :]
    return jnp.tile(jnp.cos(phase), (1, 4)), jnp.tile(jnp.sin(phase), (1, 4))


def dot(first, second, core=None):
    return jnp.dot(first, second, preferred_element_type=f32)


def contract_last(first, second, core=None):
    return lax.dot_general(first, second, (((1,), (1,)), ((), ())), preferred_element_type=f32)


def contract_first(first, second):
    return lax.dot_general(first, second, (((0,), (0,)), ((), ())), preferred_element_type=f32)


def adam_step(weight, grad, first, second, rate, decay):
    first = beta_one * first + (1.0 - beta_one) * grad
    second = beta_two * second + (1.0 - beta_two) * grad * grad
    corrected_first = first / (1.0 - beta_one**STEP)
    corrected_second = second / (1.0 - beta_two**STEP)
    fresh = weight - rate * (
        corrected_first / (jnp.sqrt(corrected_second) + adam_eps) + decay * weight
    )
    return (fresh, first, second)


def swiglu(gate_both, grad_act):
    rows, columns = gate_both.shape
    hidden = columns // 2
    block = 256

    def kernel(gate_ref, grad_ref, activation_out, grad_out):
        gate_part, up_part = gate_ref[:, :hidden], gate_ref[:, hidden:]
        grad = grad_ref[...]
        sigmoid = jax.nn.sigmoid(gate_part)
        gate_act = gate_part * sigmoid
        activation_out[...] = (gate_act * up_part).astype(bf16)
        grad_out[:, :hidden] = (
            grad * up_part * sigmoid * (1.0 + gate_part * (1.0 - sigmoid))
        ).astype(bf16)
        grad_out[:, hidden:] = (grad * gate_act).astype(bf16)

    def spec(width):
        return pl.BlockSpec((block, width), lambda step: (step, 0))

    return pl.pallas_call(
        kernel,
        grid=(rows // block,),
        in_specs=[spec(columns), spec(hidden)],
        out_specs=[spec(hidden), spec(columns)],
        out_shape=[
            jax.ShapeDtypeStruct((rows, hidden), bf16),
            jax.ShapeDtypeStruct((rows, columns), bf16),
        ],
        compiler_params=pltpu.CompilerParams(vmem_limit_bytes=40 * 2**20),
        cost_estimate=pl.CostEstimate(
            flops=20 * rows * hidden, bytes_accessed=18 * rows * hidden, transcendentals=rows * hidden
        ),
        name="swiglu",
    )(gate_both, grad_act)


def write_step(refs, grad, rate):
    weight_ref, first_ref, second_ref, grad_out, new_out, moment_out, square_out = refs
    fresh, first, second = adam_step(
        weight_ref[...], grad, first_ref[...], second_ref[...], rate, decay_rate
    )
    grad_out[...] = grad
    new_out[...] = fresh
    moment_out[...] = first
    square_out[...] = second


def gate_step(pieces, weight, first, second, rate, sharers, units):
    ranks, groups, rows, _ = pieces.shape
    block = pl.BlockSpec(
        (rows, sharers * ranks * units), lambda kind, group: (0, kind * groups + group)
    )

    def kernel(pieces_ref, *refs):
        parts = [pieces_ref[rank, 0].astype(f32) for rank in range(ranks)]
        grad = jnp.concatenate(
            [
                part[:, plane * units : (plane + 1) * units]
                for plane in range(sharers)
                for part in parts
            ],
            axis=1,
        )
        write_step(refs, grad, rate)

    return pl.pallas_call(
        kernel,
        grid=(2, groups),
        in_specs=[
            pl.BlockSpec(
                (ranks, 1, rows, sharers * units),
                lambda kind, group: (0, group, 0, kind),
            )
        ]
        + [block] * 3,
        out_specs=[block] * 4,
        out_shape=[jax.ShapeDtypeStruct(weight.shape, f32)] * 4,
        compiler_params=pltpu.CompilerParams(vmem_limit_bytes=40 * 2**20),
        cost_estimate=pl.CostEstimate(
            flops=20 * weight.size, bytes_accessed=30 * weight.size, transcendentals=weight.size
        ),
        name="gate_step",
    )(pieces, weight, first, second)


def attn_step(pieces, out_grad, weight, first, second, rate):
    ranks, rows, columns = pieces.shape
    local_width = columns // 3
    block = pl.BlockSpec((rows, ranks * local_width), lambda kind: (0, kind))

    def kernel(pieces_ref, out_ref, *refs):
        kind = pl.program_id(0)

        @pl.when(kind < 3)
        def _():
            parts = [pieces_ref[rank].astype(f32) for rank in range(ranks)]
            grad = jnp.concatenate(
                [
                    part[:, start : start + HEAD]
                    for start in range(0, local_width, HEAD)
                    for part in parts
                ],
                axis=1,
            )
            write_step(refs, grad, rate)

        @pl.when(kind == 3)
        def _():
            write_step(refs, out_ref[...], rate)

    return pl.pallas_call(
        kernel,
        grid=(4,),
        in_specs=[
            pl.BlockSpec((ranks, rows, local_width), lambda kind: (0, 0, jnp.minimum(kind, 2))),
            pl.BlockSpec((rows, ranks * local_width), lambda kind: (0, 0)),
        ]
        + [block] * 3,
        out_specs=[block] * 4,
        out_shape=[jax.ShapeDtypeStruct(weight.shape, f32)] * 4,
        compiler_params=pltpu.CompilerParams(vmem_limit_bytes=40 * 2**20),
        cost_estimate=pl.CostEstimate(
            flops=20 * weight.size, bytes_accessed=30 * weight.size, transcendentals=weight.size
        ),
        name="attn_step",
    )(pieces, out_grad, weight, first, second)


def first_half(shape):
    return lax.broadcasted_iota(jnp.int32, shape, 1) % HEAD < HEAD // 2


def of_head(values, head, axis=1):
    return jnp.where(
        lax.broadcasted_iota(jnp.int32, values.shape, axis) // HEAD == head,
        values,
        jnp.zeros_like(values),
    )


def rotate(values, cosine, sine):
    ahead = pltpu.roll(values, pair_width - HEAD // 2, 1)
    behind = pltpu.roll(values, HEAD // 2, 1)
    return values * cosine + jnp.where(first_half(values.shape), -ahead, behind) * sine


def unrotate(values, cosine, sine):
    sined = values * sine
    ahead = pltpu.roll(sined, pair_width - HEAD // 2, 1)
    behind = pltpu.roll(sined, HEAD // 2, 1)
    return values * cosine + jnp.where(first_half(values.shape), ahead, -behind)


def forward_kernel(
    query_ref,
    key_ref,
    value_ref,
    cos_rows,
    sin_rows,
    cos_ref,
    sin_ref,
    key_pos,
    query_pos,
    query_out,
    key_out,
    value_out,
    mixed_out,
    total_out,
):
    @pl.when(pl.program_id(1) == 0)
    def _():
        key_out[...] = rotate(key_ref[...], cos_ref[...], sin_ref[...]).astype(bf16)
        value_out[...] = value_ref[...].astype(bf16)

    queries = rotate(query_ref[...], cos_rows[...], sin_rows[...]).astype(bf16)
    query_out[...] = queries
    keys, values = key_out[...], value_out[...]
    allowed = key_pos[:, :1] <= query_pos[...]
    mixed = jnp.zeros((pair_width, queries.shape[0]), f32)
    for head in range(2):
        scores = contract_last(keys, of_head(queries, head) * bf16(score_scale))
        scores = jnp.where(allowed, scores, masked)
        peak = jnp.max(scores, axis=0, keepdims=True)
        weights = jnp.exp(scores - peak)
        total = jnp.sum(weights, axis=0, keepdims=True)
        probs = (weights * (1.0 / total)).astype(bf16)
        mixed += of_head(contract_first(values, probs), head, 0)
        total_out[head] = peak + jnp.log(total)
    mixed_out[...] = mixed.T.astype(bf16)


def backward_kernel(
    query_ref,
    key_ref,
    value_ref,
    grad_ref,
    total_ref,
    cos_rows,
    sin_rows,
    cos_ref,
    sin_ref,
    key_pos,
    query_pos,
    query_out,
    key_out,
    value_out,
    key_sum,
    value_sum,
):
    step = pl.program_id(1)

    @pl.when(step == 0)
    def _():
        key_sum[...] = jnp.zeros_like(key_sum)
        value_sum[...] = jnp.zeros_like(value_sum)

    keys, values = key_ref[...], value_ref[...]
    allowed = key_pos[:, :1] <= query_pos[...]
    grad_query = jnp.zeros((pair_width, query_ref.shape[0]), f32)
    for head in range(2):
        queries = of_head(query_ref[...], head) * bf16(score_scale)
        grads = of_head(grad_ref[...], head)
        scores = jnp.where(allowed, contract_last(keys, queries), masked)
        probs = jnp.exp(scores - total_ref[head])
        grad_probs = contract_last(values, grads)
        delta = jnp.sum(probs * grad_probs, axis=0, keepdims=True)
        grad_scores = (probs * (grad_probs - delta)).astype(bf16)
        value_sum[...] += dot(probs.astype(bf16), grads)
        key_sum[...] += dot(grad_scores, queries)
        grad_query += of_head(contract_first(keys, grad_scores), head, 0)
    query_out[...] = unrotate(
        (grad_query * score_scale).T, cos_rows[...], sin_rows[...]
    ).astype(bf16)

    @pl.when(step == pl.num_programs(1) - 1)
    def _():
        key_out[...] = unrotate(key_sum[...], cos_ref[...], sin_ref[...]).astype(bf16)
        value_out[...] = value_sum[...].astype(bf16)


def attention_specs(seq_len, pairs):
    rows = pl.BlockSpec((query_block, pair_width), lambda pair, step: (step, pair))
    whole = [
        pl.BlockSpec((seq_len, pair_width), lambda pair, step, at=at: (0, at * pairs + pair))
        for at in range(3)
    ]
    tables = [pl.BlockSpec((query_block, pair_width), lambda pair, step: (step, 0))] * 2 + [
        pl.BlockSpec((seq_len, pair_width), lambda pair, step: (0, 0))
    ] * 3
    places = pl.BlockSpec((1, query_block), lambda pair, step: (0, step))
    totals = pl.BlockSpec((2, 1, query_block), lambda pair, step: (pair, 0, step))
    return rows, whole, tables + [places], totals


def attention_forward(projected, tables):
    seq_len = projected.shape[0]
    pairs = projected.shape[1] // 3 // pair_width
    rows, whole, table_specs, totals = attention_specs(seq_len, pairs)
    low = jax.ShapeDtypeStruct((seq_len, pairs * pair_width), bf16)
    cosine, sine, key_pos, query_pos = tables
    return pl.pallas_call(
        forward_kernel,
        grid=(pairs, seq_len // query_block),
        in_specs=[rows, whole[1], whole[2]] + table_specs,
        out_specs=[rows, whole[0], whole[0], rows, totals],
        out_shape=[low] * 4 + [jax.ShapeDtypeStruct((2 * pairs, 1, seq_len), f32)],
        compiler_params=pltpu.CompilerParams(vmem_limit_bytes=40 * 2**20),
        cost_estimate=pl.CostEstimate(
            flops=pairs * seq_len * seq_len,
            bytes_accessed=seq_len * pairs * pair_width,
            transcendentals=0,
        ),
        name="attention_forward",
    )(projected, projected, projected, cosine, sine, cosine, sine, key_pos, query_pos)


def attention_backward(queries, keys, values, grads, totals, tables):
    seq_len = queries.shape[0]
    pairs = queries.shape[1] // pair_width
    rows, whole, table_specs, total_spec = attention_specs(seq_len, pairs)
    low = jax.ShapeDtypeStruct((seq_len, pairs * pair_width), bf16)
    cosine, sine, key_pos, query_pos = tables
    return pl.pallas_call(
        backward_kernel,
        grid=(pairs, seq_len // query_block),
        in_specs=[rows, whole[0], whole[0], rows, total_spec] + table_specs,
        out_specs=[rows, whole[0], whole[0]],
        out_shape=[low] * 3,
        scratch_shapes=[pltpu.VMEM((seq_len, pair_width), f32)] * 2,
        compiler_params=pltpu.CompilerParams(vmem_limit_bytes=40 * 2**20),
        cost_estimate=pl.CostEstimate(
            flops=pairs * seq_len * seq_len,
            bytes_accessed=seq_len * pairs * pair_width,
            transcendentals=0,
        ),
        name="attention_backward",
    )(queries, keys, values, grads, totals, cosine, sine, cosine, sine, key_pos, query_pos)


def swap(values, axis, bits):
    return lax.ppermute(values, axis, [(i, i ^ bits) for i in range(lax.axis_size(axis))])


def bit_of(axis, bit):
    return (lax.axis_index(axis) >> bit) & 1


def pick(values, index, axis):
    return lax.dynamic_index_in_dim(values, index, axis, keepdims=False)


def bit_count(axis):
    return lax.axis_size(axis).bit_length() - 1


def paired(values, axis, bit):
    other = swap(values, axis, 1 << bit)
    mine = bit_of(axis, bit) == 0
    return jnp.stack([jnp.where(mine, values, other), jnp.where(mine, other, values)])


def halved(values, axis, bit):
    values = values.reshape((2, values.shape[0] // 2) + values.shape[1:])
    own = bit_of(axis, bit)
    other = swap(pick(values, 1 - own, 0), axis, 1 << bit)
    return pick(values, own, 0).astype(f32) + other.astype(f32)


def after(values, *others):
    return lax.optimization_barrier((values, others))[0]


def row_orders():
    bits = list(range(1, bit_count("ctx")))
    return bits, bits[::-1]


def gather_even(own):
    orders = row_orders()
    parts = jnp.split(own, 2)
    for step in range(len(orders[0])):
        others = lax.optimization_barrier(
            [swap(part, "ctx", 1 << order[step]) for part, order in zip(parts, orders)]
        )
        merged = []
        for part, other, order in zip(parts, others, orders):
            low = bit_of("ctx", order[step]) == 0
            place = sum(bit > order[step] for bit in order[:step])
            merged.append(
                jnp.stack([jnp.where(low, part, other), jnp.where(low, other, part)], axis=place)
            )
        parts = merged
    return jnp.stack(parts, axis=len(orders[0]))


def gather_odd(even):
    other = swap(even, "ctx", 1)
    low = bit_of("ctx", 0) == 0
    whole = jnp.stack(
        [jnp.where(low, even, other), jnp.where(low, other, even)], axis=even.ndim - 3
    )
    return whole.reshape(-1, even.shape[-1])


def gather_whole(own):
    return lax.all_gather(own, "ctx", axis=0, tiled=True)


def scatter_rows(rows, weight, product, beside=None):
    ranks = lax.axis_size("ctx")
    own_rows = rows.shape[0] // ranks
    core = bit_of("ctx", 0)
    rows = rows.reshape(ranks // 2, 2, own_rows, rows.shape[1])

    def of_core(which):
        return pick(rows, which, 1).reshape(-1, rows.shape[-1])

    other = swap(product(of_core(1 - core), weight, 1 - core).astype(bf16), "ctx", 1)
    total = (product(of_core(core), weight, core) + other.astype(f32)).astype(bf16)
    orders = row_orders()
    count = len(orders[0])
    halves = total.reshape((2,) * count + (2, own_rows // 2, total.shape[-1]))
    parts = [lax.index_in_dim(halves, half, count, keepdims=False) for half in range(2)]
    for step in range(count)[::-1]:
        near, far = [], []
        for part, order in zip(parts, orders):
            place = sum(bit > order[step] for bit in order[:step])
            own = bit_of("ctx", order[step])
            near.append(pick(part, own, place))
            far.append(pick(part, 1 - own, place).astype(bf16))
        others = [swap(part, "ctx", 1 << order[step]) for part, order in zip(far, orders)]
        if step == 0:
            others, beside = lax.optimization_barrier((others, beside))
        else:
            others = lax.optimization_barrier(others)
        parts = [part.astype(f32) + other.astype(f32) for part, other in zip(near, others)]
    sums = jnp.concatenate(parts)
    return (sums, total) if beside is None else (sums, total, beside)


def exchange_held(pieces):
    pieces = lax.optimization_barrier(pieces)
    held = pieces[:1] + [
        swap(piece, "ctx", offset) for offset, piece in enumerate(pieces) if offset
    ]
    return lax.optimization_barrier(held)


def in_order(held, axis):
    held, me = jnp.stack(held), lax.axis_index("ctx")
    return jnp.stack([pick(held, me ^ rank, 0) for rank in range(held.shape[0])], axis=axis)


def exchange(pieces):
    me = lax.axis_index("ctx")
    return in_order(
        exchange_held([pick(pieces, me ^ offset, 0) for offset in range(pieces.shape[0])]), 0
    )


def body(
    tokens,
    cotangent,
    block_ids,
    attn_weight,
    gate_up,
    down_weight,
    norm_gains,
    attn_first,
    attn_second,
    gate_first,
    gate_second,
    down_first,
    down_second,
    gain_first,
    gain_second,
):
    every = ("dp", "ctx")
    width = attn_weight.shape[1] // 4
    planes = lax.axis_size("dp")
    ranks = lax.axis_size("ctx")
    own_rows = attn_weight.shape[0]
    units = down_weight.shape[0]
    rows = tokens.shape[1]
    half = rows // 2
    seq_len = rows * ranks
    local_heads = HEADS // ranks
    local_width = local_heads * HEAD
    aligned = local_heads == planes
    rank = lax.axis_index("ctx")
    top = bit_count("dp") - 1
    sharers = planes // 2
    side = bit_of("dp", top)
    hidden = sharers * units

    positions = (
        block_ids[:, None] * half + jnp.arange(half, dtype=jnp.int32)[None, :]
    ).reshape(-1)
    cosine, sine = angle_tables(positions)
    tables = (
        cosine,
        sine,
        jnp.broadcast_to(positions[:, None], (seq_len, pair_width)),
        positions[None, :],
    )

    gain_rows = 16
    inputs_even = gather_even(tokens[0])
    grad_out_theirs = swap(cotangent[0], "dp", 1 << top)

    attn_low = attn_weight.astype(bf16)
    qkv_pieces = (
        attn_low[:, : 3 * width]
        .reshape(own_rows, 3, local_heads, ranks, HEAD)
        .transpose(3, 0, 1, 2, 4)
        .reshape(ranks, own_rows, 3 * local_width)
    )
    qkv_own = exchange(qkv_pieces).reshape(ranks * own_rows, 3 * local_width)

    def over_planes(values):
        for bit in range(top):
            values = paired(values, "dp", bit)
        return values.reshape((sharers,) + values.shape[top:])

    gains_low = norm_gains.astype(bf16)
    for bit in range(bit_count("dp")):
        gains_low = paired(gains_low, "dp", bit)
    gains_own = gains_low.reshape(planes, 2 * own_rows)
    up_from = gate_up.shape[1] // 2
    gate_low = gate_up.astype(bf16)

    gain_piece = jnp.pad(
        gains_own, ((0, gain_rows - planes), (0, 2 * hidden - 2 * own_rows))
    )

    def rank_columns(at):
        return jnp.concatenate(
            [
                jnp.concatenate(
                    [
                        lax.dynamic_slice_in_dim(
                            gate_low, kind * up_from + (plane * ranks + at) * units, units, 1
                        )
                        for kind in range(2)
                        for plane in range(group * sharers, (group + 1) * sharers)
                    ],
                    axis=1,
                )
                for group in range(2)
            ]
            + [gain_piece]
        )

    gate_pieces = [rank_columns(rank ^ offset) for offset in range(ranks)]
    out_low = attn_low[:, 3 * width :]
    if aligned:
        out_proj = lax.all_gather(out_low, "dp", axis=0, tiled=True)
    else:
        out_all = lax.all_gather(out_low, every, axis=0, tiled=True)
        out_proj = pick(out_all.reshape(local_heads, ranks, HEAD, width), rank, 1)
        out_proj = out_proj.reshape(local_width, width)
    qkv_own, out_proj, gate_pieces = lax.optimization_barrier((qkv_own, out_proj, gate_pieces))
    qkv = lax.all_gather(qkv_own, "dp", axis=0, tiled=True)
    gate_pieces, inputs_even, grad_out_theirs = lax.optimization_barrier(
        (gate_pieces, inputs_even, grad_out_theirs)
    )
    gate_held = exchange_held(gate_pieces)
    gate_own = in_order([held[: 2 * own_rows].reshape(2, own_rows, -1) for held in gate_held], 1)
    gate_own = gate_own.reshape(2, ranks * own_rows, 2 * hidden)
    gains_low = in_order(
        [held[2 * own_rows : 2 * own_rows + planes, : 2 * own_rows] for held in gate_held], 0
    )
    gains_low = gains_low.reshape(ranks, planes, 2, own_rows).transpose(2, 1, 0, 3)
    gains_low = gains_low.reshape(2, width).astype(f32)
    gain_one, gain_two = gains_low[0], gains_low[1]
    inputs_low = gather_odd(inputs_even)
    inputs_all = inputs_low.astype(f32)
    normed_all = inputs_all * rms_scale(inputs_all)
    hidden_one = (normed_all * gain_one).astype(bf16)
    qkv, hidden_one, gate_own, gain_two, grad_out_own, grad_out_theirs, down = (
        lax.optimization_barrier(
            (
                qkv,
                hidden_one,
                gate_own,
                gain_two,
                cotangent[0],
                grad_out_theirs,
                down_weight.astype(bf16),
            )
        )
    )

    gate_mine = over_planes(pick(gate_own, side, 0))
    gate_halves = jnp.split(pick(gate_own, 1 - side, 0), 2)
    gate_halves[0] = swap(gate_halves[0], "dp", 1 << top)
    grad_out_near = gather_whole(grad_out_own)
    projected = dot(hidden_one, qkv)
    queries, keys, values, mixed_low, totals = attention_forward(projected, tables)
    mixed_low, gate_mine, gate_halves, down, grad_out_near, grad_out_theirs = (
        lax.optimization_barrier(
            (mixed_low, gate_mine, gate_halves, down, grad_out_near, grad_out_theirs)
        )
    )
    grad_out_far = gather_whole(grad_out_theirs)
    gate_halves[1] = swap(gate_halves[1], "dp", 1 << top)

    inputs = tokens[0].astype(f32)
    mixed_out, _, (gate_halves, grad_out_far) = scatter_rows(
        mixed_low, out_proj, dot, (gate_halves, grad_out_far)
    )
    gate_theirs = jnp.concatenate(gate_halves)
    middle = inputs + mixed_out
    inv_two = rms_scale(middle)
    normed_two = middle * inv_two
    hidden_two_own = (normed_two * gain_two).astype(bf16)
    hidden_two_near, hidden_two_theirs, gate_theirs, down = lax.optimization_barrier(
        (
            gather_whole(hidden_two_own),
            swap(hidden_two_own, "dp", 1 << top),
            over_planes(gate_theirs),
            down,
        ),
    )
    hidden_two_far = gather_whole(hidden_two_theirs)
    grad_outs = [grad_out_near, grad_out_far]
    down = over_planes(down).reshape(hidden, width)
    gate = jnp.concatenate(
        [
            jnp.where(side == 0, gate_mine, gate_theirs),
            jnp.where(side == 0, gate_theirs, gate_mine),
        ]
    ).reshape(width, 2 * hidden)

    def mlp(hidden_two, grad_out):
        return swiglu(dot(hidden_two, gate), contract_last(grad_out, down))

    activation_near, grad_both_near = mlp(hidden_two_near, grad_outs[0])
    grad_two, _ = scatter_rows(grad_both_near, gate, contract_last)
    hidden_two_far, grad_outs[1], grad_two = lax.optimization_barrier(
        (hidden_two_far, grad_outs[1], grad_two)
    )
    activation_far, grad_both_far = mlp(hidden_two_far, grad_outs[1])
    activations = [activation_near, activation_far]
    hidden_twos = [hidden_two_near, hidden_two_far]
    grad_boths = [grad_both_near, grad_both_far]

    def gate_terms(group):
        rows_in_group = width // 2
        terms = sum(
            contract_first(
                lax.dynamic_slice_in_dim(hidden_two, group * rows_in_group, rows_in_group, 1),
                grad_both,
            )
            for hidden_two, grad_both in zip(hidden_twos, grad_boths)
        )
        return terms.astype(bf16).reshape(sharers, ranks * own_rows, 2 * hidden)

    def sum_planes(values):
        for bit in range(top)[::-1]:
            values = halved(values.astype(bf16), "dp", bit)
        return values[0]

    grad_two_far, started = scatter_rows(grad_both_far, gate, contract_last)
    hidden_twos, grad_boths, activations, started = lax.optimization_barrier(
        (hidden_twos, grad_boths, activations, started)
    )
    term_theirs = sum_planes(gate_terms(1 - side)).astype(bf16)
    grad_two += swap(grad_two_far.astype(bf16), "dp", 1 << top).astype(f32)
    term_mine = gate_terms(side)
    down_term = sum(contract_first(a, g) for a, g in zip(activations, grad_outs)).astype(bf16)
    grad_two, term_mine, term_theirs, down_term, activations = lax.optimization_barrier(
        (grad_two, term_mine, term_theirs, down_term, activations)
    )
    theirs_halves = jnp.split(term_theirs, 2)
    theirs_halves[0] = swap(theirs_halves[0], "dp", 1 << top)
    output_far, _ = scatter_rows(activations[1], down, dot)
    down_grad = sum_planes(down_term.reshape(sharers, units, width))

    reduced_two = grad_two * gain_two
    grad_gain_two = jnp.sum(grad_two * normed_two, axis=0)
    grad_after = cotangent[0].astype(f32) + inv_two * (
        reduced_two - normed_two * jnp.mean(reduced_two * normed_two, axis=-1, keepdims=True)
    )
    after_low = gather_whole(grad_after.astype(bf16))
    grad_mixed = contract_last(after_low, out_proj).astype(bf16)
    out_term = contract_first(mixed_low, after_low).astype(bf16)
    grad_mixed, out_term, term_mine, theirs_halves, down_grad, output_far = (
        lax.optimization_barrier(
            (grad_mixed, out_term, term_mine, theirs_halves, down_grad, output_far)
        )
    )
    theirs_halves[1] = swap(theirs_halves[1], "dp", 1 << top)
    term_mine = sum_planes(term_mine).astype(bf16)
    grad_proj = jnp.concatenate(
        attention_backward(queries, keys, values, grad_mixed, totals, tables), axis=1
    )
    qkv_term = contract_first(hidden_one, grad_proj).astype(bf16)
    if aligned:
        out_term = out_term.reshape(width, local_width)
        qkv_term = jnp.concatenate([qkv_term, out_term], axis=1)
    else:
        spread = jnp.zeros((local_heads, ranks, HEAD, width), bf16)
        spread = lax.dynamic_update_index_in_dim(
            spread, out_term.reshape(local_heads, 1, HEAD, width), rank, 1
        )
        out_grad = lax.psum_scatter(
            spread.reshape(HEADS * HEAD, width), every, scatter_dimension=0, tiled=True
        )
    grad_proj, qkv_term, term_mine, theirs_halves = lax.optimization_barrier(
        (grad_proj, qkv_term, term_mine, theirs_halves)
    )
    term_theirs = jnp.concatenate(theirs_halves)
    qkv_term = lax.psum_scatter(qkv_term, "dp", scatter_dimension=0, tiled=True)
    if aligned:
        out_grad = qkv_term[:, 3 * local_width :].reshape(own_rows, width)
        qkv_term = qkv_term[:, : 3 * local_width]
    out_grad = out_grad.astype(f32)
    gain_one_parts = []

    def gained(part, weight, core):
        product = contract_last(part, weight)
        normed_part = pick(normed_all.reshape(ranks // 2, 2, rows, width), core, 1)
        gain_one_parts.append(jnp.sum(product * normed_part.reshape(-1, width), axis=0))
        return product

    grad_one, _ = scatter_rows(grad_proj, qkv, gained)
    grad_gain_one = sum(gain_one_parts)
    inv_one = rms_scale(inputs)
    normed_one = inputs * inv_one
    reduced_one = grad_one * gain_one
    grad_input = grad_after + inv_one * (
        reduced_one - normed_one * jnp.mean(reduced_one * normed_one, axis=-1, keepdims=True)
    )

    output_near, _ = scatter_rows(after(activations[0], grad_proj), down, dot)
    term_cols = jnp.stack(
        [
            jnp.where(side == 0, term_mine, term_theirs),
            jnp.where(side == 0, term_theirs, term_mine),
        ]
    )
    term_cols = term_cols.reshape(2, ranks, own_rows, 2 * hidden).transpose(1, 0, 2, 3)
    gate_pieces = exchange(term_cols)
    gain_grad = jnp.stack([grad_gain_one, grad_gain_two]).reshape(2, planes, ranks, -1)
    gain_grad = gain_grad.transpose(2, 1, 0, 3)
    for bit in range(bit_count("ctx"))[::-1]:
        gain_grad = halved(gain_grad, "ctx", bit)
    qkv_term, out_grad, gate_pieces, output_near, output_far, grad_input, gain_grad, down_grad = (
        lax.optimization_barrier(
            (
                qkv_term,
                out_grad,
                gate_pieces,
                output_near,
                output_far,
                grad_input,
                gain_grad,
                down_grad,
            )
        )
    )
    qkv_pieces = exchange(qkv_term.reshape(ranks, own_rows, 3 * local_width))
    output_far = swap(output_far.astype(bf16), "dp", 1 << top)
    gain_grad = gain_grad[0]
    for bit in range(bit_count("dp"))[::-1]:
        gain_grad = halved(gain_grad, "dp", bit)
    qkv_pieces, output_far, gain_grad = lax.optimization_barrier(
        (qkv_pieces, output_far, gain_grad)
    )
    outputs = middle + output_near + output_far.astype(f32)
    gain_grad = gain_grad.reshape(2, -1)
    attn_grad, attn_new, attn_moment, attn_square = attn_step(
        qkv_pieces, out_grad, attn_weight, attn_first, attn_second, 3.0 / math.sqrt(D)
    )
    gate_grad, gate_new, gate_moment, gate_square = gate_step(
        gate_pieces, gate_up, gate_first, gate_second, 3.0 / math.sqrt(D), sharers, units
    )
    down_new, down_moment, down_square = adam_step(
        down_weight, down_grad, down_first, down_second, 3.0 / math.sqrt(FF), decay_rate
    )
    gain_new, gain_moment, gain_square = adam_step(
        norm_gains, gain_grad, gain_first, gain_second, gain_rate, 0.0
    )
    return (
        outputs.astype(bf16)[None],
        grad_input.astype(bf16)[None],
        attn_grad,
        gate_grad,
        down_grad,
        gain_grad,
        attn_new,
        gate_new,
        down_new,
        gain_new,
        attn_moment,
        gate_moment,
        down_moment,
        gain_moment,
        attn_square,
        gate_square,
        down_square,
        gain_square,
    )


def solution(mesh):
    acts = P("dp", "ctx", None)
    weight = P(("dp", "ctx"), None)
    gains = P(None, ("dp", "ctx"))
    four = (weight, weight, weight, gains)
    return jax.shard_map(
        body,
        mesh=mesh,
        in_specs=(acts, acts, P()) + four + (weight,) * 6 + (gains,) * 2,
        out_specs=(acts, acts) + four * 4,
        check_vma=False,
    )
```

time: 1230 us -> 716 us (0.58)
  waiting for transfers between devices: 857 us -> 307 us
  blocking collectives: 106 us -> 0 us
  starting transfers between devices: 10.2 us -> 91.2 us
  Pallas kernels: 0 us -> 53.9 us
  matrix products: 137 us -> 86.6 us
  local copies, waits for them, and re-layouts: 39.7 us -> 80.8 us
    reduce_scatter x8 -> x1, waiting for transfers between devices: 381 us -> 0.61 us  [body(): qkv_term = lax.psum_scatter(qkv_term, 'dp', scatter_dimension=0, tiled=True)]
    all_gather x8 -> x7, waiting for transfers between devices: 345 us -> 27 us  [the longest x1 25.9 us: body(): qkv = lax.all_gather(qkv_own, 'dp', axis=0, tiled=True)]
    ppermute x0 -> x84, waiting for transfers between devices: none -> 279 us  [swap(): lax.ppermute(values, axis, [(i, i ^ bits) for i in range(lax.axis_size(ax...]
    unnamed x18 -> x8, waiting for transfers between devices: 131 us -> 0.13 us
    ppermute x0 -> x84, starting transfers between devices: none -> 90.5 us  [swap(): lax.ppermute(values, axis, [(i, i ^ bits) for i in range(lax.axis_size(ax...]
    all_to_all x2 -> x0, blocking collectives: 65.6 us -> none  [exchange(): lax.all_to_all(pieces, 'ctx', split_axis=0, concat_axis=0, tiled=True)]
    pallas_call x0 -> x6, Pallas kernels: none -> 53.9 us  [the longest x1 18.5 us: attention_backward(): pl.pallas_call(backward_kernel, grid=(pairs, seq_len // query_block), in_...]
    all_gather x1 -> x0, blocking collectives: 40 us -> none  [body(): lax.all_gather(norm_gains.astype(bf16), every, axis=1, tiled=True)]
  transfers between devices with their start and end apart: 19 -> 92, of which waited for: 16 -> 45; matrix products, arithmetic and copies ran while one was open for 15% -> 23% of each run, Pallas kernels for 0% -> 4%
where the time goes in v2:
time: 716 us; the launch traced here: 706 us
  waiting for transfers between devices  307 us (43%)
  starting transfers between devices  91.2 us (13%)
  matrix products  86.6 us (12%)
  local copies, waits for them, and re-layouts  80.8 us (11%)
  other arithmetic  69.6 us (10%)
  Pallas kernels  53.9 us (8%)
  between operations  17.5 us (2%)
    ppermute x84, waiting for transfers between devices, swap(): lax.ppermute(values, axis, [(i, i ^ bits) for i in range(lax.axis_size(ax...  279 us
    ppermute x84, starting transfers between devices, swap(): lax.ppermute(values, axis, [(i, i ^ bits) for i in range(lax.axis_size(ax...  90.5 us
    dot_general x9, matrix products, dot(): return jnp.dot(first, second, preferred_element_type=f32)  31.2 us
    unnamed x316, local copies, waits for them, and re-layouts  31 us
    dot_general x9, matrix products, contract_last(): lax.dot_general(first, second, (((1,), (1,)), ((), ())), preferred_elemen...  28.2 us
    dot_general x8, matrix products, contract_first(): lax.dot_general(first, second, (((0,), (0,)), ((), ())), preferred_elemen...  27.2 us
    all_gather x1, waiting for transfers between devices, body(): qkv = lax.all_gather(qkv_own, 'dp', axis=0, tiled=True)  25.9 us
    pallas_call x1, Pallas kernels, attention_backward(): pl.pallas_call(backward_kernel, grid=(pairs, seq_len // query_block), in_...  18.5 us
  transfers between devices with their start and end apart: 92, of which 45 were waited for; matrix products, arithmetic and copies ran while one was open for 23% of the time, Pallas kernels for 4%

profile of v2, /device:TPU:0, one launch (start us, length us, event | category | flops | bytes accessed | tf_op | source)
XLA Modules:
  0.0 706.3 jit_solution(8078847703880586023)
XLA Ops:
  54.4 11.2 %collective-permute-done.11 = bf16[2,64,2048]{2,1,0:T(8,128)(2,1)S(1)} collective-permute-done((bf16[2,64,2048]{2,1,0:T(8,128)(2,1)S(1)}, bf16[2,64,2048]{2,1,0:T(8,128)(2,1)S(1)}, u32[]{:S(2)}, u32[]{:S(2)}) %collective-permute-start.11) | collective-permute-done | bytes 524320 | tf_op jit(solution)/shard_map/ppermute | solution.py:366
  88.2 12.8 %collective-permute-done.19 = bf16[144,1024]{1,0:T(8,128)(2,1)S(1)} collective-permute-done((bf16[144,1024]{1,0:T(8,128)(2,1)}, bf16[144,1024]{1,0:T(8,128)(2,1)S(1)}, u32[]{:S(2)}, u32[]{:S(2)}) %collective-permute-start.19) | collective-permute-done | bytes 294944 | tf_op jit(solution)/shard_map/ppermute | solution.py:366
  120.5 25.9 %all-gather.10.cloned.1.call-done = bf16[2048,768]{1,0:T(8,128)(2,1)} async-done(((bf16[512,768]{1,0:T(8,128)(2,1)}), bf16[2048,768]{1,0:T(8,128)(2,1)}) %all-gather.10.cloned.1.call-update) | async-done | bytes 3145744 | tf_op jit(solution)/shard_map/all_gather | solution.py:588
  153.0 6.4 fusion.96.query_ref.key_ref.value_ref
  159.7 17.7 %attention_forward.1 = (bf16[1024,256]{1,0:T(8,128)(2,1)S(1)}, bf16[1024,256]{1,0:T(8,128)(2,1)S(1)}, bf16[1024,256]{1,0:T(8,128)(2,1)S(1)}, bf16[1024,256]{1,0:T(8,128)(2,1)S(1)}, f32[4,1,1024]{2,1,0:T(1,128)S(1)}) custom-call(f32[1024,768]{1,0:T(8,128)S(1)} %fusion.96.query_ref.key_ref.value_ref, f32[1024,768]{1,0:T(8,128)S(1)} %fusion.96.query_ref.key_ref.value_ref, ...), custom_call_target="tpu_custom_call" | custom-call | flops 2097152 | bytes 262144 | tf_op jit(solution)/shard_map/attention_forward/pallas_call | solution.py:326
  177.4 6.9 collective-permute-done.22
  189.4 4.5 collective-permute-done.24
  202.2 11.6 %collective-permute-done.25 = bf16[2,64,2048]{2,1,0:T(8,128)(2,1)} collective-permute-done((bf16[2,64,2048]{2,1,0:T(8,128)(2,1)}, bf16[2,64,2048]{2,1,0:T(8,128)(2,1)}, u32[]{:S(2)}, u32[]{:S(2)}) %collective-permute-start.25) | collective-permute-done | bytes 524320 | tf_op jit(solution)/shard_map/ppermute | solution.py:366
  242.8 33.4 %collective-permute-done.31 = bf16[512,1024]{1,0:T(8,128)(2,1)S(1)} collective-permute-done((bf16[512,1024]{1,0:T(8,128)(2,1)S(1)}, bf16[512,1024]{1,0:T(8,128)(2,1)S(1)}, u32[]{:S(2)}, u32[]{:S(2)}) %collective-permute-start.31) | collective-permute-done | bytes 1048608 | tf_op jit(solution)/shard_map/ppermute | solution.py:366
  284.5 4.5 fusion.97.gate_ref
  289.0 13.6 %collective-permute-done.32 = bf16[256,2048]{1,0:T(8,128)(2,1)S(1)} collective-permute-done((bf16[256,2048]{1,0:T(8,128)(2,1)S(1)}, bf16[256,2048]{1,0:T(8,128)(2,1)S(1)}, u32[]{:S(2)}, u32[]{:S(2)}) %collective-permute-start.32) | collective-permute-done | bytes 1048608 | tf_op jit(solution)/shard_map/ppermute | solution.py:366
  323.2 11.5 %collective-permute-done.34 = bf16[2,64,2048]{2,1,0:T(8,128)(2,1)S(1)} collective-permute-done((bf16[2,64,2048]{2,1,0:T(8,128)(2,1)S(1)}, bf16[2,64,2048]{2,1,0:T(8,128)(2,1)S(1)}, u32[]{:S(2)}, u32[]{:S(2)}) %collective-permute-start.34) | collective-permute-done | bytes 524320 | tf_op jit(solution)/shard_map/ppermute | solution.py:366
  338.3 4.7 collective-permute-done.36
  345.5 7.7 %fusion.99.gate_ref = f32[1024,1024]{1,0:T(8,128)S(1)} fusion(bf16[1024,2048]{1,0:T(8,128)(2,1)} %all-gather.18.cloned.1.call-done, bf16[2048,1024]{1,0:T(8,128)(2,1)} %bitcast.568), kind=kOutput, calls=%fused_computation.465 | convolution fusion | flops 4294967296 | bytes 12582912 | tf_op jit(solution)/shard_map/dot_general | solution.py:44
  364.0 4.5 collective-permute-done.38
  368.5 5.6 add_convert_fusion.6
  405.3 9.3 %collective-permute-done.44 = bf16[1,512,1024]{2,1,0:T(8,128)(2,1)S(1)} collective-permute-done((bf16[1,512,1024]{2,1,0:T(8,128)(2,1)S(1)}, bf16[1,512,1024]{2,1,0:T(8,128)(2,1)S(1)}, u32[]{:S(2)}, u32[]{:S(2)}) %collective-permute-start.44) | collective-permute-done | bytes 1048608 | tf_op jit(solution)/shard_map/ppermute | solution.py:366
  416.0 7.6 %collective-permute-done.43 = bf16[128,2048]{1,0:T(8,128)(2,1)S(1)} collective-permute-done((bf16[128,2048]{1,0:T(8,128)(2,1)S(1)}, bf16[128,2048]{1,0:T(8,128)(2,1)S(1)}, u32[]{:S(2)}, u32[]{:S(2)}) %collective-permute-start.43) | collective-permute-done | bytes 524320 | tf_op jit(solution)/shard_map/ppermute | solution.py:366
  447.9 8.3 %collective-permute-done.48 = bf16[2,64,2048]{2,1,0:T(8,128)(2,1)} collective-permute-done((bf16[2,64,2048]{2,1,0:T(8,128)(2,1)}, bf16[2,64,2048]{2,1,0:T(8,128)(2,1)}, u32[]{:S(2)}, u32[]{:S(2)}) %collective-permute-start.48) | collective-permute-done | bytes 524320 | tf_op jit(solution)/shard_map/ppermute | solution.py:366
  462.6 19.8 %collective-permute-done.46 = bf16[1,256,2048]{2,1,0:T(8,128)(2,1)} collective-permute-done((bf16[1,256,2048]{2,1,0:T(8,128)(2,1)}, bf16[1,256,2048]{2,1,0:T(8,128)(2,1)}, u32[]{:S(2)}, u32[]{:S(2)}) %collective-permute-start.46) | collective-permute-done | bytes 1048608 | tf_op jit(solution)/shard_map/ppermute | solution.py:366
  486.2 4.6 convolution_convert_fusion.6
  492.2 18.5 %attention_backward.1 = (bf16[1024,256]{1,0:T(8,128)(2,1)S(1)}, bf16[1024,256]{1,0:T(8,128)(2,1)S(1)}, bf16[1024,256]{1,0:T(8,128)(2,1)S(1)}) custom-call(bf16[1024,256]{1,0:T(8,128)(2,1)S(1)} %copy-done.13, bf16[1024,256]{1,0:T(8,128)(2,1)S(1)} %copy-done.15, bf16[1024,256]{1,0:T(8,128)(2,1)S(1)} %copy-done.17, ...), custom_call_target="tpu_custom_call" | custom-call | flops 2097152 | bytes 262144 | tf_op jit(solution)/shard_map/attention_backward/pallas_call | solution.py:348
  521.4 5.4 convolution_convert_fusion
  529.2 23.5 %collective-permute-done.52 = bf16[1,512,1024]{2,1,0:T(8,128)(2,1)} collective-permute-done((bf16[1,512,1024]{2,1,0:T(8,128)(2,1)}, bf16[1,512,1024]{2,1,0:T(8,128)(2,1)}, u32[]{:S(2)}, u32[]{:S(2)}) %collective-permute-start.52) | collective-permute-done | bytes 1048608 | tf_op jit(solution)/shard_map/ppermute | solution.py:366
  561.6 4.9 fusion.3
  573.1 11.7 %collective-permute-done.58 = bf16[2,64,1024]{2,1,0:T(8,128)(2,1)S(1)} collective-permute-done((bf16[2,64,1024]{2,1,0:T(8,128)(2,1)S(1)}, bf16[2,64,1024]{2,1,0:T(8,128)(2,1)S(1)}, u32[]{:S(2)}, u32[]{:S(2)}) %collective-permute-start.58) | collective-permute-done | bytes 262176 | tf_op jit(solution)/shard_map/ppermute | solution.py:366
  614.4 5.4 collective-permute-done.68
  645.2 7.8 %multiply_subtract_fusion = (f32[256,2048]{1,0:T(8,128)}, f32[256,2048]{1,0:T(8,128)}, f32[256,2048]{1,0:T(8,128)}) fusion(f32[256,2048]{1,0:T(8,128)} %param.20, f32[256,2048]{1,0:T(8,128)} %fusion.5, f32[256,2048]{1,0:T(8,128)} %param.26, f32[256,2048]{1,0:T(8,128)} %param.27), kind=kLoop, calls=%fused_computation.54 | loop fusion | flops 7864320 | bytes 14680064 | tf_op jit(solution)/shard_map/sub | solution.py:60
  653.7 10.0 %gate_step.1 = (f32[64,16384]{1,0:T(8,128)}, f32[64,16384]{1,0:T(8,128)}, f32[64,16384]{1,0:T(8,128)}, f32[64,16384]{1,0:T(8,128)}) custom-call(bf16[8,2,64,1024]{3,2,1,0:T(8,128)(2,1)S(1)} %dynamic-slice_dynamic-update-slice_fusion.pieces_ref, f32[64,16384]{1,0:T(8,128)S(1)} %copy-done, f32[64,16384]{1,0:T(8,128)S(1)} %copy-done.2, f32[64,16384]{1,0:T(8,128)} %refs_2_.3), custom_call_target="tpu_custom_call" | custom-call | flops 20971520 | bytes 31457280 | tf_op jit(solution)/shard_map/gate_step/pallas_call | solution.py:131
  667.8 4.9 collective-permute-done.78
  673.1 19.8 %collective-permute-done.81 = bf16[128,2048]{1,0:T(8,128)(2,1)S(1)} collective-permute-done((bf16[128,2048]{1,0:T(8,128)(2,1)S(1)}, bf16[128,2048]{1,0:T(8,128)(2,1)S(1)}, u32[]{:S(2)}, u32[]{:S(2)}) %collective-permute-start.81) | collective-permute-done | bytes 524320 | tf_op jit(solution)/shard_map/ppermute | solution.py:366
  694.5 4.8 attn_step.1
  (712 shorter events, 340.0 us)
Async XLA Ops:
  7.2 60.6 %all-gather.8.cloned.1.call-start = ((), (), s32[]{:S(2)}) async-start(), calls=%async_computation.1 | async-start | bytes 1310720 | tf_op jit(solution)/shard_map/all_gather | solution.py:582
  14.6 24.3 %collective-permute-start.1 = (bf16[64,768]{1,0:T(8,128)(2,1)}, bf16[64,768]{1,0:T(8,128)(2,1)}, u32[]{:S(2)}, u32[]{:S(2)}) collective-permute-start(bf16[64,768]{1,0:T(8,128)(2,1)} %get-tuple-element.212), channel_id=1, source_target_pairs={{0,2},{1,3},{2,0},{3,1},{4,6},{5,7},{6,4},{7,5},{8,10},{9,11},{10,... | collective-permute-start | bytes 294920 | tf_op jit(solution)/shard_map/ppermute | solution.py:366
  17.1 24.3 %collective-permute-start.2 = (bf16[64,768]{1,0:T(8,128)(2,1)}, bf16[64,768]{1,0:T(8,128)(2,1)}, u32[]{:S(2)}, u32[]{:S(2)}) collective-permute-start(bf16[64,768]{1,0:T(8,128)(2,1)} %get-tuple-element.213), channel_id=1, source_target_pairs={{0,3},{1,2},{2,1},{3,0},{4,7},{5,6},{6,5},{7,4},{8,11},{9,10},{10,... | collective-permute-start | bytes 294920 | tf_op jit(solution)/shard_map/ppermute | solution.py:366
  17.2 25.6 %collective-permute-start.3 = (bf16[64,768]{1,0:T(8,128)(2,1)}, bf16[64,768]{1,0:T(8,128)(2,1)}, u32[]{:S(2)}, u32[]{:S(2)}) collective-permute-start(bf16[64,768]{1,0:T(8,128)(2,1)} %get-tuple-element.214), channel_id=1, source_target_pairs={{0,4},{1,5},{2,6},{3,7},{4,0},{5,1},{6,2},{7,3},{8,12},{9,13},{10,... | collective-permute-start | bytes 294920 | tf_op jit(solution)/shard_map/ppermute | solution.py:366
  20.7 125.8 %all-gather.10.cloned.1.call-start = ((), (), s32[]{:S(2)}) async-start(), calls=%async_computation.2 | async-start | bytes 3932160 | tf_op jit(solution)/shard_map/all_gather | solution.py:588
  44.5 27.3 %collective-permute-start.13 = (bf16[128,2048]{1,0:T(8,128)(2,1)S(1)}, bf16[128,2048]{1,0:T(8,128)(2,1)S(1)}, u32[]{:S(2)}, u32[]{:S(2)}) collective-permute-start(bf16[128,2048]{1,0:T(8,128)(2,1)S(1)} %bitcast.564), channel_id=1, source_target_pairs={{0,16},{8,24},{16,0},{24,8},{1,17},{9,25},{17,1},{25,9},{2,18},{10... | collective-permute-start | bytes 1572872 | tf_op jit(solution)/shard_map/ppermute | solution.py:366
  75.0 26.0 %collective-permute-start.19 = (bf16[144,1024]{1,0:T(8,128)(2,1)}, bf16[144,1024]{1,0:T(8,128)(2,1)S(1)}, u32[]{:S(2)}, u32[]{:S(2)}) collective-permute-start(bf16[144,1024]{1,0:T(8,128)(2,1)} %get-tuple-element.253), channel_id=1, source_target_pairs={{0,5},{1,4},{2,7},{3,6},{4,1},{5,0},{6,3},{7,2},{8,13},{9,12},{10,... | collective-permute-start | bytes 884744 | tf_op jit(solution)/shard_map/ppermute | solution.py:366
  75.2 25.8 %collective-permute-start.20 = (bf16[144,1024]{1,0:T(8,128)(2,1)}, bf16[144,1024]{1,0:T(8,128)(2,1)S(1)}, u32[]{:S(2)}, u32[]{:S(2)}) collective-permute-start(bf16[144,1024]{1,0:T(8,128)(2,1)} %get-tuple-element.254), channel_id=1, source_target_pairs={{0,6},{1,7},{2,4},{3,5},{4,2},{5,3},{6,0},{7,1},{8,14},{9,15},{10,... | collective-permute-start | bytes 884744 | tf_op jit(solution)/shard_map/ppermute | solution.py:366
  85.0 102.3 %all-gather.12.cloned.1.call-start = ((), (), s32[]{:S(2)}) async-start(), calls=%async_computation.3 | async-start | bytes 4718592 | tf_op jit(solution)/shard_map/all_gather | solution.py:431
  146.5 86.0 %all-gather.14.cloned.1.call-start = ((), (), s32[]{:S(2)}) async-start(), calls=%async_computation.4 | async-start | bytes 4718592 | tf_op jit(solution)/shard_map/all_gather | solution.py:431
  147.9 36.4 %collective-permute-start.22 = (bf16[512,1024]{1,0:T(8,128)(2,1)}, bf16[512,1024]{1,0:T(8,128)(2,1)}, u32[]{:S(2)}, u32[]{:S(2)}) collective-permute-start(bf16[512,1024]{1,0:T(8,128)(2,1)} %dynamic-slice_bitcast_fusion.2), channel_id=1, source_target_pairs={{0,8},{8,0},{16,24},{24,16},{1,9},{9,1},{17,25},{25,17},{2,10},{10... | collective-permute-start | bytes 3145736 | tf_op jit(solution)/shard_map/ppermute | solution.py:366
  151.8 35.5 %collective-permute-start.23 = (bf16[256,1024]{1,0:T(8,128)(2,1)S(1)}, bf16[256,1024]{1,0:T(8,128)(2,1)}, u32[]{:S(2)}, u32[]{:S(2)}) collective-permute-start(bf16[256,1024]{1,0:T(8,128)(2,1)S(1)} %get-tuple-element.453), channel_id=1, source_target_pairs={{0,16},{8,24},{16,0},{24,8},{1,17},{9,25},{17,1},{25,9},{2,18},{10... | collective-permute-start | bytes 1572872 | tf_op jit(solution)/shard_map/ppermute | solution.py:366
  187.3 90.5 %all-gather.16.cloned.1.call-start = ((), (), s32[]{:S(2)}) async-start(), calls=%async_computation.5 | async-start | bytes 4718592 | tf_op jit(solution)/shard_map/all_gather | solution.py:431
  202.2 24.8 %collective-permute-start.29 = (bf16[256,1024]{1,0:T(8,128)(2,1)}, bf16[256,1024]{1,0:T(8,128)(2,1)}, u32[]{:S(2)}, u32[]{:S(2)}) collective-permute-start(bf16[256,1024]{1,0:T(8,128)(2,1)} %get-tuple-element.277), channel_id=1, source_target_pairs={{0,16},{8,24},{16,0},{24,8},{1,17},{9,25},{17,1},{25,9},{2,18},{10... | collective-permute-start | bytes 1572872 | tf_op jit(solution)/shard_map/ppermute | solution.py:366
  237.2 108.3 %all-gather.18.cloned.1.call-start = ((), (), s32[]{:S(2)}) async-start(), calls=%async_computation.6 | async-start | bytes 4718592 | tf_op jit(solution)/shard_map/all_gather | solution.py:431
  239.5 36.6 %collective-permute-start.31 = (bf16[512,1024]{1,0:T(8,128)(2,1)S(1)}, bf16[512,1024]{1,0:T(8,128)(2,1)S(1)}, u32[]{:S(2)}, u32[]{:S(2)}) collective-permute-start(bf16[512,1024]{1,0:T(8,128)(2,1)S(1)} %constant_dynamic-update-slice_fusion.40), channel_id=1, source_target_pairs={{0,8},{8,0},{16,24},{24,16},{1,9},{9,1},{17,25},{25,17},{2,10},{10... | collective-permute-start | bytes 3145736 | tf_op jit(solution)/shard_map/ppermute | solution.py:366
  240.3 37.4 %collective-permute-start.30 = (bf16[128,2048]{1,0:T(8,128)(2,1)S(1)}, bf16[128,2048]{1,0:T(8,128)(2,1)}, u32[]{:S(2)}, u32[]{:S(2)}) collective-permute-start(bf16[128,2048]{1,0:T(8,128)(2,1)S(1)} %copy-done.72), channel_id=1, source_target_pairs={{0,16},{8,24},{16,0},{24,8},{1,17},{9,25},{17,1},{25,9},{2,18},{10... | collective-permute-start | bytes 1572872 | tf_op jit(solution)/shard_map/ppermute | solution.py:366
  277.8 208.4 %all-gather.20.cloned.1.call-start = ((), (), s32[]{:S(2)}) async-start(), calls=%async_computation.7 | async-start | bytes 4718592 | tf_op jit(solution)/shard_map/all_gather | solution.py:431
  278.1 24.5 %collective-permute-start.32 = (bf16[256,2048]{1,0:T(8,128)(2,1)S(1)}, bf16[256,2048]{1,0:T(8,128)(2,1)S(1)}, u32[]{:S(2)}, u32[]{:S(2)}) collective-permute-start(bf16[256,2048]{1,0:T(8,128)(2,1)S(1)} %copy-done.42), channel_id=1, source_target_pairs={{0,8},{8,0},{16,24},{24,16},{1,9},{9,1},{17,25},{25,17},{2,10},{10... | collective-permute-start | bytes 3145736 | tf_op jit(solution)/shard_map/ppermute | solution.py:366
  382.3 32.3 %collective-permute-start.44 = (bf16[1,512,1024]{2,1,0:T(8,128)(2,1)S(1)}, bf16[1,512,1024]{2,1,0:T(8,128)(2,1)S(1)}, u32[]{:S(2)}, u32[]{:S(2)}) collective-permute-start(bf16[1,512,1024]{2,1,0:T(8,128)(2,1)S(1)} %dynamic-slice_bitcast_fusion.1), channel_id=1, source_target_pairs={{0,8},{8,0},{16,24},{24,16},{1,9},{9,1},{17,25},{25,17},{2,10},{10... | collective-permute-start | bytes 3145736 | tf_op jit(solution)/shard_map/ppermute | solution.py:366
  398.4 25.2 %collective-permute-start.43 = (bf16[128,2048]{1,0:T(8,128)(2,1)S(1)}, bf16[128,2048]{1,0:T(8,128)(2,1)S(1)}, u32[]{:S(2)}, u32[]{:S(2)}) collective-permute-start(bf16[128,2048]{1,0:T(8,128)(2,1)S(1)} %pad_maximum_fusion.11), channel_id=1, source_target_pairs={{0,16},{8,24},{16,0},{24,8},{1,17},{9,25},{17,1},{25,9},{2,18},{10... | collective-permute-start | bytes 1572872 | tf_op jit(solution)/shard_map/ppermute | solution.py:366
  429.7 204.3 %reduce-scatter.2.cloned.1.call-start = ((), (), s32[]{:S(2)}) async-start(), calls=%async_computation.8 | async-start | bytes 5242880 | tf_op jit(solution)/shard_map/reduce_scatter | solution.py:739
  444.6 47.5 %collective-permute-start.45 = (bf16[256,1024]{1,0:T(8,128)(2,1)}, bf16[256,1024]{1,0:T(8,128)(2,1)}, u32[]{:S(2)}, u32[]{:S(2)}) collective-permute-start(bf16[256,1024]{1,0:T(8,128)(2,1)} %get-tuple-element.527), channel_id=1, source_target_pairs={{0,16},{8,24},{16,0},{24,8},{1,17},{9,25},{17,1},{25,9},{2,18},{10... | collective-permute-start | bytes 1572872 | tf_op jit(solution)/shard_map/ppermute | solution.py:366
  445.7 36.7 %collective-permute-start.46 = (bf16[1,256,2048]{2,1,0:T(8,128)(2,1)}, bf16[1,256,2048]{2,1,0:T(8,128)(2,1)}, u32[]{:S(2)}, u32[]{:S(2)}) collective-permute-start(bf16[1,256,2048]{2,1,0:T(8,128)(2,1)} %dynamic-slice_bitcast_fusion), channel_id=1, source_target_pairs={{0,8},{8,0},{16,24},{24,16},{1,9},{9,1},{17,25},{25,17},{2,10},{10... | collective-permute-start | bytes 3145736 | tf_op jit(solution)/shard_map/ppermute | solution.py:366
  459.8 25.4 %collective-permute-start.50 = (bf16[64,2048]{1,0:T(8,128)(2,1)S(1)}, bf16[64,2048]{1,0:T(8,128)(2,1)S(1)}, u32[]{:S(2)}, u32[]{:S(2)}) collective-permute-start(bf16[64,2048]{1,0:T(8,128)(2,1)S(1)} %fusion.54), channel_id=1, source_target_pairs={{0,2},{1,3},{2,0},{3,1},{4,6},{5,7},{6,4},{7,5},{8,10},{9,11},{10,... | collective-permute-start | bytes 786440 | tf_op jit(solution)/shard_map/ppermute | solution.py:366
  516.9 35.8 %collective-permute-start.52 = (bf16[1,512,1024]{2,1,0:T(8,128)(2,1)}, bf16[1,512,1024]{2,1,0:T(8,128)(2,1)}, u32[]{:S(2)}, u32[]{:S(2)}) collective-permute-start(bf16[1,512,1024]{2,1,0:T(8,128)(2,1)} %constant_dynamic-slice_fusion.16), channel_id=1, source_target_pairs={{0,8},{8,0},{16,24},{24,16},{1,9},{9,1},{17,25},{25,17},{2,10},{10... | collective-permute-start | bytes 3145736 | tf_op jit(solution)/shard_map/ppermute | solution.py:366
  516.9 37.4 %collective-permute-start.53 = (bf16[256,1024]{1,0:T(8,128)(2,1)}, bf16[256,1024]{1,0:T(8,128)(2,1)}, u32[]{:S(2)}, u32[]{:S(2)}) collective-permute-start(bf16[256,1024]{1,0:T(8,128)(2,1)} %get-tuple-element.333), channel_id=1, source_target_pairs={{0,16},{8,24},{16,0},{24,8},{1,17},{9,25},{17,1},{25,9},{2,18},{10... | collective-permute-start | bytes 1572872 | tf_op jit(solution)/shard_map/ppermute | solution.py:366
  638.9 24.8 %collective-permute-start.74 = (bf16[64,768]{1,0:T(8,128)(2,1)S(1)}, bf16[64,768]{1,0:T(8,128)(2,1)S(1)}, u32[]{:S(2)}, u32[]{:S(2)}) collective-permute-start(bf16[64,768]{1,0:T(8,128)(2,1)S(1)} %get-tuple-element.370), channel_id=1, source_target_pairs={{0,1},{1,0},{2,3},{3,2},{4,5},{5,4},{6,7},{7,6},{8,9},{9,8},{10,11... | collective-permute-start | bytes 294920 | tf_op jit(solution)/shard_map/ppermute | solution.py:366
  639.0 26.8 %collective-permute-start.75 = (bf16[64,768]{1,0:T(8,128)(2,1)S(1)}, bf16[64,768]{1,0:T(8,128)(2,1)S(1)}, u32[]{:S(2)}, u32[]{:S(2)}) collective-permute-start(bf16[64,768]{1,0:T(8,128)(2,1)S(1)} %get-tuple-element.371), channel_id=1, source_target_pairs={{0,2},{1,3},{2,0},{3,1},{4,6},{5,7},{6,4},{7,5},{8,10},{9,11},{10,... | collective-permute-start | bytes 294920 | tf_op jit(solution)/shard_map/ppermute | solution.py:366
  640.5 25.9 %collective-permute-start.76 = (bf16[64,768]{1,0:T(8,128)(2,1)S(1)}, bf16[64,768]{1,0:T(8,128)(2,1)S(1)}, u32[]{:S(2)}, u32[]{:S(2)}) collective-permute-start(bf16[64,768]{1,0:T(8,128)(2,1)S(1)} %get-tuple-element.372), channel_id=1, source_target_pairs={{0,3},{1,2},{2,1},{3,0},{4,7},{5,6},{6,5},{7,4},{8,11},{9,10},{10,... | collective-permute-start | bytes 294920 | tf_op jit(solution)/shard_map/ppermute | solution.py:366
  640.8 26.9 %collective-permute-start.77 = (bf16[64,768]{1,0:T(8,128)(2,1)S(1)}, bf16[64,768]{1,0:T(8,128)(2,1)S(1)}, u32[]{:S(2)}, u32[]{:S(2)}) collective-permute-start(bf16[64,768]{1,0:T(8,128)(2,1)S(1)} %get-tuple-element.373), channel_id=1, source_target_pairs={{0,4},{1,5},{2,6},{3,7},{4,0},{5,1},{6,2},{7,3},{8,12},{9,13},{10,... | collective-permute-start | bytes 294920 | tf_op jit(solution)/shard_map/ppermute | solution.py:366
  666.5 26.5 %collective-permute-start.81 = (bf16[128,2048]{1,0:T(8,128)(2,1)S(1)}, bf16[128,2048]{1,0:T(8,128)(2,1)S(1)}, u32[]{:S(2)}, u32[]{:S(2)}) collective-permute-start(bf16[128,2048]{1,0:T(8,128)(2,1)S(1)} %copy-done.77), channel_id=1, source_target_pairs={{0,16},{8,24},{16,0},{24,8},{1,17},{9,25},{17,1},{25,9},{2,18},{10... | collective-permute-start | bytes 1572872 | tf_op jit(solution)/shard_map/ppermute | solution.py:366
  (184 other events, 1712.7 us)
Sparse Core Ops, SparseCore 0:
  20.8 41.2 all-gather.7
  85.1 61.2 all-gather.9
  148.3 35.3 all-gather.11
  187.4 45.0 all-gather.13
  237.3 35.9 all-gather.15
  277.9 35.9 all-gather.17
  429.8 44.6 all-gather.19
  558.0 76.0 reduce-scatter.1

commit v3 on v2

--- a/solution.py
+++ b/solution.py
@@ -28,6 +28,8 @@
 bf16 = jnp.bfloat16
 f32 = jnp.float32
 
+light = pl.CostEstimate(flops=0, bytes_accessed=0, transcendentals=0)
+
 
 def rms_scale(values):
     return lax.rsqrt(jnp.mean(values * values, axis=-1, keepdims=True) + norm_eps)
@@ -50,6 +52,13 @@
 
 def contract_first(first, second):
     return lax.dot_general(first, second, (((0,), (0,)), ((), ())), preferred_element_type=f32)
+
+
+def thirds(values, axis):
+    size = values.shape[axis] // 16
+    first = -(-size // 3)
+    second = first + (size - first + 1) // 2
+    return jnp.split(values, [16 * first, 16 * second], axis=axis)
 
 
 def adam_step(weight, grad, first, second, rate, decay):
@@ -92,11 +101,52 @@
             jax.ShapeDtypeStruct((rows, columns), bf16),
         ],
         compiler_params=pltpu.CompilerParams(vmem_limit_bytes=40 * 2**20),
-        cost_estimate=pl.CostEstimate(
-            flops=20 * rows * hidden, bytes_accessed=18 * rows * hidden, transcendentals=rows * hidden
-        ),
+        cost_estimate=light,
         name="swiglu",
     )(gate_both, grad_act)
+
+
+def normed_rows(inputs, gain):
+    rows, width = inputs.shape
+    block = 256
+
+    def kernel(inputs_ref, gain_ref, normed_out):
+        values = inputs_ref[...].astype(f32)
+        normed_out[...] = (values * rms_scale(values) * gain_ref[...]).astype(bf16)
+
+    spec = pl.BlockSpec((block, width), lambda step: (step, 0))
+    return pl.pallas_call(
+        kernel,
+        grid=(rows // block,),
+        in_specs=[spec, pl.BlockSpec((1, width), lambda step: (0, 0))],
+        out_specs=spec,
+        out_shape=jax.ShapeDtypeStruct((rows, width), bf16),
+        compiler_params=pltpu.CompilerParams(vmem_limit_bytes=40 * 2**20),
+        cost_estimate=light,
+        name="normed_rows",
+    )(inputs, gain.reshape(1, width))
+
+
+def place_pieces(held, rank, groups, rows):
+    ranks, columns = len(held), held[0].shape[1]
+
+    def kernel(rank_ref, *refs):
+        out_ref = refs[ranks]
+        for group in range(groups):
+            for offset in range(ranks):
+                piece = refs[offset][group * rows : (group + 1) * rows]
+                out_ref[group, rank_ref[0] ^ offset] = piece
+
+    return pl.pallas_call(
+        kernel,
+        in_specs=[pl.BlockSpec(memory_space=pltpu.SMEM)]
+        + [pl.BlockSpec(memory_space=pltpu.VMEM)] * ranks,
+        out_specs=pl.BlockSpec(memory_space=pltpu.VMEM),
+        out_shape=jax.ShapeDtypeStruct((groups, ranks, rows, columns), held[0].dtype),
+        compiler_params=pltpu.CompilerParams(vmem_limit_bytes=40 * 2**20),
+        cost_estimate=light,
+        name="place_pieces",
+    )(rank.reshape(1), *held)
 
 
 def write_step(refs, grad, rate):
@@ -108,6 +158,25 @@
     new_out[...] = fresh
     moment_out[...] = first
     square_out[...] = second
+
+
+def plain_step(grad, weight, first, second, rate):
+    rows, width = weight.shape
+    block = pl.BlockSpec((rows // 4, width), lambda step: (step, 0))
+
+    def kernel(grad_ref, *refs):
+        write_step(refs, grad_ref[...], rate)
+
+    return pl.pallas_call(
+        kernel,
+        grid=(4,),
+        in_specs=[block] * 4,
+        out_specs=[block] * 4,
+        out_shape=[jax.ShapeDtypeStruct(weight.shape, f32)] * 4,
+        compiler_params=pltpu.CompilerParams(vmem_limit_bytes=40 * 2**20),
+        cost_estimate=light,
+        name="plain_step",
+    )(grad, weight, first, second)
 
 
 def gate_step(pieces, weight, first, second, rate, sharers, units):
@@ -142,7 +211,7 @@
         out_shape=[jax.ShapeDtypeStruct(weight.shape, f32)] * 4,
         compiler_params=pltpu.CompilerParams(vmem_limit_bytes=40 * 2**20),
         cost_estimate=pl.CostEstimate(
-            flops=20 * weight.size, bytes_accessed=30 * weight.size, transcendentals=weight.size
+            flops=2**14 * weight.size, bytes_accessed=30 * weight.size, transcendentals=0
         ),
         name="gate_step",
     )(pieces, weight, first, second)
@@ -184,9 +253,7 @@
         out_specs=[block] * 4,
         out_shape=[jax.ShapeDtypeStruct(weight.shape, f32)] * 4,
         compiler_params=pltpu.CompilerParams(vmem_limit_bytes=40 * 2**20),
-        cost_estimate=pl.CostEstimate(
-            flops=20 * weight.size, bytes_accessed=30 * weight.size, transcendentals=weight.size
-        ),
+        cost_estimate=light,
         name="attn_step",
     )(pieces, out_grad, weight, first, second)
 
@@ -330,11 +397,7 @@
         out_specs=[rows, whole[0], whole[0], rows, totals],
         out_shape=[low] * 4 + [jax.ShapeDtypeStruct((2 * pairs, 1, seq_len), f32)],
         compiler_params=pltpu.CompilerParams(vmem_limit_bytes=40 * 2**20),
-        cost_estimate=pl.CostEstimate(
-            flops=pairs * seq_len * seq_len,
-            bytes_accessed=seq_len * pairs * pair_width,
-            transcendentals=0,
-        ),
+        cost_estimate=light,
         name="attention_forward",
     )(projected, projected, projected, cosine, sine, cosine, sine, key_pos, query_pos)
 
@@ -353,11 +416,7 @@
         out_shape=[low] * 3,
         scratch_shapes=[pltpu.VMEM((seq_len, pair_width), f32)] * 2,
         compiler_params=pltpu.CompilerParams(vmem_limit_bytes=40 * 2**20),
-        cost_estimate=pl.CostEstimate(
-            flops=pairs * seq_len * seq_len,
-            bytes_accessed=seq_len * pairs * pair_width,
-            transcendentals=0,
-        ),
+        cost_estimate=light,
         name="attention_backward",
     )(queries, keys, values, grads, totals, cosine, sine, cosine, sine, key_pos, query_pos)
 
@@ -400,22 +459,18 @@
     return bits, bits[::-1]
 
 
-def gather_even(own):
+def gather_step(parts, step, beside=None):
     orders = row_orders()
-    parts = jnp.split(own, 2)
-    for step in range(len(orders[0])):
-        others = lax.optimization_barrier(
-            [swap(part, "ctx", 1 << order[step]) for part, order in zip(parts, orders)]
+    others = [swap(part, "ctx", 1 << order[step]) for part, order in zip(parts, orders)]
+    others, beside = lax.optimization_barrier((others, beside))
+    merged = []
+    for part, other, order in zip(parts, others, orders):
+        low = bit_of("ctx", order[step]) == 0
+        place = sum(bit > order[step] for bit in order[:step])
+        merged.append(
+            jnp.stack([jnp.where(low, part, other), jnp.where(low, other, part)], axis=place)
         )
-        merged = []
-        for part, other, order in zip(parts, others, orders):
-            low = bit_of("ctx", order[step]) == 0
-            place = sum(bit > order[step] for bit in order[:step])
-            merged.append(
-                jnp.stack([jnp.where(low, part, other), jnp.where(low, other, part)], axis=place)
-            )
-        parts = merged
-    return jnp.stack(parts, axis=len(orders[0]))
+    return merged, beside
 
 
 def gather_odd(even):
@@ -431,7 +486,7 @@
     return lax.all_gather(own, "ctx", axis=0, tiled=True)
 
 
-def scatter_rows(rows, weight, product, beside=None):
+def scatter_rows(rows, weight, product, beside=None, ahead=None, then=None):
     ranks = lax.axis_size("ctx")
     own_rows = rows.shape[0] // ranks
     core = bit_of("ctx", 0)
@@ -457,18 +512,19 @@
         if step == 0:
             others, beside = lax.optimization_barrier((others, beside))
         else:
-            others = lax.optimization_barrier(others)
+            others, ahead = lax.optimization_barrier((others, ahead))
+            beside = then(ahead) if then else beside
         parts = [part.astype(f32) + other.astype(f32) for part, other in zip(near, others)]
     sums = jnp.concatenate(parts)
-    return (sums, total) if beside is None else (sums, total, beside)
-
-
-def exchange_held(pieces):
+    return sums, total, beside, ahead
+
+
+def exchange_held(pieces, beside=None):
     pieces = lax.optimization_barrier(pieces)
     held = pieces[:1] + [
         swap(piece, "ctx", offset) for offset, piece in enumerate(pieces) if offset
     ]
-    return lax.optimization_barrier(held)
+    return lax.optimization_barrier((held, beside))
 
 
 def in_order(held, axis):
@@ -476,11 +532,14 @@
     return jnp.stack([pick(held, me ^ rank, 0) for rank in range(held.shape[0])], axis=axis)
 
 
-def exchange(pieces):
+def exchange(pieces, beside=None):
     me = lax.axis_index("ctx")
-    return in_order(
-        exchange_held([pick(pieces, me ^ offset, 0) for offset in range(pieces.shape[0])]), 0
-    )
+    pieces = [pick(pieces, me ^ offset, 0) for offset in range(pieces.shape[0])]
+    shape = pieces[0].shape
+    held, beside = exchange_held(pieces, beside)
+    held = [piece.reshape(-1, shape[-1]) for piece in held]
+    placed = place_pieces(held, me, 1, held[0].shape[0]).reshape((len(held),) + shape)
+    return placed if beside is None else (placed, beside)
 
 
 def body(
@@ -530,7 +589,6 @@
     )
 
     gain_rows = 16
-    inputs_even = gather_even(tokens[0])
     grad_out_theirs = swap(cotangent[0], "dp", 1 << top)
 
     attn_low = attn_weight.astype(bf16)
@@ -540,17 +598,34 @@
         .transpose(3, 0, 1, 2, 4)
         .reshape(ranks, own_rows, 3 * local_width)
     )
-    qkv_own = exchange(qkv_pieces).reshape(ranks * own_rows, 3 * local_width)
-
-    def over_planes(values):
-        for bit in range(top):
+    def cross_planes(values):
+        for bit in range(top - 1):
             values = paired(values, "dp", bit)
-        return values.reshape((sharers,) + values.shape[top:])
+        return values, swap(values, "dp", 1 << (top - 1))
+
+    def join_planes(pair):
+        values, other = pair
+        low = bit_of("dp", top - 1) == 0
+        joined = jnp.stack([jnp.where(low, values, other), jnp.where(low, other, values)])
+        return joined.reshape((sharers,) + values.shape[top - 1 :])
 
     gains_low = norm_gains.astype(bf16)
-    for bit in range(bit_count("dp")):
-        gains_low = paired(gains_low, "dp", bit)
-    gains_own = gains_low.reshape(planes, 2 * own_rows)
+    inputs_even = jnp.split(tokens[0], 2)
+    steps = len(row_orders()[0])
+    plane = lax.axis_index("dp")
+    gains_low = [gains_low] + [swap(gains_low, "dp", offset) for offset in range(1, planes)]
+    inputs_even, gains_low = gather_step(inputs_even, 0, gains_low)
+    for step in range(1, steps - 1):
+        inputs_even = gather_step(inputs_even, step)[0]
+    gains_low = jnp.stack(gains_low)
+    gains_own = jnp.stack([pick(gains_low, plane ^ at, 0) for at in range(planes)])
+    gains_own = gains_own.reshape(planes, 2 * own_rows)
+    qkv_held = exchange_held([pick(qkv_pieces, rank ^ offset, 0) for offset in range(ranks)])[0]
+    inputs_even, qkv_held = gather_step(inputs_even, steps - 1, qkv_held)
+    inputs_even = jnp.stack(inputs_even, axis=steps)
+    qkv_own = place_pieces(qkv_held, rank, 1, own_rows).reshape(
+        ranks * own_rows, 3 * local_width
+    )
     up_from = gate_up.shape[1] // 2
     gate_low = gate_up.astype(bf16)
 
@@ -584,14 +659,14 @@
         out_all = lax.all_gather(out_low, every, axis=0, tiled=True)
         out_proj = pick(out_all.reshape(local_heads, ranks, HEAD, width), rank, 1)
         out_proj = out_proj.reshape(local_width, width)
-    qkv_own, out_proj, gate_pieces = lax.optimization_barrier((qkv_own, out_proj, gate_pieces))
+    qkv_own, out_proj, gate_pieces, inputs_even = lax.optimization_barrier(
+        (qkv_own, out_proj, gate_pieces, inputs_even)
+    )
     qkv = lax.all_gather(qkv_own, "dp", axis=0, tiled=True)
-    gate_pieces, inputs_even, grad_out_theirs = lax.optimization_barrier(
-        (gate_pieces, inputs_even, grad_out_theirs)
-    )
-    gate_held = exchange_held(gate_pieces)
-    gate_own = in_order([held[: 2 * own_rows].reshape(2, own_rows, -1) for held in gate_held], 1)
-    gate_own = gate_own.reshape(2, ranks * own_rows, 2 * hidden)
+    gate_held, grad_out_theirs = exchange_held(gate_pieces, grad_out_theirs)
+    gate_own = place_pieces(gate_held, rank, 2, own_rows).reshape(
+        2, ranks * own_rows, 2 * hidden
+    )
     gains_low = in_order(
         [held[2 * own_rows : 2 * own_rows + planes, : 2 * own_rows] for held in gate_held], 0
     )
@@ -599,9 +674,7 @@
     gains_low = gains_low.reshape(2, width).astype(f32)
     gain_one, gain_two = gains_low[0], gains_low[1]
     inputs_low = gather_odd(inputs_even)
-    inputs_all = inputs_low.astype(f32)
-    normed_all = inputs_all * rms_scale(inputs_all)
-    hidden_one = (normed_all * gain_one).astype(bf16)
+    hidden_one = normed_rows(inputs_low, gain_one)
     qkv, hidden_one, gate_own, gain_two, grad_out_own, grad_out_theirs, down = (
         lax.optimization_barrier(
             (
@@ -616,40 +689,53 @@
         )
     )
 
-    gate_mine = over_planes(pick(gate_own, side, 0))
+    gate_mine = cross_planes(pick(gate_own, side, 0))
     gate_halves = jnp.split(pick(gate_own, 1 - side, 0), 2)
     gate_halves[0] = swap(gate_halves[0], "dp", 1 << top)
     grad_out_near = gather_whole(grad_out_own)
     projected = dot(hidden_one, qkv)
     queries, keys, values, mixed_low, totals = attention_forward(projected, tables)
-    mixed_low, gate_mine, gate_halves, down, grad_out_near, grad_out_theirs = (
+    mixed_low, gate_mine, gate_halves, down_halves, grad_out_near, grad_out_theirs = (
         lax.optimization_barrier(
-            (mixed_low, gate_mine, gate_halves, down, grad_out_near, grad_out_theirs)
+            (
+                mixed_low,
+                gate_mine,
+                gate_halves,
+                jnp.split(down, 2),
+                grad_out_near,
+                grad_out_theirs,
+            )
         )
     )
     grad_out_far = gather_whole(grad_out_theirs)
+    gate_halves[0] = cross_planes(gate_halves[0])
     gate_halves[1] = swap(gate_halves[1], "dp", 1 << top)
 
     inputs = tokens[0].astype(f32)
-    mixed_out, _, (gate_halves, grad_out_far) = scatter_rows(
-        mixed_low, out_proj, dot, (gate_halves, grad_out_far)
-    )
-    gate_theirs = jnp.concatenate(gate_halves)
+    mixed_out, _, (gate_halves, down_halves, grad_out_far), _ = scatter_rows(
+        mixed_low, out_proj, dot, (gate_halves, down_halves, grad_out_far)
+    )
     middle = inputs + mixed_out
     inv_two = rms_scale(middle)
     normed_two = middle * inv_two
     hidden_two_own = (normed_two * gain_two).astype(bf16)
-    hidden_two_near, hidden_two_theirs, gate_theirs, down = lax.optimization_barrier(
+    gate_halves[1] = cross_planes(gate_halves[1])
+    down_halves[0] = cross_planes(down_halves[0])
+    hidden_two_near, hidden_two_theirs, gate_halves, down_halves = lax.optimization_barrier(
         (
             gather_whole(hidden_two_own),
             swap(hidden_two_own, "dp", 1 << top),
-            over_planes(gate_theirs),
-            down,
+            gate_halves,
+            down_halves,
         ),
     )
+    down_halves[1] = cross_planes(down_halves[1])
+    gate_mine = join_planes(gate_mine)
+    gate_theirs = jnp.concatenate([join_planes(pair) for pair in gate_halves], axis=1)
+    down = jnp.concatenate([join_planes(pair) for pair in down_halves], axis=1)
+    down = down.reshape(hidden, width)
     hidden_two_far = gather_whole(hidden_two_theirs)
     grad_outs = [grad_out_near, grad_out_far]
-    down = over_planes(down).reshape(hidden, width)
     gate = jnp.concatenate(
         [
             jnp.where(side == 0, gate_mine, gate_theirs),
@@ -657,15 +743,15 @@
         ]
     ).reshape(width, 2 * hidden)
 
-    def mlp(hidden_two, grad_out):
-        return swiglu(dot(hidden_two, gate), contract_last(grad_out, down))
-
-    activation_near, grad_both_near = mlp(hidden_two_near, grad_outs[0])
-    grad_two, _ = scatter_rows(grad_both_near, gate, contract_last)
-    hidden_two_far, grad_outs[1], grad_two = lax.optimization_barrier(
-        (hidden_two_far, grad_outs[1], grad_two)
-    )
-    activation_far, grad_both_far = mlp(hidden_two_far, grad_outs[1])
+    activation_near, grad_both_near = swiglu(
+        dot(hidden_two_near, gate), contract_last(grad_outs[0], down)
+    )
+    grad_two, _, _, far_inputs = scatter_rows(
+        grad_both_near, gate, contract_last, ahead=(hidden_two_far, grad_outs[1])
+    )
+    hidden_two_far, grad_outs[1] = far_inputs
+    gate_both, grad_two = lax.optimization_barrier((dot(hidden_two_far, gate), grad_two))
+    activation_far, grad_both_far = swiglu(gate_both, contract_last(grad_outs[1], down))
     activations = [activation_near, activation_far]
     hidden_twos = [hidden_two_near, hidden_two_far]
     grad_boths = [grad_both_near, grad_both_far]
@@ -686,21 +772,24 @@
             values = halved(values.astype(bf16), "dp", bit)
         return values[0]
 
-    grad_two_far, started = scatter_rows(grad_both_far, gate, contract_last)
+    grad_two_far, started, _, _ = scatter_rows(grad_both_far, gate, contract_last)
     hidden_twos, grad_boths, activations, started = lax.optimization_barrier(
         (hidden_twos, grad_boths, activations, started)
     )
+    down_term = sum(contract_first(a, g) for a, g in zip(activations, grad_outs)).astype(bf16)
     term_theirs = sum_planes(gate_terms(1 - side)).astype(bf16)
     grad_two += swap(grad_two_far.astype(bf16), "dp", 1 << top).astype(f32)
     term_mine = gate_terms(side)
-    down_term = sum(contract_first(a, g) for a, g in zip(activations, grad_outs)).astype(bf16)
     grad_two, term_mine, term_theirs, down_term, activations = lax.optimization_barrier(
         (grad_two, term_mine, term_theirs, down_term, activations)
     )
-    theirs_halves = jnp.split(term_theirs, 2)
-    theirs_halves[0] = swap(theirs_halves[0], "dp", 1 << top)
-    output_far, _ = scatter_rows(activations[1], down, dot)
-    down_grad = sum_planes(down_term.reshape(sharers, units, width))
+    theirs_parts = thirds(term_theirs, 0)
+    down_parts = thirds(down_term.reshape(sharers, units, width), 1)
+    def cross(parts, at):
+        theirs, downs = list(parts[0]), list(parts[1])
+        theirs[at] = swap(theirs[at], "dp", 1 << top)
+        downs[at] = sum_planes(downs[at])
+        return theirs, downs
 
     reduced_two = grad_two * gain_two
     grad_gain_two = jnp.sum(grad_two * normed_two, axis=0)
@@ -708,21 +797,29 @@
         reduced_two - normed_two * jnp.mean(reduced_two * normed_two, axis=-1, keepdims=True)
     )
     after_low = gather_whole(grad_after.astype(bf16))
+    output_far, _, parts, _ = scatter_rows(
+        activations[1],
+        down,
+        dot,
+        ahead=cross((theirs_parts, down_parts), 0),
+        then=lambda parts: cross(parts, 1),
+    )
     grad_mixed = contract_last(after_low, out_proj).astype(bf16)
     out_term = contract_first(mixed_low, after_low).astype(bf16)
-    grad_mixed, out_term, term_mine, theirs_halves, down_grad, output_far = (
-        lax.optimization_barrier(
-            (grad_mixed, out_term, term_mine, theirs_halves, down_grad, output_far)
-        )
-    )
-    theirs_halves[1] = swap(theirs_halves[1], "dp", 1 << top)
+    if aligned:
+        out_term = out_term.reshape(width, local_width)
+    grad_mixed, out_term, term_mine, parts, output_far = lax.optimization_barrier(
+        (grad_mixed, out_term, term_mine, parts, output_far)
+    )
+    parts = cross(parts, 2)
     term_mine = sum_planes(term_mine).astype(bf16)
-    grad_proj = jnp.concatenate(
-        attention_backward(queries, keys, values, grad_mixed, totals, tables), axis=1
-    )
+    grad_parts = attention_backward(queries, keys, values, grad_mixed, totals, tables)
+    grad_parts, term_mine, parts = lax.optimization_barrier((grad_parts, term_mine, parts))
+    term_theirs = jnp.concatenate(parts[0])
+    down_grad = jnp.concatenate(parts[1])
+    grad_proj = jnp.concatenate(grad_parts, axis=1)
     qkv_term = contract_first(hidden_one, grad_proj).astype(bf16)
     if aligned:
-        out_term = out_term.reshape(width, local_width)
         qkv_term = jnp.concatenate([qkv_term, out_term], axis=1)
     else:
         spread = jnp.zeros((local_heads, ranks, HEAD, width), bf16)
@@ -732,15 +829,16 @@
         out_grad = lax.psum_scatter(
             spread.reshape(HEADS * HEAD, width), every, scatter_dimension=0, tiled=True
         )
-    grad_proj, qkv_term, term_mine, theirs_halves = lax.optimization_barrier(
-        (grad_proj, qkv_term, term_mine, theirs_halves)
-    )
-    term_theirs = jnp.concatenate(theirs_halves)
+    grad_proj, qkv_term, inputs_low, activation_near = lax.optimization_barrier(
+        (grad_proj, qkv_term, inputs_low, activations[0])
+    )
     qkv_term = lax.psum_scatter(qkv_term, "dp", scatter_dimension=0, tiled=True)
     if aligned:
         out_grad = qkv_term[:, 3 * local_width :].reshape(own_rows, width)
         qkv_term = qkv_term[:, : 3 * local_width]
     out_grad = out_grad.astype(f32)
+    inputs_all = inputs_low.astype(f32)
+    normed_all = inputs_all * rms_scale(inputs_all)
     gain_one_parts = []
 
     def gained(part, weight, core):
@@ -749,7 +847,7 @@
         gain_one_parts.append(jnp.sum(product * normed_part.reshape(-1, width), axis=0))
         return product
 
-    grad_one, _ = scatter_rows(grad_proj, qkv, gained)
+    grad_one = scatter_rows(grad_proj, qkv, gained)[0]
     grad_gain_one = sum(gain_one_parts)
     inv_one = rms_scale(inputs)
     normed_one = inputs * inv_one
@@ -758,7 +856,7 @@
         reduced_one - normed_one * jnp.mean(reduced_one * normed_one, axis=-1, keepdims=True)
     )
 
-    output_near, _ = scatter_rows(after(activations[0], grad_proj), down, dot)
+    output_near = scatter_rows(activation_near, down, dot)[0]
     term_cols = jnp.stack(
         [
             jnp.where(side == 0, term_mine, term_theirs),
@@ -771,38 +869,31 @@
     gain_grad = gain_grad.transpose(2, 1, 0, 3)
     for bit in range(bit_count("ctx"))[::-1]:
         gain_grad = halved(gain_grad, "ctx", bit)
-    qkv_term, out_grad, gate_pieces, output_near, output_far, grad_input, gain_grad, down_grad = (
-        lax.optimization_barrier(
-            (
-                qkv_term,
-                out_grad,
-                gate_pieces,
-                output_near,
-                output_far,
-                grad_input,
-                gain_grad,
-                down_grad,
-            )
-        )
-    )
-    qkv_pieces = exchange(qkv_term.reshape(ranks, own_rows, 3 * local_width))
-    output_far = swap(output_far.astype(bf16), "dp", 1 << top)
-    gain_grad = gain_grad[0]
-    for bit in range(bit_count("dp"))[::-1]:
-        gain_grad = halved(gain_grad, "dp", bit)
-    qkv_pieces, output_far, gain_grad = lax.optimization_barrier(
-        (qkv_pieces, output_far, gain_grad)
-    )
+    gate_stepped = gate_step(
+        gate_pieces, gate_up, gate_first, gate_second, 3.0 / math.sqrt(D), sharers, units
+    )
+    down_stepped = plain_step(
+        down_grad, down_weight, down_first, down_second, 3.0 / math.sqrt(FF)
+    )
+    held_back = (gate_stepped, down_stepped, output_near, output_far, grad_input, gain_grad)
+    qkv_term, out_grad, held_back = lax.optimization_barrier((qkv_term, out_grad, held_back))
+    gate_stepped, down_stepped, output_near, output_far, grad_input, gain_grad = held_back
+    gate_grad, gate_new, gate_moment, gate_square = gate_stepped
+    down_grad, down_new, down_moment, down_square = down_stepped
+    output_far = output_far.astype(bf16)
+    gain_parts = [pick(gain_grad[0], plane ^ offset, 0) for offset in range(planes)]
+    qkv_pieces, output_far = exchange(
+        qkv_term.reshape(ranks, own_rows, 3 * local_width), swap(output_far, "dp", 1 << top)
+    )
+    gain_parts, output_far = lax.optimization_barrier((gain_parts, output_far))
     outputs = middle + output_near + output_far.astype(f32)
+    gain_grad = sum(
+        gain_parts[:1]
+        + [swap(part, "dp", offset) for offset, part in enumerate(gain_parts) if offset]
+    )
     gain_grad = gain_grad.reshape(2, -1)
     attn_grad, attn_new, attn_moment, attn_square = attn_step(
         qkv_pieces, out_grad, attn_weight, attn_first, attn_second, 3.0 / math.sqrt(D)
-    )
-    gate_grad, gate_new, gate_moment, gate_square = gate_step(
-        gate_pieces, gate_up, gate_first, gate_second, 3.0 / math.sqrt(D), sharers, units
-    )
-    down_new, down_moment, down_square = adam_step(
-        down_weight, down_grad, down_first, down_second, 3.0 / math.sqrt(FF), decay_rate
     )
     gain_new, gain_moment, gain_square = adam_step(
         norm_gains, gain_grad, gain_first, gain_second, gain_rate, 0.0

time: 716 us -> 660 us (0.922)
  waiting for transfers between devices: 307 us -> 251 us
  Pallas kernels: 53.9 us -> 62.1 us
    ppermute x84 -> x91, waiting for transfers between devices: 279 us -> 236 us  [swap(): lax.ppermute(values, axis, [(i, i ^ bits) for i in range(lax.axis_size(ax...]
    all_gather x1, waiting for transfers between devices: 25.9 us -> 14.5 us  [body(): qkv = lax.all_gather(qkv_own, 'dp', axis=0, tiled=True)]
    pallas_call x0 -> x6, Pallas kernels: none -> 8.56 us  [the longest x1 4.38 us: plain_step(): pl.pallas_call(kernel, grid=(4,), in_specs=[block] * 4, out_specs=[block]...]
    sub x2 -> x1, other arithmetic: 8.43 us -> 0.59 us  [adam_step(): weight - rate * (corrected_first / (jnp.sqrt(corrected_second) + adam_eps...]
    ppermute x84 -> x91, starting transfers between devices: 90.5 us -> 84.2 us  [swap(): lax.ppermute(values, axis, [(i, i ^ bits) for i in range(lax.axis_size(ax...]
    unnamed x316 -> x303, local copies, waits for them, and re-layouts: 31 us -> 33 us
  transfers between devices with their start and end apart: 92 -> 99, of which waited for: 45 -> 51; matrix products, arithmetic and copies ran while one was open for 23% -> 22% of each run, Pallas kernels for 4% -> 9%
where the time goes in v3:
time: 660 us; the launch traced here: 651 us
  waiting for transfers between devices  251 us (38%)
  matrix products  88.1 us (13%)
  starting transfers between devices  85.1 us (13%)
  local copies, waits for them, and re-layouts  79.5 us (12%)
  other arithmetic  67.6 us (10%)
  Pallas kernels  62.1 us (9%)
  between operations  17.6 us (3%)
    ppermute x91, waiting for transfers between devices, swap(): lax.ppermute(values, axis, [(i, i ^ bits) for i in range(lax.axis_size(ax...  236 us
    ppermute x91, starting transfers between devices, swap(): lax.ppermute(values, axis, [(i, i ^ bits) for i in range(lax.axis_size(ax...  84.2 us
    unnamed x303, local copies, waits for them, and re-layouts  33 us
    dot_general x9, matrix products, dot(): return jnp.dot(first, second, preferred_element_type=f32)  32 us
    dot_general x9, matrix products, contract_last(): lax.dot_general(first, second, (((1,), (1,)), ((), ())), preferred_elemen...  30.3 us
    dot_general x8, matrix products, contract_first(): lax.dot_general(first, second, (((0,), (0,)), ((), ())), preferred_elemen...  25.7 us
    pallas_call x1, Pallas kernels, attention_backward(): pl.pallas_call(backward_kernel, grid=(pairs, seq_len // query_block), in_...  18.5 us
    pallas_call x1, Pallas kernels, attention_forward(): pl.pallas_call(forward_kernel, grid=(pairs, seq_len // query_block), in_s...  17.7 us
  transfers between devices with their start and end apart: 99, of which 51 were waited for; matrix products, arithmetic and copies ran while one was open for 22% of the time, Pallas kernels for 9%

profile of v3, /device:TPU:0, one launch (start us, length us, event | category | flops | bytes accessed | tf_op | source)
XLA Modules:
  0.0 651.1 jit_solution(6092765556487222435)
XLA Ops:
  56.0 4.6 collective-permute-done.5
  70.3 4.4 collective-permute-done.16.refs_2_
  81.2 13.2 %collective-permute-done.19.refs_5_ = bf16[144,1024]{1,0:T(8,128)(2,1)} collective-permute-done((bf16[144,1024]{1,0:T(8,128)(2,1)}, bf16[144,1024]{1,0:T(8,128)(2,1)}, u32[]{:S(2)}, u32[]{:S(2)}) %collective-permute-start.19) | collective-permute-done | bytes 294944 | tf_op jit(solution)/shard_map/ppermute | solution.py:425
  111.5 14.5 %all-gather.10.cloned.1.call-done = bf16[2048,768]{1,0:T(8,128)(2,1)} async-done(((bf16[512,768]{1,0:T(8,128)(2,1)}), bf16[2048,768]{1,0:T(8,128)(2,1)}) %all-gather.10.cloned.1.call-update) | async-done | bytes 3145744 | tf_op jit(solution)/shard_map/all_gather | solution.py:665
  131.7 5.5 fusion.91.query_ref.key_ref.value_ref
  137.4 17.7 %attention_forward.1 = (bf16[1024,256]{1,0:T(8,128)(2,1)S(1)}, bf16[1024,256]{1,0:T(8,128)(2,1)S(1)}, bf16[1024,256]{1,0:T(8,128)(2,1)S(1)}, bf16[1024,256]{1,0:T(8,128)(2,1)S(1)}, f32[4,1,1024]{2,1,0:T(1,128)S(1)}) custom-call(f32[1024,768]{1,0:T(8,128)S(1)} %fusion.91.query_ref.key_ref.value_ref, f32[1024,768]{1,0:T(8,128)S(1)} %fusion.91.query_ref.key_ref.value_ref, ...), custom_call_target="tpu_custom_call" | custom-call | tf_op jit(solution)/shard_map/attention_forward/pallas_call | solution.py:393
  158.6 8.8 %collective-permute-done.23 = bf16[512,1024]{1,0:T(8,128)(2,1)} collective-permute-done((bf16[512,1024]{1,0:T(8,128)(2,1)S(1)}, bf16[512,1024]{1,0:T(8,128)(2,1)}, u32[]{:S(2)}, u32[]{:S(2)}) %collective-permute-start.23) | collective-permute-done | bytes 1048608 | tf_op jit(solution)/shard_map/ppermute | solution.py:425
  169.6 4.5 collective-permute-done.25
  184.0 9.8 %collective-permute-done.26 = bf16[2,64,2048]{2,1,0:T(8,128)(2,1)} collective-permute-done((bf16[2,64,2048]{2,1,0:T(8,128)(2,1)}, bf16[2,64,2048]{2,1,0:T(8,128)(2,1)}, u32[]{:S(2)}, u32[]{:S(2)}) %collective-permute-start.26) | collective-permute-done | bytes 524320 | tf_op jit(solution)/shard_map/ppermute | solution.py:425
  223.8 19.3 %collective-permute-done.32 = bf16[128,2048]{1,0:T(8,128)(2,1)} collective-permute-done((bf16[128,2048]{1,0:T(8,128)(2,1)}, bf16[128,2048]{1,0:T(8,128)(2,1)}, u32[]{:S(2)}, u32[]{:S(2)}) %collective-permute-start.32) | collective-permute-done | bytes 524320 | tf_op jit(solution)/shard_map/ppermute | solution.py:425
  244.5 10.2 %collective-permute-done.34 = bf16[128,2048]{1,0:T(8,128)(2,1)} collective-permute-done((bf16[128,2048]{1,0:T(8,128)(2,1)}, bf16[128,2048]{1,0:T(8,128)(2,1)}, u32[]{:S(2)}, u32[]{:S(2)}) %collective-permute-start.34) | collective-permute-done | bytes 524320 | tf_op jit(solution)/shard_map/ppermute | solution.py:425
  263.9 4.5 fusion.92.gate_ref
  290.2 12.1 %collective-permute-done.37 = bf16[2,64,2048]{2,1,0:T(8,128)(2,1)} collective-permute-done((bf16[2,64,2048]{2,1,0:T(8,128)(2,1)S(1)}, bf16[2,64,2048]{2,1,0:T(8,128)(2,1)}, u32[]{:S(2)}, u32[]{:S(2)}) %collective-permute-start.37) | collective-permute-done | bytes 524320 | tf_op jit(solution)/shard_map/ppermute | solution.py:425
  308.4 6.4 fusion.94.gate_ref
  325.1 4.5 collective-permute-done.41
  329.6 5.7 add_convert_fusion.6
  367.2 12.7 %collective-permute-done.47 = bf16[1,512,1024]{2,1,0:T(8,128)(2,1)S(1)} collective-permute-done((bf16[1,512,1024]{2,1,0:T(8,128)(2,1)S(1)}, bf16[1,512,1024]{2,1,0:T(8,128)(2,1)S(1)}, u32[]{:S(2)}, u32[]{:S(2)}) %collective-permute-start.47) | collective-permute-done | bytes 1048608 | tf_op jit(solution)/shard_map/ppermute | solution.py:425
  406.5 13.8 %collective-permute-done.51 = bf16[176,1024]{1,0:T(8,128)(2,1)S(1)} collective-permute-done((bf16[176,1024]{1,0:T(8,128)(2,1)S(1)}, bf16[176,1024]{1,0:T(8,128)(2,1)S(1)}, u32[]{:S(2)}, u32[]{:S(2)}) %collective-permute-start.51) | collective-permute-done | bytes 360480 | tf_op jit(solution)/shard_map/ppermute | solution.py:425
  425.6 7.8 %collective-permute-done.56 = bf16[1,80,2048]{2,1,0:T(8,128)(2,1)S(1)} collective-permute-done((bf16[1,80,2048]{2,1,0:T(8,128)(2,1)S(1)}, bf16[1,80,2048]{2,1,0:T(8,128)(2,1)S(1)}, u32[]{:S(2)}, u32[]{:S(2)}) %collective-permute-start.56) | collective-permute-done | bytes 327712 | tf_op jit(solution)/shard_map/ppermute | solution.py:425
  436.2 5.4 collective-permute-done.55
  442.6 4.4 convolution_convert_fusion.6
  449.5 4.4 convolution_convert_fusion.7.grad_ref
  461.2 18.5 %attention_backward.1 = (bf16[1024,256]{1,0:T(8,128)(2,1)S(1)}, bf16[1024,256]{1,0:T(8,128)(2,1)S(1)}, bf16[1024,256]{1,0:T(8,128)(2,1)S(1)}) custom-call(bf16[1024,256]{1,0:T(8,128)(2,1)S(1)} %copy-done.21, bf16[1024,256]{1,0:T(8,128)(2,1)S(1)} %copy-done.23, bf16[1024,256]{1,0:T(8,128)(2,1)S(1)} %copy-done.25, bf16[1024,256]{1,0:T(8,128)(2,1)S(1)} %copy-done.26, ...), custom_call_target="tpu_custom_call" | custom-call | tf_op jit(solution)/shard_map/attention_backward/pallas_call | solution.py:411
  479.7 13.1 %collective-permute-done.59 = bf16[1,80,2048]{2,1,0:T(8,128)(2,1)} collective-permute-done((bf16[1,80,2048]{2,1,0:T(8,128)(2,1)}, bf16[1,80,2048]{2,1,0:T(8,128)(2,1)}, u32[]{:S(2)}, u32[]{:S(2)}) %collective-permute-start.59) | collective-permute-done | bytes 327712 | tf_op jit(solution)/shard_map/ppermute | solution.py:425
  525.8 7.3 %collective-permute-done.61 = bf16[2,64,1024]{2,1,0:T(8,128)(2,1)S(1)} collective-permute-done((bf16[2,64,1024]{2,1,0:T(8,128)(2,1)}, bf16[2,64,1024]{2,1,0:T(8,128)(2,1)S(1)}, u32[]{:S(2)}, u32[]{:S(2)}) %collective-permute-start.61) | collective-permute-done | bytes 262176 | tf_op jit(solution)/shard_map/ppermute | solution.py:425
  542.0 4.4 plain_step.1
  546.4 4.9 collective-permute-done.64
  568.4 4.6 collective-permute-done.77
  582.1 7.6 %collective-permute-done.73 = bf16[2,64,2048]{2,1,0:T(8,128)(2,1)S(1)} collective-permute-done((bf16[2,64,2048]{2,1,0:T(8,128)(2,1)S(1)}, bf16[2,64,2048]{2,1,0:T(8,128)(2,1)S(1)}, u32[]{:S(2)}, u32[]{:S(2)}) %collective-permute-start.73) | collective-permute-done | bytes 524320 | tf_op jit(solution)/shard_map/ppermute | solution.py:425
  593.6 10.1 %gate_step.1 = (f32[64,16384]{1,0:T(8,128)}, f32[64,16384]{1,0:T(8,128)}, f32[64,16384]{1,0:T(8,128)}, f32[64,16384]{1,0:T(8,128)}) custom-call(bf16[8,2,64,1024]{3,2,1,0:T(8,128)(2,1)S(1)} %bitcast.487, f32[64,16384]{1,0:T(8,128)S(1)} %copy-done.8, f32[64,16384]{1,0:T(8,128)S(1)} %copy-done.33, f32[64,16384]{1,0:T(8,128)} %refs_2_.3), custom_call_target="tpu_custom_call" | custom-call | flops 17179869184 | bytes 31457280 | tf_op jit(solution)/shard_map/gate_step/pallas_call | solution.py:200
  625.9 6.2 collective-permute-done.87
  638.6 4.8 attn_step.1
  (700 shorter events, 358.0 us)
Async XLA Ops:
  7.2 57.3 %all-gather.8.cloned.1.call-start = ((), (), s32[]{:S(2)}) async-start(), calls=%async_computation.1 | async-start | bytes 1310720 | tf_op jit(solution)/shard_map/all_gather | solution.py:657
  9.1 35.9 %collective-permute-start.1 = (bf16[64,2048]{1,0:T(8,128)(2,1)}, bf16[64,2048]{1,0:T(8,128)(2,1)}, u32[]{:S(2)}, u32[]{:S(2)}) collective-permute-start(bf16[64,2048]{1,0:T(8,128)(2,1)} %get-tuple-element.665), channel_id=1, source_target_pairs={{0,4},{1,5},{2,6},{3,7},{4,0},{5,1},{6,2},{7,3},{8,12},{9,13},{10,... | collective-permute-start | bytes 786440 | tf_op jit(solution)/shard_map/ppermute | solution.py:425
  12.1 32.9 %collective-permute-start = (bf16[64,2048]{1,0:T(8,128)(2,1)}, bf16[64,2048]{1,0:T(8,128)(2,1)}, u32[]{:S(2)}, u32[]{:S(2)}) collective-permute-start(bf16[64,2048]{1,0:T(8,128)(2,1)} %get-tuple-element.666), channel_id=1, source_target_pairs={{0,2},{1,3},{2,0},{3,1},{4,6},{5,7},{6,4},{7,5},{8,10},{9,11},{10,... | collective-permute-start | bytes 786440 | tf_op jit(solution)/shard_map/ppermute | solution.py:425
  16.0 109.9 %all-gather.10.cloned.1.call-start = ((), (), s32[]{:S(2)}) async-start(), calls=%async_computation.2 | async-start | bytes 3932160 | tf_op jit(solution)/shard_map/all_gather | solution.py:665
  42.3 26.7 %collective-permute-start.22 = (bf16[128,2048]{1,0:T(8,128)(2,1)}, bf16[128,2048]{1,0:T(8,128)(2,1)}, u32[]{:S(2)}, u32[]{:S(2)}) collective-permute-start(bf16[128,2048]{1,0:T(8,128)(2,1)} %bitcast.507), channel_id=1, source_target_pairs={{0,16},{8,24},{16,0},{24,8},{1,17},{9,25},{17,1},{25,9},{2,18},{10... | collective-permute-start | bytes 1572872 | tf_op jit(solution)/shard_map/ppermute | solution.py:425
  64.5 102.9 %all-gather.12.cloned.1.call-start = ((), (), s32[]{:S(2)}) async-start(), calls=%async_computation.3 | async-start | bytes 4718592 | tf_op jit(solution)/shard_map/all_gather | solution.py:486
  69.0 25.4 %collective-permute-start.19 = (bf16[144,1024]{1,0:T(8,128)(2,1)}, bf16[144,1024]{1,0:T(8,128)(2,1)}, u32[]{:S(2)}, u32[]{:S(2)}) collective-permute-start(bf16[144,1024]{1,0:T(8,128)(2,1)} %get-tuple-element.308), channel_id=1, source_target_pairs={{0,5},{1,4},{2,7},{3,6},{4,1},{5,0},{6,3},{7,2},{8,13},{9,12},{10,... | collective-permute-start | bytes 884744 | tf_op jit(solution)/shard_map/ppermute | solution.py:425
  69.0 25.4 %collective-permute-start.20 = (bf16[144,1024]{1,0:T(8,128)(2,1)}, bf16[144,1024]{1,0:T(8,128)(2,1)}, u32[]{:S(2)}, u32[]{:S(2)}) collective-permute-start(bf16[144,1024]{1,0:T(8,128)(2,1)} %get-tuple-element.309), channel_id=1, source_target_pairs={{0,6},{1,7},{2,4},{3,5},{4,2},{5,3},{6,0},{7,1},{8,14},{9,15},{10,... | collective-permute-start | bytes 884744 | tf_op jit(solution)/shard_map/ppermute | solution.py:425
  80.1 22.4 %collective-permute-start.14 = (bf16[2,2,2,64,2048]{4,3,0,1,2:T(8,128)(2,1)}, bf16[2,2,2,64,2048]{4,3,0,1,2:T(8,128)(2,1)}, u32[]{:S(2)}, u32[]{:S(2)}) collective-permute-start(bf16[2,2,2,64,2048]{4,3,0,1,2:T(8,128)(2,1)} %pad_maximum_fusion.3), channel_id=1, source_target_pairs={{0,1},{1,0},{2,3},{3,2},{4,5},{5,4},{6,7},{7,6},{8,9},{9,8},{10,11... | collective-permute-start | bytes 6291464 | tf_op jit(solution)/shard_map/ppermute | solution.py:425
  126.0 85.7 %all-gather.14.cloned.1.call-start = ((), (), s32[]{:S(2)}) async-start(), calls=%async_computation.4 | async-start | bytes 4718592 | tf_op jit(solution)/shard_map/all_gather | solution.py:486
  130.2 28.4 %collective-permute-start.24 = (bf16[256,1024]{1,0:T(8,128)(2,1)S(1)}, bf16[256,1024]{1,0:T(8,128)(2,1)}, u32[]{:S(2)}, u32[]{:S(2)}) collective-permute-start(bf16[256,1024]{1,0:T(8,128)(2,1)S(1)} %get-tuple-element.553), channel_id=1, source_target_pairs={{0,16},{8,24},{16,0},{24,8},{1,17},{9,25},{17,1},{25,9},{2,18},{10... | collective-permute-start | bytes 1572872 | tf_op jit(solution)/shard_map/ppermute | solution.py:425
  131.4 36.0 %collective-permute-start.23 = (bf16[512,1024]{1,0:T(8,128)(2,1)S(1)}, bf16[512,1024]{1,0:T(8,128)(2,1)}, u32[]{:S(2)}, u32[]{:S(2)}) collective-permute-start(bf16[512,1024]{1,0:T(8,128)(2,1)S(1)} %dynamic-slice_bitcast_fusion.1), channel_id=1, source_target_pairs={{0,8},{8,0},{16,24},{24,16},{1,9},{9,1},{17,25},{25,17},{2,10},{10... | collective-permute-start | bytes 3145736 | tf_op jit(solution)/shard_map/ppermute | solution.py:425
  167.4 87.3 %all-gather.16.cloned.1.call-start = ((), (), s32[]{:S(2)}) async-start(), calls=%async_computation.5 | async-start | bytes 4718592 | tf_op jit(solution)/shard_map/all_gather | solution.py:486
  182.4 25.5 %collective-permute-start.31 = (bf16[256,1024]{1,0:T(8,128)(2,1)}, bf16[256,1024]{1,0:T(8,128)(2,1)}, u32[]{:S(2)}, u32[]{:S(2)}) collective-permute-start(bf16[256,1024]{1,0:T(8,128)(2,1)} %get-tuple-element.332), channel_id=1, source_target_pairs={{0,16},{8,24},{16,0},{24,8},{1,17},{9,25},{17,1},{25,9},{2,18},{10... | collective-permute-start | bytes 1572872 | tf_op jit(solution)/shard_map/ppermute | solution.py:425
  182.4 25.5 %collective-permute-start.30 = (bf16[256,1024]{1,0:T(8,128)(2,1)}, bf16[256,1024]{1,0:T(8,128)(2,1)}, u32[]{:S(2)}, u32[]{:S(2)}) collective-permute-start(bf16[256,1024]{1,0:T(8,128)(2,1)} %collective-permute-done.24), channel_id=1, source_target_pairs={{0,8},{8,0},{16,24},{24,16},{1,9},{9,1},{17,25},{25,17},{2,10},{10... | collective-permute-start | bytes 1572872 | tf_op jit(solution)/shard_map/ppermute | solution.py:425
  216.8 86.9 %all-gather.18.cloned.1.call-start = ((), (), s32[]{:S(2)}) async-start(), calls=%async_computation.6 | async-start | bytes 4718592 | tf_op jit(solution)/shard_map/all_gather | solution.py:486
  216.9 26.2 %collective-permute-start.32 = (bf16[128,2048]{1,0:T(8,128)(2,1)}, bf16[128,2048]{1,0:T(8,128)(2,1)}, u32[]{:S(2)}, u32[]{:S(2)}) collective-permute-start(bf16[128,2048]{1,0:T(8,128)(2,1)} %multiply_convert_fusion), channel_id=1, source_target_pairs={{0,16},{8,24},{16,0},{24,8},{1,17},{9,25},{17,1},{25,9},{2,18},{10... | collective-permute-start | bytes 1572872 | tf_op jit(solution)/shard_map/ppermute | solution.py:425
  218.8 25.7 %collective-permute-start.33 = (bf16[256,1024]{1,0:T(8,128)(2,1)}, bf16[256,1024]{1,0:T(8,128)(2,1)}, u32[]{:S(2)}, u32[]{:S(2)}) collective-permute-start(bf16[256,1024]{1,0:T(8,128)(2,1)} %collective-permute-done.31), channel_id=1, source_target_pairs={{0,8},{8,0},{16,24},{24,16},{1,9},{9,1},{17,25},{25,17},{2,10},{10... | collective-permute-start | bytes 1572872 | tf_op jit(solution)/shard_map/ppermute | solution.py:425
  220.2 34.5 %collective-permute-start.34 = (bf16[128,2048]{1,0:T(8,128)(2,1)}, bf16[128,2048]{1,0:T(8,128)(2,1)}, u32[]{:S(2)}, u32[]{:S(2)}) collective-permute-start(bf16[128,2048]{1,0:T(8,128)(2,1)} %get-tuple-element.355), channel_id=1, source_target_pairs={{0,8},{8,0},{16,24},{24,16},{1,9},{9,1},{17,25},{25,17},{2,10},{10... | collective-permute-start | bytes 1572872 | tf_op jit(solution)/shard_map/ppermute | solution.py:425
  254.7 187.9 %all-gather.20.cloned.1.call-start = ((), (), s32[]{:S(2)}) async-start(), calls=%async_computation.7 | async-start | bytes 4718592 | tf_op jit(solution)/shard_map/all_gather | solution.py:486
  345.6 34.3 %collective-permute-start.47 = (bf16[1,512,1024]{2,1,0:T(8,128)(2,1)S(1)}, bf16[1,512,1024]{2,1,0:T(8,128)(2,1)S(1)}, u32[]{:S(2)}, u32[]{:S(2)}) collective-permute-start(bf16[1,512,1024]{2,1,0:T(8,128)(2,1)S(1)} %dynamic-slice_bitcast_fusion), channel_id=1, source_target_pairs={{0,8},{8,0},{16,24},{24,16},{1,9},{9,1},{17,25},{25,17},{2,10},{10... | collective-permute-start | bytes 3145736 | tf_op jit(solution)/shard_map/ppermute | solution.py:425
  361.7 23.9 %collective-permute-start.46 = (bf16[128,2048]{1,0:T(8,128)(2,1)S(1)}, bf16[128,2048]{1,0:T(8,128)(2,1)S(1)}, u32[]{:S(2)}, u32[]{:S(2)}) collective-permute-start(bf16[128,2048]{1,0:T(8,128)(2,1)S(1)} %pad_maximum_fusion.11), channel_id=1, source_target_pairs={{0,16},{8,24},{16,0},{24,8},{1,17},{9,25},{17,1},{25,9},{2,18},{10... | collective-permute-start | bytes 1572872 | tf_op jit(solution)/shard_map/ppermute | solution.py:425
  391.6 216.5 %reduce-scatter.2.cloned.1.call-start = ((), (), s32[]{:S(2)}) async-start(), calls=%async_computation.8 | async-start | bytes 5242880 | tf_op jit(solution)/shard_map/reduce_scatter | solution.py:835
  398.7 21.6 %collective-permute-start.49 = (bf16[2,64,2048]{2,1,0:T(8,128)(2,1)S(1)}, bf16[2,64,2048]{2,1,0:T(8,128)(2,1)S(1)}, u32[]{:S(2)}, u32[]{:S(2)}) collective-permute-start(bf16[2,64,2048]{2,1,0:T(8,128)(2,1)S(1)} %dynamic-slice_bitcast_fusion.9), channel_id=1, source_target_pairs={{0,4},{1,5},{2,6},{3,7},{4,0},{5,1},{6,2},{7,3},{8,12},{9,13},{10,... | collective-permute-start | bytes 1572872 | tf_op jit(solution)/shard_map/ppermute | solution.py:425
  455.0 39.8 %collective-permute-start.57 = (bf16[1,512,1024]{2,1,0:T(8,128)(2,1)}, bf16[1,512,1024]{2,1,0:T(8,128)(2,1)}, u32[]{:S(2)}, u32[]{:S(2)}) collective-permute-start(bf16[1,512,1024]{2,1,0:T(8,128)(2,1)} %constant_dynamic-slice_fusion.17), channel_id=1, source_target_pairs={{0,8},{8,0},{16,24},{24,16},{1,9},{9,1},{17,25},{25,17},{2,10},{10... | collective-permute-start | bytes 3145736 | tf_op jit(solution)/shard_map/ppermute | solution.py:425
  455.7 37.1 %collective-permute-start.59 = (bf16[1,80,2048]{2,1,0:T(8,128)(2,1)}, bf16[1,80,2048]{2,1,0:T(8,128)(2,1)}, u32[]{:S(2)}, u32[]{:S(2)}) collective-permute-start(bf16[1,80,2048]{2,1,0:T(8,128)(2,1)} %constant_dynamic-slice_fusion.16), channel_id=1, source_target_pairs={{0,8},{8,0},{16,24},{24,16},{1,9},{9,1},{17,25},{25,17},{2,10},{10... | collective-permute-start | bytes 983048 | tf_op jit(solution)/shard_map/ppermute | solution.py:425
  457.8 38.7 %collective-permute-start.58 = (bf16[160,1024]{1,0:T(8,128)(2,1)}, bf16[160,1024]{1,0:T(8,128)(2,1)}, u32[]{:S(2)}, u32[]{:S(2)}) collective-permute-start(bf16[160,1024]{1,0:T(8,128)(2,1)} %split.56), channel_id=1, source_target_pairs={{0,16},{8,24},{16,0},{24,8},{1,17},{9,25},{17,1},{25,9},{2,18},{10... | collective-permute-start | bytes 983048 | tf_op jit(solution)/shard_map/ppermute | solution.py:425
  514.8 38.1 %collective-permute-start.67 = (bf16[512,2048]{1,0:T(8,128)(2,1)}, bf16[512,2048]{1,0:T(8,128)(2,1)}, u32[]{:S(2)}, u32[]{:S(2)}) collective-permute-start(bf16[512,2048]{1,0:T(8,128)(2,1)} %convolution_convert_fusion.4), channel_id=1, source_target_pairs={{0,1},{1,0},{2,3},{3,2},{4,5},{5,4},{6,7},{7,6},{8,9},{9,8},{10,11... | collective-permute-start | bytes 6291464 | tf_op jit(solution)/shard_map/ppermute | solution.py:425
  523.2 37.3 %collective-permute-start.72 = (bf16[512,2048]{1,0:T(8,128)(2,1)}, bf16[512,2048]{1,0:T(8,128)(2,1)}, u32[]{:S(2)}, u32[]{:S(2)}) collective-permute-start(bf16[512,2048]{1,0:T(8,128)(2,1)} %get-tuple-element.517), channel_id=1, source_target_pairs={{0,1},{1,0},{2,3},{3,2},{4,5},{5,4},{6,7},{7,6},{8,9},{9,8},{10,11... | collective-permute-start | bytes 6291464 | tf_op jit(solution)/shard_map/ppermute | solution.py:425
  577.3 26.4 %collective-permute-start.79 = (f32[1,4,2,64]{3,2,1,0:T(2,128)S(1)}, f32[1,4,2,64]{3,2,1,0:T(2,128)S(1)}, u32[]{:S(2)}, u32[]{:S(2)}) collective-permute-start(f32[1,4,2,64]{3,2,1,0:T(2,128)S(1)} %constant_dynamic-slice_fusion.4), channel_id=1, source_target_pairs={{0,1},{1,0},{2,3},{3,2},{4,5},{5,4},{6,7},{7,6},{8,9},{9,8},{10,11... | collective-permute-start | bytes 6152 | tf_op jit(solution)/shard_map/ppermute | solution.py:425
  578.8 24.9 %collective-permute-start.70 = (bf16[64,2048]{1,0:T(8,128)(2,1)S(1)}, bf16[64,2048]{1,0:T(8,128)(2,1)S(1)}, u32[]{:S(2)}, u32[]{:S(2)}) collective-permute-start(bf16[64,2048]{1,0:T(8,128)(2,1)S(1)} %fusion.53), channel_id=1, source_target_pairs={{0,2},{1,3},{2,0},{3,1},{4,6},{5,7},{6,4},{7,5},{8,10},{9,11},{10,... | collective-permute-start | bytes 786440 | tf_op jit(solution)/shard_map/ppermute | solution.py:425
  580.3 23.4 %collective-permute-start.71 = (bf16[64,2048]{1,0:T(8,128)(2,1)S(1)}, bf16[64,2048]{1,0:T(8,128)(2,1)S(1)}, u32[]{:S(2)}, u32[]{:S(2)}) collective-permute-start(bf16[64,2048]{1,0:T(8,128)(2,1)S(1)} %fusion.54), channel_id=1, source_target_pairs={{0,4},{1,5},{2,6},{3,7},{4,0},{5,1},{6,2},{7,3},{8,12},{9,13},{10,... | collective-permute-start | bytes 786440 | tf_op jit(solution)/shard_map/ppermute | solution.py:425
  (209 other events, 1576.5 us)
Sparse Core Ops, SparseCore 0:
  16.1 27.3 all-gather.7
  64.6 61.2 all-gather.9
  127.8 35.3 all-gather.11
  167.6 43.5 all-gather.13
  217.0 36.4 all-gather.15
  255.2 36.7 all-gather.17
  391.7 46.2 all-gather.19
  525.9 75.1 reduce-scatter.1

commit v4 on v3

--- a/solution.py
+++ b/solution.py
@@ -42,11 +42,11 @@
     return jnp.tile(jnp.cos(phase), (1, 4)), jnp.tile(jnp.sin(phase), (1, 4))
 
 
-def dot(first, second, core=None):
+def dot(first, second):
     return jnp.dot(first, second, preferred_element_type=f32)
 
 
-def contract_last(first, second, core=None):
+def contract_last(first, second):
     return lax.dot_general(first, second, (((1,), (1,)), ((), ())), preferred_element_type=f32)
 
 
@@ -110,17 +110,22 @@
     rows, width = inputs.shape
     block = 256
 
-    def kernel(inputs_ref, gain_ref, normed_out):
+    def kernel(inputs_ref, gain_ref, normed_out, scale_out):
         values = inputs_ref[...].astype(f32)
-        normed_out[...] = (values * rms_scale(values) * gain_ref[...]).astype(bf16)
+        scale = rms_scale(values)
+        normed_out[...] = (values * scale * gain_ref[...]).astype(bf16)
+        scale_out[...] = jnp.broadcast_to(scale, scale_out.shape)
 
     spec = pl.BlockSpec((block, width), lambda step: (step, 0))
     return pl.pallas_call(
         kernel,
         grid=(rows // block,),
         in_specs=[spec, pl.BlockSpec((1, width), lambda step: (0, 0))],
-        out_specs=spec,
-        out_shape=jax.ShapeDtypeStruct((rows, width), bf16),
+        out_specs=[spec, pl.BlockSpec((block, 128), lambda step: (step, 0))],
+        out_shape=[
+            jax.ShapeDtypeStruct((rows, width), bf16),
+            jax.ShapeDtypeStruct((rows, 128), f32),
+        ],
         compiler_params=pltpu.CompilerParams(vmem_limit_bytes=40 * 2**20),
         cost_estimate=light,
         name="normed_rows",
@@ -147,6 +152,65 @@
         cost_estimate=light,
         name="place_pieces",
     )(rank.reshape(1), *held)
+
+
+def core_product(rows, weight, core, other, transposed, normed=None):
+    groups, _, own_rows, depth = rows.shape
+    width = weight.shape[0] if transposed else weight.shape[1]
+    count, block = groups * own_rows, 512
+
+    def kernel(core_ref, rows_ref, weight_ref, *refs):
+        refs = list(refs)
+        part = rows_ref[...].reshape(count, depth)
+        contract = ((1,), (1,)) if transposed else ((1,), (0,))
+        product = lax.dot_general(
+            part, weight_ref[...], (contract, ((), ())), preferred_element_type=f32
+        )
+        if normed is not None:
+            inputs_ref, scale_ref, gain_out = refs.pop(0), refs.pop(0), refs.pop()
+            values = inputs_ref[...].reshape(count, block).astype(f32)
+            scale = scale_ref[...].reshape(count, 128)[:, :1]
+            gain_out[...] = jnp.sum(product * (values * scale), axis=0, keepdims=True)
+        if other is not None:
+            product += refs.pop(0)[...].astype(f32)
+        refs[0][...] = product.astype(bf16)
+
+    def of_core(columns, moving):
+        return pl.BlockSpec(
+            (groups, 1, own_rows, columns),
+            lambda step, core_ref: (0, core_ref[0], 0, step if moving else 0),
+        )
+
+    operands = [rows, weight]
+    in_specs = [
+        of_core(depth, False),
+        pl.BlockSpec((block, depth), lambda step, core_ref: (step, 0))
+        if transposed
+        else pl.BlockSpec((depth, block), lambda step, core_ref: (0, step)),
+    ]
+    column = pl.BlockSpec((count, block), lambda step, core_ref: (0, step))
+    out_specs, out_shape = [column], [jax.ShapeDtypeStruct((count, width), bf16)]
+    if normed is not None:
+        operands += [values.reshape(groups, 2, own_rows, -1) for values in normed]
+        in_specs += [of_core(block, True), of_core(128, False)]
+        out_specs.append(pl.BlockSpec((1, block), lambda step, core_ref: (0, step)))
+        out_shape.append(jax.ShapeDtypeStruct((1, width), f32))
+    if other is not None:
+        operands.append(other)
+        in_specs.append(column)
+    return pl.pallas_call(
+        kernel,
+        grid_spec=pltpu.PrefetchScalarGridSpec(
+            num_scalar_prefetch=1,
+            grid=(width // block,),
+            in_specs=in_specs,
+            out_specs=out_specs,
+        ),
+        out_shape=out_shape,
+        compiler_params=pltpu.CompilerParams(vmem_limit_bytes=40 * 2**20),
+        cost_estimate=light,
+        name="core_product",
+    )(core.reshape(1), *operands)
 
 
 def write_step(refs, grad, rate):
@@ -211,7 +275,7 @@
         out_shape=[jax.ShapeDtypeStruct(weight.shape, f32)] * 4,
         compiler_params=pltpu.CompilerParams(vmem_limit_bytes=40 * 2**20),
         cost_estimate=pl.CostEstimate(
-            flops=2**14 * weight.size, bytes_accessed=30 * weight.size, transcendentals=0
+            flops=2**12 * weight.size, bytes_accessed=weight.size, transcendentals=0
         ),
         name="gate_step",
     )(pieces, weight, first, second)
@@ -486,17 +550,22 @@
     return lax.all_gather(own, "ctx", axis=0, tiled=True)
 
 
+def plainly(multiply):
+    def product(rows, weight, core, other):
+        result = multiply(pick(rows, core, 1).reshape(-1, rows.shape[-1]), weight)
+        return (result if other is None else result + other.astype(f32)).astype(bf16)
+
+    return product
+
+
 def scatter_rows(rows, weight, product, beside=None, ahead=None, then=None):
     ranks = lax.axis_size("ctx")
     own_rows = rows.shape[0] // ranks
     core = bit_of("ctx", 0)
     rows = rows.reshape(ranks // 2, 2, own_rows, rows.shape[1])
 
-    def of_core(which):
-        return pick(rows, which, 1).reshape(-1, rows.shape[-1])
-
-    other = swap(product(of_core(1 - core), weight, 1 - core).astype(bf16), "ctx", 1)
-    total = (product(of_core(core), weight, core) + other.astype(f32)).astype(bf16)
+    other = swap(product(rows, weight, 1 - core, None), "ctx", 1)
+    total = product(rows, weight, core, other)
     orders = row_orders()
     count = len(orders[0])
     halves = total.reshape((2,) * count + (2, own_rows // 2, total.shape[-1]))
@@ -674,7 +743,7 @@
     gains_low = gains_low.reshape(2, width).astype(f32)
     gain_one, gain_two = gains_low[0], gains_low[1]
     inputs_low = gather_odd(inputs_even)
-    hidden_one = normed_rows(inputs_low, gain_one)
+    hidden_one, scale_one = normed_rows(inputs_low, gain_one)
     qkv, hidden_one, gate_own, gain_two, grad_out_own, grad_out_theirs, down = (
         lax.optimization_barrier(
             (
@@ -713,7 +782,7 @@
 
     inputs = tokens[0].astype(f32)
     mixed_out, _, (gate_halves, down_halves, grad_out_far), _ = scatter_rows(
-        mixed_low, out_proj, dot, (gate_halves, down_halves, grad_out_far)
+        mixed_low, out_proj, plainly(dot), (gate_halves, down_halves, grad_out_far)
     )
     middle = inputs + mixed_out
     inv_two = rms_scale(middle)
@@ -747,7 +816,7 @@
         dot(hidden_two_near, gate), contract_last(grad_outs[0], down)
     )
     grad_two, _, _, far_inputs = scatter_rows(
-        grad_both_near, gate, contract_last, ahead=(hidden_two_far, grad_outs[1])
+        grad_both_near, gate, plainly(contract_last), ahead=(hidden_two_far, grad_outs[1])
     )
     hidden_two_far, grad_outs[1] = far_inputs
     gate_both, grad_two = lax.optimization_barrier((dot(hidden_two_far, gate), grad_two))
@@ -772,7 +841,7 @@
             values = halved(values.astype(bf16), "dp", bit)
         return values[0]
 
-    grad_two_far, started, _, _ = scatter_rows(grad_both_far, gate, contract_last)
+    grad_two_far, started, _, _ = scatter_rows(grad_both_far, gate, plainly(contract_last))
     hidden_twos, grad_boths, activations, started = lax.optimization_barrier(
         (hidden_twos, grad_boths, activations, started)
     )
@@ -800,16 +869,13 @@
     output_far, _, parts, _ = scatter_rows(
         activations[1],
         down,
-        dot,
+        plainly(dot),
         ahead=cross((theirs_parts, down_parts), 0),
         then=lambda parts: cross(parts, 1),
     )
     grad_mixed = contract_last(after_low, out_proj).astype(bf16)
-    out_term = contract_first(mixed_low, after_low).astype(bf16)
-    if aligned:
-        out_term = out_term.reshape(width, local_width)
-    grad_mixed, out_term, term_mine, parts, output_far = lax.optimization_barrier(
-        (grad_mixed, out_term, term_mine, parts, output_far)
+    grad_mixed, mixed_low, after_low, term_mine, parts, output_far = lax.optimization_barrier(
+        (grad_mixed, mixed_low, after_low, term_mine, parts, output_far)
     )
     parts = cross(parts, 2)
     term_mine = sum_planes(term_mine).astype(bf16)
@@ -819,7 +885,9 @@
     down_grad = jnp.concatenate(parts[1])
     grad_proj = jnp.concatenate(grad_parts, axis=1)
     qkv_term = contract_first(hidden_one, grad_proj).astype(bf16)
+    out_term = contract_first(mixed_low, after_low).astype(bf16)
     if aligned:
+        out_term = out_term.reshape(width, local_width)
         qkv_term = jnp.concatenate([qkv_term, out_term], axis=1)
     else:
         spread = jnp.zeros((local_heads, ranks, HEAD, width), bf16)
@@ -837,14 +905,11 @@
         out_grad = qkv_term[:, 3 * local_width :].reshape(own_rows, width)
         qkv_term = qkv_term[:, : 3 * local_width]
     out_grad = out_grad.astype(f32)
-    inputs_all = inputs_low.astype(f32)
-    normed_all = inputs_all * rms_scale(inputs_all)
     gain_one_parts = []
 
-    def gained(part, weight, core):
-        product = contract_last(part, weight)
-        normed_part = pick(normed_all.reshape(ranks // 2, 2, rows, width), core, 1)
-        gain_one_parts.append(jnp.sum(product * normed_part.reshape(-1, width), axis=0))
+    def gained(*operands):
+        product, gain = core_product(*operands, True, (inputs_low, scale_one))
+        gain_one_parts.append(gain.reshape(width))
         return product
 
     grad_one = scatter_rows(grad_proj, qkv, gained)[0]
@@ -856,7 +921,9 @@
         reduced_one - normed_one * jnp.mean(reduced_one * normed_one, axis=-1, keepdims=True)
     )
 
-    output_near = scatter_rows(activation_near, down, dot)[0]
+    output_near = scatter_rows(
+        activation_near, down, lambda *operands: core_product(*operands, False)[0]
+    )[0]
     term_cols = jnp.stack(
         [
             jnp.where(side == 0, term_mine, term_theirs),

time: 660 us -> 654 us (level)
  Pallas kernels: 62.1 us -> 78.4 us
  matrix products: 88.1 us -> 74 us
  waiting for transfers between devices: 251 us -> 244 us
  other arithmetic: 67.6 us -> 60.8 us
    pallas_call x0 -> x4, Pallas kernels: none -> 15.1 us  [core_product(): pl.pallas_call(kernel, grid_spec=pltpu.PrefetchScalarGridSpec(num_scalar_...]
    unnamed x303 -> x308, local copies, waits for them, and re-layouts: 33 us -> 45.7 us
    ppermute x91, waiting for transfers between devices: 236 us -> 229 us  [swap(): lax.ppermute(values, axis, [(i, i ^ bits) for i in range(lax.axis_size(ax...]
    dot_general x9 -> x7, matrix products: 30.3 us -> 23.6 us  [contract_last(): lax.dot_general(first, second, (((1,), (1,)), ((), ())), preferred_elemen...]
    dot_general x9 -> x7, matrix products: 32 us -> 26.3 us  [dot(): return jnp.dot(first, second, preferred_element_type=f32)]
  transfers between devices with their start and end apart: 99 -> 99, of which waited for: 51 -> 50; matrix products, arithmetic and copies ran while one was open for 22% -> 21% of each run, Pallas kernels for 9% -> 11%
where the time goes in v4:
time: 654 us; the launch traced here: 644 us
  waiting for transfers between devices  244 us (37%)
  starting transfers between devices  85.3 us (13%)
  local copies, waits for them, and re-layouts  84.2 us (13%)
  Pallas kernels  78.4 us (12%)
  matrix products  74 us (11%)
  other arithmetic  60.8 us (9%)
  between operations  17.5 us (3%)
    ppermute x91, waiting for transfers between devices, swap(): lax.ppermute(values, axis, [(i, i ^ bits) for i in range(lax.axis_size(ax...  229 us
    ppermute x91, starting transfers between devices, swap(): lax.ppermute(values, axis, [(i, i ^ bits) for i in range(lax.axis_size(ax...  84.8 us
    unnamed x308, local copies, waits for them, and re-layouts  45.7 us
    dot_general x7, matrix products, dot(): return jnp.dot(first, second, preferred_element_type=f32)  26.3 us
    dot_general x8, matrix products, contract_first(): lax.dot_general(first, second, (((0,), (0,)), ((), ())), preferred_elemen...  24.1 us
    dot_general x7, matrix products, contract_last(): lax.dot_general(first, second, (((1,), (1,)), ((), ())), preferred_elemen...  23.6 us
    pallas_call x1, Pallas kernels, attention_backward(): pl.pallas_call(backward_kernel, grid=(pairs, seq_len // query_block), in_...  18.4 us
    pallas_call x1, Pallas kernels, attention_forward(): pl.pallas_call(forward_kernel, grid=(pairs, seq_len // query_block), in_s...  17.7 us
  transfers between devices with their start and end apart: 99, of which 50 were waited for; matrix products, arithmetic and copies ran while one was open for 21% of the time, Pallas kernels for 11%

profile of v4, /device:TPU:0, one launch (start us, length us, event | category | flops | bytes accessed | tf_op | source)
XLA Modules:
  0.0 644.3 jit_solution(7794089989151030911)
XLA Ops:
  56.0 4.6 collective-permute-done.5
  70.2 4.5 collective-permute-done.16.refs_2_
  81.3 13.2 %collective-permute-done.19.refs_5_ = bf16[144,1024]{1,0:T(8,128)(2,1)} collective-permute-done((bf16[144,1024]{1,0:T(8,128)(2,1)}, bf16[144,1024]{1,0:T(8,128)(2,1)}, u32[]{:S(2)}, u32[]{:S(2)}) %collective-permute-start.19) | collective-permute-done | bytes 294944 | tf_op jit(solution)/shard_map/ppermute | solution.py:489
  112.3 13.6 %all-gather.10.cloned.1.call-done.weight_ref = bf16[2048,768]{1,0:T(8,128)(2,1)} async-done(((bf16[512,768]{1,0:T(8,128)(2,1)}), bf16[2048,768]{1,0:T(8,128)(2,1)}) %all-gather.10.cloned.1.call-update) | async-done | bytes 3145744 | tf_op jit(solution)/shard_map/all_gather | solution.py:734
  131.7 5.5 fusion.90.query_ref.key_ref.value_ref
  137.4 17.7 %attention_forward.1 = (bf16[1024,256]{1,0:T(8,128)(2,1)S(1)}, bf16[1024,256]{1,0:T(8,128)(2,1)S(1)}, bf16[1024,256]{1,0:T(8,128)(2,1)S(1)}, bf16[1024,256]{1,0:T(8,128)(2,1)S(1)}, f32[4,1,1024]{2,1,0:T(1,128)S(1)}) custom-call(f32[1024,768]{1,0:T(8,128)S(1)} %fusion.90.query_ref.key_ref.value_ref, f32[1024,768]{1,0:T(8,128)S(1)} %fusion.90.query_ref.key_ref.value_ref, ...), custom_call_target="tpu_custom_call" | custom-call | tf_op jit(solution)/shard_map/attention_forward/pallas_call | solution.py:457
  157.3 10.1 %collective-permute-done.23 = bf16[512,1024]{1,0:T(8,128)(2,1)} collective-permute-done((bf16[512,1024]{1,0:T(8,128)(2,1)S(1)}, bf16[512,1024]{1,0:T(8,128)(2,1)}, u32[]{:S(2)}, u32[]{:S(2)}) %collective-permute-start.23) | collective-permute-done | bytes 1048608 | tf_op jit(solution)/shard_map/ppermute | solution.py:489
  169.6 4.5 collective-permute-done.25
  183.0 10.8 %collective-permute-done.26 = bf16[2,64,2048]{2,1,0:T(8,128)(2,1)} collective-permute-done((bf16[2,64,2048]{2,1,0:T(8,128)(2,1)}, bf16[2,64,2048]{2,1,0:T(8,128)(2,1)}, u32[]{:S(2)}, u32[]{:S(2)}) %collective-permute-start.26) | collective-permute-done | bytes 524320 | tf_op jit(solution)/shard_map/ppermute | solution.py:489
  199.6 7.2 %collective-permute-done.31 = bf16[256,1024]{1,0:T(8,128)(2,1)} collective-permute-done((bf16[256,1024]{1,0:T(8,128)(2,1)}, bf16[256,1024]{1,0:T(8,128)(2,1)}, u32[]{:S(2)}, u32[]{:S(2)}) %collective-permute-start.31) | collective-permute-done | bytes 524320 | tf_op jit(solution)/shard_map/ppermute | solution.py:489
  206.8 4.6 collective-permute-done.28
  223.8 19.5 %collective-permute-done.32 = bf16[128,2048]{1,0:T(8,128)(2,1)} collective-permute-done((bf16[128,2048]{1,0:T(8,128)(2,1)}, bf16[128,2048]{1,0:T(8,128)(2,1)}, u32[]{:S(2)}, u32[]{:S(2)}) %collective-permute-start.32) | collective-permute-done | bytes 524320 | tf_op jit(solution)/shard_map/ppermute | solution.py:489
  244.4 10.2 %collective-permute-done.34 = bf16[128,2048]{1,0:T(8,128)(2,1)} collective-permute-done((bf16[128,2048]{1,0:T(8,128)(2,1)}, bf16[128,2048]{1,0:T(8,128)(2,1)}, u32[]{:S(2)}, u32[]{:S(2)}) %collective-permute-start.34) | collective-permute-done | bytes 524320 | tf_op jit(solution)/shard_map/ppermute | solution.py:489
  264.3 4.5 fusion.91.gate_ref
  290.3 12.2 %collective-permute-done.37 = bf16[2,64,2048]{2,1,0:T(8,128)(2,1)} collective-permute-done((bf16[2,64,2048]{2,1,0:T(8,128)(2,1)S(1)}, bf16[2,64,2048]{2,1,0:T(8,128)(2,1)}, u32[]{:S(2)}, u32[]{:S(2)}) %collective-permute-start.37) | collective-permute-done | bytes 524320 | tf_op jit(solution)/shard_map/ppermute | solution.py:489
  308.8 6.3 fusion.93.gate_ref
  325.8 4.5 collective-permute-done.41
  330.3 5.7 add_convert_fusion.4
  367.5 13.6 %collective-permute-done.47 = bf16[1,512,1024]{2,1,0:T(8,128)(2,1)S(1)} collective-permute-done((bf16[1,512,1024]{2,1,0:T(8,128)(2,1)S(1)}, bf16[1,512,1024]{2,1,0:T(8,128)(2,1)S(1)}, u32[]{:S(2)}, u32[]{:S(2)}) %collective-permute-start.47) | collective-permute-done | bytes 1048608 | tf_op jit(solution)/shard_map/ppermute | solution.py:489
  405.9 13.4 %collective-permute-done.51 = bf16[176,1024]{1,0:T(8,128)(2,1)S(1)} collective-permute-done((bf16[176,1024]{1,0:T(8,128)(2,1)S(1)}, bf16[176,1024]{1,0:T(8,128)(2,1)S(1)}, u32[]{:S(2)}, u32[]{:S(2)}) %collective-permute-start.51) | collective-permute-done | bytes 360480 | tf_op jit(solution)/shard_map/ppermute | solution.py:489
  423.9 8.4 %collective-permute-done.56 = bf16[1,80,2048]{2,1,0:T(8,128)(2,1)S(1)} collective-permute-done((bf16[1,80,2048]{2,1,0:T(8,128)(2,1)S(1)}, bf16[1,80,2048]{2,1,0:T(8,128)(2,1)S(1)}, u32[]{:S(2)}, u32[]{:S(2)}) %collective-permute-start.56) | collective-permute-done | bytes 327712 | tf_op jit(solution)/shard_map/ppermute | solution.py:489
  434.6 4.9 collective-permute-done.55
  441.2 4.7 convolution_convert_fusion.6.grad_ref
  462.2 18.4 %attention_backward.1 = (bf16[1024,256]{1,0:T(8,128)(2,1)S(1)}, bf16[1024,256]{1,0:T(8,128)(2,1)S(1)}, bf16[1024,256]{1,0:T(8,128)(2,1)S(1)}) custom-call(bf16[1024,256]{1,0:T(8,128)(2,1)S(1)} %copy-done.37, bf16[1024,256]{1,0:T(8,128)(2,1)S(1)} %copy-done.39, bf16[1024,256]{1,0:T(8,128)(2,1)S(1)} %copy-done.41, bf16[1024,256]{1,0:T(8,128)(2,1)S(1)} %copy-done.42, ...), custom_call_target="tpu_custom_call" | custom-call | tf_op jit(solution)/shard_map/attention_backward/pallas_call | solution.py:475
  515.9 6.2 collective-permute-done.61
  532.8 4.5 plain_step.1
  537.3 4.6 collective-permute-done.66
  564.9 6.3 collective-permute-done.78
  574.2 6.7 %collective-permute-done.68 = bf16[2,64,2048]{2,1,0:T(8,128)(2,1)S(1)} collective-permute-done((bf16[2,64,2048]{2,1,0:T(8,128)(2,1)S(1)}, bf16[2,64,2048]{2,1,0:T(8,128)(2,1)S(1)}, u32[]{:S(2)}, u32[]{:S(2)}) %collective-permute-start.68) | collective-permute-done | bytes 524320 | tf_op jit(solution)/shard_map/ppermute | solution.py:489
  585.3 9.9 %gate_step.1 = (f32[64,16384]{1,0:T(8,128)}, f32[64,16384]{1,0:T(8,128)}, f32[64,16384]{1,0:T(8,128)}, f32[64,16384]{1,0:T(8,128)}) custom-call(bf16[8,2,64,1024]{3,2,1,0:T(8,128)(2,1)S(1)} %bitcast.481, f32[64,16384]{1,0:T(8,128)S(1)} %copy-done.19, f32[64,16384]{1,0:T(8,128)S(1)} %copy-done.51, f32[64,16384]{1,0:T(8,128)} %refs_2_.3), custom_call_target="tpu_custom_call" | custom-call | flops 4294967296 | bytes 1048576 | tf_op jit(solution)/shard_map/gate_step/pallas_call | solution.py:264
  617.5 7.8 %collective-permute-done.87 = bf16[128,2048]{1,0:T(8,128)(2,1)} collective-permute-done((bf16[128,2048]{1,0:T(8,128)(2,1)}, bf16[128,2048]{1,0:T(8,128)(2,1)}, u32[]{:S(2)}, u32[]{:S(2)}) %collective-permute-start.87) | collective-permute-done | bytes 524320 | tf_op jit(solution)/shard_map/ppermute | solution.py:489
  631.8 4.8 attn_step.1
  (700 shorter events, 353.6 us)
Async XLA Ops:
  7.2 57.3 %all-gather.8.cloned.1.call-start = ((), (), s32[]{:S(2)}) async-start(), calls=%async_computation.1 | async-start | bytes 1310720 | tf_op jit(solution)/shard_map/all_gather | solution.py:726
  9.1 35.9 %collective-permute-start.1 = (bf16[64,2048]{1,0:T(8,128)(2,1)}, bf16[64,2048]{1,0:T(8,128)(2,1)}, u32[]{:S(2)}, u32[]{:S(2)}) collective-permute-start(bf16[64,2048]{1,0:T(8,128)(2,1)} %get-tuple-element.669), channel_id=1, source_target_pairs={{0,4},{1,5},{2,6},{3,7},{4,0},{5,1},{6,2},{7,3},{8,12},{9,13},{10,... | collective-permute-start | bytes 786440 | tf_op jit(solution)/shard_map/ppermute | solution.py:489
  12.1 32.9 %collective-permute-start = (bf16[64,2048]{1,0:T(8,128)(2,1)}, bf16[64,2048]{1,0:T(8,128)(2,1)}, u32[]{:S(2)}, u32[]{:S(2)}) collective-permute-start(bf16[64,2048]{1,0:T(8,128)(2,1)} %get-tuple-element.670), channel_id=1, source_target_pairs={{0,2},{1,3},{2,0},{3,1},{4,6},{5,7},{6,4},{7,5},{8,10},{9,11},{10,... | collective-permute-start | bytes 786440 | tf_op jit(solution)/shard_map/ppermute | solution.py:489
  16.0 109.9 %all-gather.10.cloned.1.call-start = ((), (), s32[]{:S(2)}) async-start(), calls=%async_computation.2 | async-start | bytes 3932160 | tf_op jit(solution)/shard_map/all_gather | solution.py:734
  42.3 26.7 %collective-permute-start.22 = (bf16[128,2048]{1,0:T(8,128)(2,1)}, bf16[128,2048]{1,0:T(8,128)(2,1)}, u32[]{:S(2)}, u32[]{:S(2)}) collective-permute-start(bf16[128,2048]{1,0:T(8,128)(2,1)} %bitcast.497), channel_id=1, source_target_pairs={{0,16},{8,24},{16,0},{24,8},{1,17},{9,25},{17,1},{25,9},{2,18},{10... | collective-permute-start | bytes 1572872 | tf_op jit(solution)/shard_map/ppermute | solution.py:489
  64.5 102.9 %all-gather.12.cloned.1.call-start = ((), (), s32[]{:S(2)}) async-start(), calls=%async_computation.3 | async-start | bytes 4718592 | tf_op jit(solution)/shard_map/all_gather | solution.py:550
  69.0 25.4 %collective-permute-start.19 = (bf16[144,1024]{1,0:T(8,128)(2,1)}, bf16[144,1024]{1,0:T(8,128)(2,1)}, u32[]{:S(2)}, u32[]{:S(2)}) collective-permute-start(bf16[144,1024]{1,0:T(8,128)(2,1)} %get-tuple-element.315), channel_id=1, source_target_pairs={{0,5},{1,4},{2,7},{3,6},{4,1},{5,0},{6,3},{7,2},{8,13},{9,12},{10,... | collective-permute-start | bytes 884744 | tf_op jit(solution)/shard_map/ppermute | solution.py:489
  69.0 25.4 %collective-permute-start.20 = (bf16[144,1024]{1,0:T(8,128)(2,1)}, bf16[144,1024]{1,0:T(8,128)(2,1)}, u32[]{:S(2)}, u32[]{:S(2)}) collective-permute-start(bf16[144,1024]{1,0:T(8,128)(2,1)} %get-tuple-element.316), channel_id=1, source_target_pairs={{0,6},{1,7},{2,4},{3,5},{4,2},{5,3},{6,0},{7,1},{8,14},{9,15},{10,... | collective-permute-start | bytes 884744 | tf_op jit(solution)/shard_map/ppermute | solution.py:489
  80.1 22.4 %collective-permute-start.14 = (bf16[2,2,2,64,2048]{4,3,0,1,2:T(8,128)(2,1)}, bf16[2,2,2,64,2048]{4,3,0,1,2:T(8,128)(2,1)}, u32[]{:S(2)}, u32[]{:S(2)}) collective-permute-start(bf16[2,2,2,64,2048]{4,3,0,1,2:T(8,128)(2,1)} %pad_maximum_fusion.3), channel_id=1, source_target_pairs={{0,1},{1,0},{2,3},{3,2},{4,5},{5,4},{6,7},{7,6},{8,9},{9,8},{10,11... | collective-permute-start | bytes 6291464 | tf_op jit(solution)/shard_map/ppermute | solution.py:489
  126.0 86.9 %all-gather.14.cloned.1.call-start = ((), (), s32[]{:S(2)}) async-start(), calls=%async_computation.4 | async-start | bytes 4718592 | tf_op jit(solution)/shard_map/all_gather | solution.py:550
  130.2 26.0 %collective-permute-start.24 = (bf16[256,1024]{1,0:T(8,128)(2,1)S(1)}, bf16[256,1024]{1,0:T(8,128)(2,1)S(1)}, u32[]{:S(2)}, u32[]{:S(2)}) collective-permute-start(bf16[256,1024]{1,0:T(8,128)(2,1)S(1)} %get-tuple-element.561), channel_id=1, source_target_pairs={{0,16},{8,24},{16,0},{24,8},{1,17},{9,25},{17,1},{25,9},{2,18},{10... | collective-permute-start | bytes 1572872 | tf_op jit(solution)/shard_map/ppermute | solution.py:489
  131.4 36.0 %collective-permute-start.23 = (bf16[512,1024]{1,0:T(8,128)(2,1)S(1)}, bf16[512,1024]{1,0:T(8,128)(2,1)}, u32[]{:S(2)}, u32[]{:S(2)}) collective-permute-start(bf16[512,1024]{1,0:T(8,128)(2,1)S(1)} %dynamic-slice_bitcast_fusion.1), channel_id=1, source_target_pairs={{0,8},{8,0},{16,24},{24,16},{1,9},{9,1},{17,25},{25,17},{2,10},{10... | collective-permute-start | bytes 3145736 | tf_op jit(solution)/shard_map/ppermute | solution.py:489
  167.4 87.2 %all-gather.16.cloned.1.call-start = ((), (), s32[]{:S(2)}) async-start(), calls=%async_computation.5 | async-start | bytes 4718592 | tf_op jit(solution)/shard_map/all_gather | solution.py:550
  181.4 25.5 %collective-permute-start.31 = (bf16[256,1024]{1,0:T(8,128)(2,1)}, bf16[256,1024]{1,0:T(8,128)(2,1)}, u32[]{:S(2)}, u32[]{:S(2)}) collective-permute-start(bf16[256,1024]{1,0:T(8,128)(2,1)} %get-tuple-element.340), channel_id=1, source_target_pairs={{0,16},{8,24},{16,0},{24,8},{1,17},{9,25},{17,1},{25,9},{2,18},{10... | collective-permute-start | bytes 1572872 | tf_op jit(solution)/shard_map/ppermute | solution.py:489
  181.4 25.5 %collective-permute-start.30 = (bf16[256,1024]{1,0:T(8,128)(2,1)}, bf16[256,1024]{1,0:T(8,128)(2,1)}, u32[]{:S(2)}, u32[]{:S(2)}) collective-permute-start(bf16[256,1024]{1,0:T(8,128)(2,1)} %copy-done.88), channel_id=1, source_target_pairs={{0,8},{8,0},{16,24},{24,16},{1,9},{9,1},{17,25},{25,17},{2,10},{10... | collective-permute-start | bytes 1572872 | tf_op jit(solution)/shard_map/ppermute | solution.py:489
  216.5 87.0 %all-gather.18.cloned.1.call-start = ((), (), s32[]{:S(2)}) async-start(), calls=%async_computation.6 | async-start | bytes 4718592 | tf_op jit(solution)/shard_map/all_gather | solution.py:550
  216.6 26.7 %collective-permute-start.32 = (bf16[128,2048]{1,0:T(8,128)(2,1)}, bf16[128,2048]{1,0:T(8,128)(2,1)}, u32[]{:S(2)}, u32[]{:S(2)}) collective-permute-start(bf16[128,2048]{1,0:T(8,128)(2,1)} %multiply_convert_fusion), channel_id=1, source_target_pairs={{0,16},{8,24},{16,0},{24,8},{1,17},{9,25},{17,1},{25,9},{2,18},{10... | collective-permute-start | bytes 1572872 | tf_op jit(solution)/shard_map/ppermute | solution.py:489
  219.1 25.3 %collective-permute-start.33 = (bf16[256,1024]{1,0:T(8,128)(2,1)}, bf16[256,1024]{1,0:T(8,128)(2,1)}, u32[]{:S(2)}, u32[]{:S(2)}) collective-permute-start(bf16[256,1024]{1,0:T(8,128)(2,1)} %collective-permute-done.31), channel_id=1, source_target_pairs={{0,8},{8,0},{16,24},{24,16},{1,9},{9,1},{17,25},{25,17},{2,10},{10... | collective-permute-start | bytes 1572872 | tf_op jit(solution)/shard_map/ppermute | solution.py:489
  220.6 34.0 %collective-permute-start.34 = (bf16[128,2048]{1,0:T(8,128)(2,1)}, bf16[128,2048]{1,0:T(8,128)(2,1)}, u32[]{:S(2)}, u32[]{:S(2)}) collective-permute-start(bf16[128,2048]{1,0:T(8,128)(2,1)} %get-tuple-element.363), channel_id=1, source_target_pairs={{0,8},{8,0},{16,24},{24,16},{1,9},{9,1},{17,25},{25,17},{2,10},{10... | collective-permute-start | bytes 1572872 | tf_op jit(solution)/shard_map/ppermute | solution.py:489
  254.6 186.5 %all-gather.20.cloned.1.call-start = ((), (), s32[]{:S(2)}) async-start(), calls=%async_computation.7 | async-start | bytes 4718592 | tf_op jit(solution)/shard_map/all_gather | solution.py:550
  346.5 34.7 %collective-permute-start.47 = (bf16[1,512,1024]{2,1,0:T(8,128)(2,1)S(1)}, bf16[1,512,1024]{2,1,0:T(8,128)(2,1)S(1)}, u32[]{:S(2)}, u32[]{:S(2)}) collective-permute-start(bf16[1,512,1024]{2,1,0:T(8,128)(2,1)S(1)} %dynamic-slice_bitcast_fusion), channel_id=1, source_target_pairs={{0,8},{8,0},{16,24},{24,16},{1,9},{9,1},{17,25},{25,17},{2,10},{10... | collective-permute-start | bytes 3145736 | tf_op jit(solution)/shard_map/ppermute | solution.py:489
  361.9 23.9 %collective-permute-start.46 = (bf16[128,2048]{1,0:T(8,128)(2,1)S(1)}, bf16[128,2048]{1,0:T(8,128)(2,1)S(1)}, u32[]{:S(2)}, u32[]{:S(2)}) collective-permute-start(bf16[128,2048]{1,0:T(8,128)(2,1)S(1)} %pad_maximum_fusion.11), channel_id=1, source_target_pairs={{0,16},{8,24},{16,0},{24,8},{1,17},{9,25},{17,1},{25,9},{2,18},{10... | collective-permute-start | bytes 1572872 | tf_op jit(solution)/shard_map/ppermute | solution.py:489
  391.1 208.5 %reduce-scatter.2.cloned.1.call-start = ((), (), s32[]{:S(2)}) async-start(), calls=%async_computation.8 | async-start | bytes 5242880 | tf_op jit(solution)/shard_map/reduce_scatter | solution.py:903
  446.9 39.1 %collective-permute-start.57 = (bf16[1,512,1024]{2,1,0:T(8,128)(2,1)}, bf16[1,512,1024]{2,1,0:T(8,128)(2,1)}, u32[]{:S(2)}, u32[]{:S(2)}) collective-permute-start(bf16[1,512,1024]{2,1,0:T(8,128)(2,1)} %constant_dynamic-slice_fusion.11), channel_id=1, source_target_pairs={{0,8},{8,0},{16,24},{24,16},{1,9},{9,1},{17,25},{25,17},{2,10},{10... | collective-permute-start | bytes 3145736 | tf_op jit(solution)/shard_map/ppermute | solution.py:489
  448.0 36.2 %collective-permute-start.59 = (bf16[1,80,2048]{2,1,0:T(8,128)(2,1)}, bf16[1,80,2048]{2,1,0:T(8,128)(2,1)}, u32[]{:S(2)}, u32[]{:S(2)}) collective-permute-start(bf16[1,80,2048]{2,1,0:T(8,128)(2,1)} %constant_dynamic-slice_fusion.10), channel_id=1, source_target_pairs={{0,8},{8,0},{16,24},{24,16},{1,9},{9,1},{17,25},{25,17},{2,10},{10... | collective-permute-start | bytes 983048 | tf_op jit(solution)/shard_map/ppermute | solution.py:489
  449.7 39.1 %collective-permute-start.58 = (bf16[160,1024]{1,0:T(8,128)(2,1)}, bf16[160,1024]{1,0:T(8,128)(2,1)}, u32[]{:S(2)}, u32[]{:S(2)}) collective-permute-start(bf16[160,1024]{1,0:T(8,128)(2,1)} %split.56), channel_id=1, source_target_pairs={{0,16},{8,24},{16,0},{24,8},{1,17},{9,25},{17,1},{25,9},{2,18},{10... | collective-permute-start | bytes 983048 | tf_op jit(solution)/shard_map/ppermute | solution.py:489
  505.4 39.3 %collective-permute-start.72 = (bf16[512,2048]{1,0:T(8,128)(2,1)}, bf16[512,2048]{1,0:T(8,128)(2,1)}, u32[]{:S(2)}, u32[]{:S(2)}) collective-permute-start(bf16[512,2048]{1,0:T(8,128)(2,1)} %get-tuple-element.470), channel_id=1, source_target_pairs={{0,1},{1,0},{2,3},{3,2},{4,5},{5,4},{6,7},{7,6},{8,9},{9,8},{10,11... | collective-permute-start | bytes 6291464 | tf_op jit(solution)/shard_map/ppermute | solution.py:489
  512.4 44.8 %collective-permute-start.67 = (bf16[512,2048]{1,0:T(8,128)(2,1)}, bf16[512,2048]{1,0:T(8,128)(2,1)}, u32[]{:S(2)}, u32[]{:S(2)}) collective-permute-start(bf16[512,2048]{1,0:T(8,128)(2,1)} %core_product.4), channel_id=1, source_target_pairs={{0,1},{1,0},{2,3},{3,2},{4,5},{5,4},{6,7},{7,6},{8,9},{9,8},{10,11... | collective-permute-start | bytes 6291464 | tf_op jit(solution)/shard_map/ppermute | solution.py:489
  571.2 24.0 %collective-permute-start.79 = (f32[1,4,2,64]{3,2,1,0:T(2,128)S(1)}, f32[1,4,2,64]{3,2,1,0:T(2,128)S(1)}, u32[]{:S(2)}, u32[]{:S(2)}) collective-permute-start(f32[1,4,2,64]{3,2,1,0:T(2,128)S(1)} %constant_dynamic-slice_fusion.4), channel_id=1, source_target_pairs={{0,1},{1,0},{2,3},{3,2},{4,5},{5,4},{6,7},{7,6},{8,9},{9,8},{10,11... | collective-permute-start | bytes 6152 | tf_op jit(solution)/shard_map/ppermute | solution.py:489
  571.5 23.7 %collective-permute-start.75 = (bf16[64,2048]{1,0:T(8,128)(2,1)S(1)}, bf16[64,2048]{1,0:T(8,128)(2,1)S(1)}, u32[]{:S(2)}, u32[]{:S(2)}) collective-permute-start(bf16[64,2048]{1,0:T(8,128)(2,1)S(1)} %fusion.52), channel_id=1, source_target_pairs={{0,2},{1,3},{2,0},{3,1},{4,6},{5,7},{6,4},{7,5},{8,10},{9,11},{10,... | collective-permute-start | bytes 786440 | tf_op jit(solution)/shard_map/ppermute | solution.py:489
  572.8 22.4 %collective-permute-start.76 = (bf16[64,2048]{1,0:T(8,128)(2,1)S(1)}, bf16[64,2048]{1,0:T(8,128)(2,1)S(1)}, u32[]{:S(2)}, u32[]{:S(2)}) collective-permute-start(bf16[64,2048]{1,0:T(8,128)(2,1)S(1)} %fusion.53), channel_id=1, source_target_pairs={{0,4},{1,5},{2,6},{3,7},{4,0},{5,1},{6,2},{7,3},{8,12},{9,13},{10,... | collective-permute-start | bytes 786440 | tf_op jit(solution)/shard_map/ppermute | solution.py:489
  603.0 22.3 %collective-permute-start.87 = (bf16[128,2048]{1,0:T(8,128)(2,1)}, bf16[128,2048]{1,0:T(8,128)(2,1)}, u32[]{:S(2)}, u32[]{:S(2)}) collective-permute-start(bf16[128,2048]{1,0:T(8,128)(2,1)} %pad_maximum_fusion.7), channel_id=1, source_target_pairs={{0,16},{8,24},{16,0},{24,8},{1,17},{9,25},{17,1},{25,9},{2,18},{10... | collective-permute-start | bytes 1572872 | tf_op jit(solution)/shard_map/ppermute | solution.py:489
  (212 other events, 1566.6 us)
Sparse Core Ops, SparseCore 0:
  16.1 27.3 all-gather.7
  64.6 61.2 all-gather.9
  127.8 35.3 all-gather.11
  167.5 45.2 all-gather.13
  216.7 36.8 all-gather.15
  255.3 36.7 all-gather.17
  391.2 46.2 all-gather.19
  516.0 76.3 reduce-scatter.1

commit v5 on v4

--- a/solution.py
+++ b/solution.py
@@ -744,12 +744,16 @@
     gain_one, gain_two = gains_low[0], gains_low[1]
     inputs_low = gather_odd(inputs_even)
     hidden_one, scale_one = normed_rows(inputs_low, gain_one)
-    qkv, hidden_one, gate_own, gain_two, grad_out_own, grad_out_theirs, down = (
+    gate_mine = pick(gate_own, side, 0)
+    gate_halves = jnp.split(pick(gate_own, 1 - side, 0), 2)
+    hidden_one, tables, scale_one = lax.optimization_barrier((hidden_one, tables, scale_one))
+    qkv, hidden_one, gate_mine, gate_halves, gain_two, grad_out_own, grad_out_theirs, down = (
         lax.optimization_barrier(
             (
                 qkv,
                 hidden_one,
-                gate_own,
+                gate_mine,
+                gate_halves,
                 gain_two,
                 cotangent[0],
                 grad_out_theirs,
@@ -757,9 +761,7 @@
             )
         )
     )
-
-    gate_mine = cross_planes(pick(gate_own, side, 0))
-    gate_halves = jnp.split(pick(gate_own, 1 - side, 0), 2)
+    gate_mine = cross_planes(gate_mine)
     gate_halves[0] = swap(gate_halves[0], "dp", 1 << top)
     grad_out_near = gather_whole(grad_out_own)
     projected = dot(hidden_one, qkv)
@@ -900,7 +902,13 @@
     grad_proj, qkv_term, inputs_low, activation_near = lax.optimization_barrier(
         (grad_proj, qkv_term, inputs_low, activations[0])
     )
-    qkv_term = lax.psum_scatter(qkv_term, "dp", scatter_dimension=0, tiled=True)
+    qkv_term = jnp.concatenate(
+        [
+            lax.psum_scatter(part, "dp", scatter_dimension=0, tiled=True)
+            for part in jnp.split(qkv_term, 2, axis=1)
+        ],
+        axis=1,
+    )
     if aligned:
         out_grad = qkv_term[:, 3 * local_width :].reshape(own_rows, width)
         qkv_term = qkv_term[:, : 3 * local_width]

time: 654 us -> 657 us (level)
    unnamed x308 -> x238, local copies, waits for them, and re-layouts: 45.7 us -> 41.2 us
  transfers between devices with their start and end apart: 99 -> 100, of which waited for: 50 -> 47; matrix products, arithmetic and copies ran while one was open for 21% -> 21% of each run, Pallas kernels for 11% -> 12%
where the time goes in v5:
time: 657 us; the launch traced here: 647 us
  waiting for transfers between devices  249 us (38%)
  starting transfers between devices  87.3 us (13%)
  local copies, waits for them, and re-layouts  81.9 us (12%)
  Pallas kernels  77.1 us (12%)
  matrix products  75.7 us (12%)
  other arithmetic  60.2 us (9%)
  between operations  16.4 us (2%)
    ppermute x91, waiting for transfers between devices, swap(): lax.ppermute(values, axis, [(i, i ^ bits) for i in range(lax.axis_size(ax...  229 us
    ppermute x91, starting transfers between devices, swap(): lax.ppermute(values, axis, [(i, i ^ bits) for i in range(lax.axis_size(ax...  86.1 us
    unnamed x238, local copies, waits for them, and re-layouts  41.2 us
    dot_general x7, matrix products, dot(): return jnp.dot(first, second, preferred_element_type=f32)  28.2 us
    dot_general x8, matrix products, contract_first(): lax.dot_general(first, second, (((0,), (0,)), ((), ())), preferred_elemen...  24 us
    dot_general x7, matrix products, contract_last(): lax.dot_general(first, second, (((1,), (1,)), ((), ())), preferred_elemen...  23.6 us
    all_gather x1, waiting for transfers between devices, body(): qkv = lax.all_gather(qkv_own, 'dp', axis=0, tiled=True)  19.3 us
    pallas_call x1, Pallas kernels, attention_backward(): pl.pallas_call(backward_kernel, grid=(pairs, seq_len // query_block), in_...  18.4 us
  transfers between devices with their start and end apart: 100, of which 47 were waited for; matrix products, arithmetic and copies ran while one was open for 21% of the time, Pallas kernels for 12%

profile of v5, /device:TPU:0, one launch (start us, length us, event | category | flops | bytes accessed | tf_op | source)
XLA Modules:
  0.0 647.4 jit_solution(13388136765568580477)
XLA Ops:
  55.3 7.1 %collective-permute-done.5 = bf16[2,64,2048]{2,1,0:T(8,128)(2,1)S(1)} collective-permute-done((bf16[2,64,2048]{2,1,0:T(8,128)(2,1)S(1)}, bf16[2,64,2048]{2,1,0:T(8,128)(2,1)S(1)}, u32[]{:S(2)}, u32[]{:S(2)}) %collective-permute-start.5) | collective-permute-done | bytes 524320 | tf_op jit(solution)/shard_map/ppermute | solution.py:489
  77.8 4.3 collective-permute-done.17.refs_3_
  83.1 14.7 %collective-permute-done.19.refs_5_ = bf16[144,1024]{1,0:T(8,128)(2,1)S(1)} collective-permute-done((bf16[144,1024]{1,0:T(8,128)(2,1)}, bf16[144,1024]{1,0:T(8,128)(2,1)S(1)}, u32[]{:S(2)}, u32[]{:S(2)}) %collective-permute-start.19) | collective-permute-done | bytes 294944 | tf_op jit(solution)/shard_map/ppermute | solution.py:489
  110.1 19.3 %all-gather.10.cloned.1.call-done.weight_ref = bf16[2048,768]{1,0:T(8,128)(2,1)} async-done(((bf16[512,768]{1,0:T(8,128)(2,1)}), bf16[2048,768]{1,0:T(8,128)(2,1)}) %all-gather.10.cloned.1.call-update) | async-done | bytes 3145744 | tf_op jit(solution)/shard_map/all_gather | solution.py:734
  131.4 6.1 fusion.91.query_ref.key_ref.value_ref
  137.6 17.7 %attention_forward.1 = (bf16[1024,256]{1,0:T(8,128)(2,1)S(1)}, bf16[1024,256]{1,0:T(8,128)(2,1)S(1)}, bf16[1024,256]{1,0:T(8,128)(2,1)S(1)}, bf16[1024,256]{1,0:T(8,128)(2,1)S(1)}, f32[4,1,1024]{2,1,0:T(1,128)S(1)}) custom-call(f32[1024,768]{1,0:T(8,128)S(1)} %fusion.91.query_ref.key_ref.value_ref, f32[1024,768]{1,0:T(8,128)S(1)} %fusion.91.query_ref.key_ref.value_ref, ...), custom_call_target="tpu_custom_call" | custom-call | tf_op jit(solution)/shard_map/attention_forward/pallas_call | solution.py:457
  158.8 8.4 %collective-permute-done.23 = bf16[512,1024]{1,0:T(8,128)(2,1)} collective-permute-done((bf16[512,1024]{1,0:T(8,128)(2,1)S(1)}, bf16[512,1024]{1,0:T(8,128)(2,1)}, u32[]{:S(2)}, u32[]{:S(2)}) %collective-permute-start.23) | collective-permute-done | bytes 1048608 | tf_op jit(solution)/shard_map/ppermute | solution.py:489
  170.7 4.5 collective-permute-done.25
  184.8 11.2 %collective-permute-done.26 = bf16[2,64,2048]{2,1,0:T(8,128)(2,1)} collective-permute-done((bf16[2,64,2048]{2,1,0:T(8,128)(2,1)}, bf16[2,64,2048]{2,1,0:T(8,128)(2,1)}, u32[]{:S(2)}, u32[]{:S(2)}) %collective-permute-start.26) | collective-permute-done | bytes 524320 | tf_op jit(solution)/shard_map/ppermute | solution.py:489
  200.9 7.3 %collective-permute-done.31 = bf16[256,1024]{1,0:T(8,128)(2,1)} collective-permute-done((bf16[256,1024]{1,0:T(8,128)(2,1)}, bf16[256,1024]{1,0:T(8,128)(2,1)}, u32[]{:S(2)}, u32[]{:S(2)}) %collective-permute-start.31) | collective-permute-done | bytes 524320 | tf_op jit(solution)/shard_map/ppermute | solution.py:489
  224.5 20.5 %collective-permute-done.32 = bf16[128,2048]{1,0:T(8,128)(2,1)} collective-permute-done((bf16[128,2048]{1,0:T(8,128)(2,1)}, bf16[128,2048]{1,0:T(8,128)(2,1)}, u32[]{:S(2)}, u32[]{:S(2)}) %collective-permute-start.32) | collective-permute-done | bytes 524320 | tf_op jit(solution)/shard_map/ppermute | solution.py:489
  246.1 10.2 %collective-permute-done.34 = bf16[128,2048]{1,0:T(8,128)(2,1)} collective-permute-done((bf16[128,2048]{1,0:T(8,128)(2,1)}, bf16[128,2048]{1,0:T(8,128)(2,1)}, u32[]{:S(2)}, u32[]{:S(2)}) %collective-permute-start.34) | collective-permute-done | bytes 524320 | tf_op jit(solution)/shard_map/ppermute | solution.py:489
  266.0 4.5 fusion.92.gate_ref
  292.3 11.9 %collective-permute-done.37 = bf16[2,64,2048]{2,1,0:T(8,128)(2,1)} collective-permute-done((bf16[2,64,2048]{2,1,0:T(8,128)(2,1)S(1)}, bf16[2,64,2048]{2,1,0:T(8,128)(2,1)}, u32[]{:S(2)}, u32[]{:S(2)}) %collective-permute-start.37) | collective-permute-done | bytes 524320 | tf_op jit(solution)/shard_map/ppermute | solution.py:489
  310.4 6.3 fusion.94.gate_ref
  327.4 4.5 collective-permute-done.41
  331.9 5.7 add_convert_fusion.4
  369.3 13.5 %collective-permute-done.47 = bf16[1,512,1024]{2,1,0:T(8,128)(2,1)S(1)} collective-permute-done((bf16[1,512,1024]{2,1,0:T(8,128)(2,1)S(1)}, bf16[1,512,1024]{2,1,0:T(8,128)(2,1)S(1)}, u32[]{:S(2)}, u32[]{:S(2)}) %collective-permute-start.47) | collective-permute-done | bytes 1048608 | tf_op jit(solution)/shard_map/ppermute | solution.py:489
  409.2 13.0 %collective-permute-done.51 = bf16[176,1024]{1,0:T(8,128)(2,1)S(1)} collective-permute-done((bf16[176,1024]{1,0:T(8,128)(2,1)S(1)}, bf16[176,1024]{1,0:T(8,128)(2,1)S(1)}, u32[]{:S(2)}, u32[]{:S(2)}) %collective-permute-start.51) | collective-permute-done | bytes 360480 | tf_op jit(solution)/shard_map/ppermute | solution.py:489
  426.9 8.1 %collective-permute-done.56 = bf16[1,80,2048]{2,1,0:T(8,128)(2,1)S(1)} collective-permute-done((bf16[1,80,2048]{2,1,0:T(8,128)(2,1)S(1)}, bf16[1,80,2048]{2,1,0:T(8,128)(2,1)S(1)}, u32[]{:S(2)}, u32[]{:S(2)}) %collective-permute-start.56) | collective-permute-done | bytes 327712 | tf_op jit(solution)/shard_map/ppermute | solution.py:489
  437.6 5.0 collective-permute-done.55
  444.2 4.7 convolution_convert_fusion.6.grad_ref
  465.0 18.4 %attention_backward.1 = (bf16[1024,256]{1,0:T(8,128)(2,1)S(1)}, bf16[1024,256]{1,0:T(8,128)(2,1)S(1)}, bf16[1024,256]{1,0:T(8,128)(2,1)S(1)}) custom-call(bf16[1024,256]{1,0:T(8,128)(2,1)S(1)} %copy-done.36, bf16[1024,256]{1,0:T(8,128)(2,1)S(1)} %copy-done.38, bf16[1024,256]{1,0:T(8,128)(2,1)S(1)} %copy-done.40, bf16[1024,256]{1,0:T(8,128)(2,1)S(1)} %copy-done.41, ...), custom_call_target="tpu_custom_call" | custom-call | tf_op jit(solution)/shard_map/attention_backward/pallas_call | solution.py:475
  520.9 6.3 collective-permute-done.61
  538.0 4.5 plain_step.1
  542.5 4.6 collective-permute-done.66
  549.9 4.5 core_product.7
  567.9 7.2 %collective-permute-done.78 = f32[2,4,2,64]{3,2,1,0:T(2,128)S(1)} collective-permute-done((f32[2,4,2,64]{3,2,1,0:T(2,128)S(1)}, f32[2,4,2,64]{3,2,1,0:T(2,128)S(1)}, u32[]{:S(2)}, u32[]{:S(2)}) %collective-permute-start.78) | collective-permute-done | bytes 4128 | tf_op jit(solution)/shard_map/ppermute | solution.py:489
  577.4 7.1 %collective-permute-done.68 = bf16[2,64,2048]{2,1,0:T(8,128)(2,1)S(1)} collective-permute-done((bf16[2,64,2048]{2,1,0:T(8,128)(2,1)S(1)}, bf16[2,64,2048]{2,1,0:T(8,128)(2,1)S(1)}, u32[]{:S(2)}, u32[]{:S(2)}) %collective-permute-start.68) | collective-permute-done | bytes 524320 | tf_op jit(solution)/shard_map/ppermute | solution.py:489
  588.5 9.9 %gate_step.1 = (f32[64,16384]{1,0:T(8,128)}, f32[64,16384]{1,0:T(8,128)}, f32[64,16384]{1,0:T(8,128)}, f32[64,16384]{1,0:T(8,128)}) custom-call(bf16[8,2,64,1024]{3,2,1,0:T(8,128)(2,1)S(1)} %bitcast.481, f32[64,16384]{1,0:T(8,128)S(1)} %copy-done.18, f32[64,16384]{1,0:T(8,128)S(1)} %copy-done.46, f32[64,16384]{1,0:T(8,128)} %refs_2_.3), custom_call_target="tpu_custom_call" | custom-call | flops 4294967296 | bytes 1048576 | tf_op jit(solution)/shard_map/gate_step/pallas_call | solution.py:264
  622.3 6.4 collective-permute-done.87
  635.3 4.8 attn_step.1
  (634 shorter events, 348.9 us)
Async XLA Ops:
  7.2 59.6 %all-gather.8.cloned.1.call-start = ((), (), s32[]{:S(2)}) async-start(), calls=%async_computation.2 | async-start | bytes 1310720 | tf_op jit(solution)/shard_map/all_gather | solution.py:726
  9.0 38.5 %collective-permute-start.1 = (bf16[64,2048]{1,0:T(8,128)(2,1)}, bf16[64,2048]{1,0:T(8,128)(2,1)}, u32[]{:S(2)}, u32[]{:S(2)}) collective-permute-start(bf16[64,2048]{1,0:T(8,128)(2,1)} %get-tuple-element.687), channel_id=1, source_target_pairs={{0,4},{1,5},{2,6},{3,7},{4,0},{5,1},{6,2},{7,3},{8,12},{9,13},{10,... | collective-permute-start | bytes 786440 | tf_op jit(solution)/shard_map/ppermute | solution.py:489
  12.0 35.6 %collective-permute-start = (bf16[64,2048]{1,0:T(8,128)(2,1)S(1)}, bf16[64,2048]{1,0:T(8,128)(2,1)}, u32[]{:S(2)}, u32[]{:S(2)}) collective-permute-start(bf16[64,2048]{1,0:T(8,128)(2,1)S(1)} %get-tuple-element.688), channel_id=1, source_target_pairs={{0,2},{1,3},{2,0},{3,1},{4,6},{5,7},{6,4},{7,5},{8,10},{9,11},{10,... | collective-permute-start | bytes 786440 | tf_op jit(solution)/shard_map/ppermute | solution.py:489
  15.9 113.5 %all-gather.10.cloned.1.call-start = ((), (), s32[]{:S(2)}) async-start(), calls=%async_computation.3 | async-start | bytes 3932160 | tf_op jit(solution)/shard_map/all_gather | solution.py:734
  44.8 25.5 %collective-permute-start.22 = (bf16[128,2048]{1,0:T(8,128)(2,1)}, bf16[128,2048]{1,0:T(8,128)(2,1)}, u32[]{:S(2)}, u32[]{:S(2)}) collective-permute-start(bf16[128,2048]{1,0:T(8,128)(2,1)} %bitcast.32), channel_id=1, source_target_pairs={{0,16},{8,24},{16,0},{24,8},{1,17},{9,25},{17,1},{25,9},{2,18},{10... | collective-permute-start | bytes 1572872 | tf_op jit(solution)/shard_map/ppermute | solution.py:489
  67.3 99.9 %all-gather.12.cloned.1.call-start = ((), (), s32[]{:S(2)}) async-start(), calls=%async_computation.4 | async-start | bytes 4718592 | tf_op jit(solution)/shard_map/all_gather | solution.py:550
  70.4 27.4 %collective-permute-start.19 = (bf16[144,1024]{1,0:T(8,128)(2,1)}, bf16[144,1024]{1,0:T(8,128)(2,1)S(1)}, u32[]{:S(2)}, u32[]{:S(2)}) collective-permute-start(bf16[144,1024]{1,0:T(8,128)(2,1)} %get-tuple-element.323), channel_id=1, source_target_pairs={{0,5},{1,4},{2,7},{3,6},{4,1},{5,0},{6,3},{7,2},{8,13},{9,12},{10,... | collective-permute-start | bytes 884744 | tf_op jit(solution)/shard_map/ppermute | solution.py:489
  71.7 26.1 %collective-permute-start.20 = (bf16[144,1024]{1,0:T(8,128)(2,1)}, bf16[144,1024]{1,0:T(8,128)(2,1)S(1)}, u32[]{:S(2)}, u32[]{:S(2)}) collective-permute-start(bf16[144,1024]{1,0:T(8,128)(2,1)} %get-tuple-element.324), channel_id=1, source_target_pairs={{0,6},{1,7},{2,4},{3,5},{4,2},{5,3},{6,0},{7,1},{8,14},{9,15},{10,... | collective-permute-start | bytes 884744 | tf_op jit(solution)/shard_map/ppermute | solution.py:489
  129.4 84.4 %all-gather.14.cloned.1.call-start = ((), (), s32[]{:S(2)}) async-start(), calls=%async_computation.5 | async-start | bytes 4718592 | tf_op jit(solution)/shard_map/all_gather | solution.py:550
  130.1 28.7 %collective-permute-start.24 = (bf16[256,1024]{1,0:T(8,128)(2,1)}, bf16[256,1024]{1,0:T(8,128)(2,1)}, u32[]{:S(2)}, u32[]{:S(2)}) collective-permute-start(bf16[256,1024]{1,0:T(8,128)(2,1)} %get-tuple-element.346), channel_id=1, source_target_pairs={{0,16},{8,24},{16,0},{24,8},{1,17},{9,25},{17,1},{25,9},{2,18},{10... | collective-permute-start | bytes 1572872 | tf_op jit(solution)/shard_map/ppermute | solution.py:489
  131.2 36.0 %collective-permute-start.23 = (bf16[512,1024]{1,0:T(8,128)(2,1)S(1)}, bf16[512,1024]{1,0:T(8,128)(2,1)}, u32[]{:S(2)}, u32[]{:S(2)}) collective-permute-start(bf16[512,1024]{1,0:T(8,128)(2,1)S(1)} %copy-done.61), channel_id=1, source_target_pairs={{0,8},{8,0},{16,24},{24,16},{1,9},{9,1},{17,25},{25,17},{2,10},{10... | collective-permute-start | bytes 3145736 | tf_op jit(solution)/shard_map/ppermute | solution.py:489
  167.2 89.1 %all-gather.16.cloned.1.call-start = ((), (), s32[]{:S(2)}) async-start(), calls=%async_computation.6 | async-start | bytes 4718592 | tf_op jit(solution)/shard_map/all_gather | solution.py:550
  182.5 25.8 %collective-permute-start.31 = (bf16[256,1024]{1,0:T(8,128)(2,1)}, bf16[256,1024]{1,0:T(8,128)(2,1)}, u32[]{:S(2)}, u32[]{:S(2)}) collective-permute-start(bf16[256,1024]{1,0:T(8,128)(2,1)} %get-tuple-element.356), channel_id=1, source_target_pairs={{0,16},{8,24},{16,0},{24,8},{1,17},{9,25},{17,1},{25,9},{2,18},{10... | collective-permute-start | bytes 1572872 | tf_op jit(solution)/shard_map/ppermute | solution.py:489
  183.3 24.9 %collective-permute-start.30 = (bf16[256,1024]{1,0:T(8,128)(2,1)}, bf16[256,1024]{1,0:T(8,128)(2,1)}, u32[]{:S(2)}, u32[]{:S(2)}) collective-permute-start(bf16[256,1024]{1,0:T(8,128)(2,1)} %collective-permute-done.24), channel_id=1, source_target_pairs={{0,8},{8,0},{16,24},{24,16},{1,9},{9,1},{17,25},{25,17},{2,10},{10... | collective-permute-start | bytes 1572872 | tf_op jit(solution)/shard_map/ppermute | solution.py:489
  218.3 87.1 %all-gather.18.cloned.1.call-start = ((), (), s32[]{:S(2)}) async-start(), calls=%async_computation.7 | async-start | bytes 4718592 | tf_op jit(solution)/shard_map/all_gather | solution.py:550
  218.3 26.7 %collective-permute-start.32 = (bf16[128,2048]{1,0:T(8,128)(2,1)}, bf16[128,2048]{1,0:T(8,128)(2,1)}, u32[]{:S(2)}, u32[]{:S(2)}) collective-permute-start(bf16[128,2048]{1,0:T(8,128)(2,1)} %multiply_convert_fusion), channel_id=1, source_target_pairs={{0,16},{8,24},{16,0},{24,8},{1,17},{9,25},{17,1},{25,9},{2,18},{10... | collective-permute-start | bytes 1572872 | tf_op jit(solution)/shard_map/ppermute | solution.py:489
  220.8 25.3 %collective-permute-start.33 = (bf16[256,1024]{1,0:T(8,128)(2,1)}, bf16[256,1024]{1,0:T(8,128)(2,1)}, u32[]{:S(2)}, u32[]{:S(2)}) collective-permute-start(bf16[256,1024]{1,0:T(8,128)(2,1)} %collective-permute-done.31), channel_id=1, source_target_pairs={{0,8},{8,0},{16,24},{24,16},{1,9},{9,1},{17,25},{25,17},{2,10},{10... | collective-permute-start | bytes 1572872 | tf_op jit(solution)/shard_map/ppermute | solution.py:489
  222.3 34.1 %collective-permute-start.34 = (bf16[128,2048]{1,0:T(8,128)(2,1)}, bf16[128,2048]{1,0:T(8,128)(2,1)}, u32[]{:S(2)}, u32[]{:S(2)}) collective-permute-start(bf16[128,2048]{1,0:T(8,128)(2,1)} %get-tuple-element.379), channel_id=1, source_target_pairs={{0,8},{8,0},{16,24},{24,16},{1,9},{9,1},{17,25},{25,17},{2,10},{10... | collective-permute-start | bytes 1572872 | tf_op jit(solution)/shard_map/ppermute | solution.py:489
  256.4 187.8 %all-gather.20.cloned.1.call-start = ((), (), s32[]{:S(2)}) async-start(), calls=%async_computation.8 | async-start | bytes 4718592 | tf_op jit(solution)/shard_map/all_gather | solution.py:550
  348.0 34.7 %collective-permute-start.47 = (bf16[1,512,1024]{2,1,0:T(8,128)(2,1)S(1)}, bf16[1,512,1024]{2,1,0:T(8,128)(2,1)S(1)}, u32[]{:S(2)}, u32[]{:S(2)}) collective-permute-start(bf16[1,512,1024]{2,1,0:T(8,128)(2,1)S(1)} %dynamic-slice_bitcast_fusion), channel_id=1, source_target_pairs={{0,8},{8,0},{16,24},{24,16},{1,9},{9,1},{17,25},{25,17},{2,10},{10... | collective-permute-start | bytes 3145736 | tf_op jit(solution)/shard_map/ppermute | solution.py:489
  363.6 23.8 %collective-permute-start.46 = (bf16[128,2048]{1,0:T(8,128)(2,1)S(1)}, bf16[128,2048]{1,0:T(8,128)(2,1)S(1)}, u32[]{:S(2)}, u32[]{:S(2)}) collective-permute-start(bf16[128,2048]{1,0:T(8,128)(2,1)S(1)} %pad_maximum_fusion.12), channel_id=1, source_target_pairs={{0,16},{8,24},{16,0},{24,8},{1,17},{9,25},{17,1},{25,9},{2,18},{10... | collective-permute-start | bytes 1572872 | tf_op jit(solution)/shard_map/ppermute | solution.py:489
  393.9 209.9 %reduce-scatter.5.cloned.1.call-start = ((), (), s32[]{:S(2)}) async-start(), calls=%async_computation.10 | async-start | bytes 2621440 | tf_op jit(solution)/shard_map/reduce_scatter | solution.py:907
  449.9 39.2 %collective-permute-start.57 = (bf16[1,512,1024]{2,1,0:T(8,128)(2,1)}, bf16[1,512,1024]{2,1,0:T(8,128)(2,1)}, u32[]{:S(2)}, u32[]{:S(2)}) collective-permute-start(bf16[1,512,1024]{2,1,0:T(8,128)(2,1)} %constant_dynamic-slice_fusion.11), channel_id=1, source_target_pairs={{0,8},{8,0},{16,24},{24,16},{1,9},{9,1},{17,25},{25,17},{2,10},{10... | collective-permute-start | bytes 3145736 | tf_op jit(solution)/shard_map/ppermute | solution.py:489
  451.0 36.2 %collective-permute-start.59 = (bf16[1,80,2048]{2,1,0:T(8,128)(2,1)}, bf16[1,80,2048]{2,1,0:T(8,128)(2,1)}, u32[]{:S(2)}, u32[]{:S(2)}) collective-permute-start(bf16[1,80,2048]{2,1,0:T(8,128)(2,1)} %constant_dynamic-slice_fusion.10), channel_id=1, source_target_pairs={{0,8},{8,0},{16,24},{24,16},{1,9},{9,1},{17,25},{25,17},{2,10},{10... | collective-permute-start | bytes 983048 | tf_op jit(solution)/shard_map/ppermute | solution.py:489
  452.7 39.2 %collective-permute-start.58 = (bf16[160,1024]{1,0:T(8,128)(2,1)}, bf16[160,1024]{1,0:T(8,128)(2,1)}, u32[]{:S(2)}, u32[]{:S(2)}) collective-permute-start(bf16[160,1024]{1,0:T(8,128)(2,1)} %split.62), channel_id=1, source_target_pairs={{0,16},{8,24},{16,0},{24,8},{1,17},{9,25},{17,1},{25,9},{2,18},{10... | collective-permute-start | bytes 983048 | tf_op jit(solution)/shard_map/ppermute | solution.py:489
  500.0 105.1 %reduce-scatter.3.cloned.1.call-start = ((), (), s32[]{:S(2)}) async-start(), calls=%async_computation.9 | async-start | bytes 2621440 | tf_op jit(solution)/shard_map/reduce_scatter | solution.py:907
  510.5 39.4 %collective-permute-start.72 = (bf16[512,2048]{1,0:T(8,128)(2,1)}, bf16[512,2048]{1,0:T(8,128)(2,1)}, u32[]{:S(2)}, u32[]{:S(2)}) collective-permute-start(bf16[512,2048]{1,0:T(8,128)(2,1)} %get-tuple-element.486), channel_id=1, source_target_pairs={{0,1},{1,0},{2,3},{3,2},{4,5},{5,4},{6,7},{7,6},{8,9},{9,8},{10,11... | collective-permute-start | bytes 6291464 | tf_op jit(solution)/shard_map/ppermute | solution.py:489
  517.6 42.8 %collective-permute-start.67 = (bf16[512,2048]{1,0:T(8,128)(2,1)}, bf16[512,2048]{1,0:T(8,128)(2,1)}, u32[]{:S(2)}, u32[]{:S(2)}) collective-permute-start(bf16[512,2048]{1,0:T(8,128)(2,1)} %core_product.4), channel_id=1, source_target_pairs={{0,1},{1,0},{2,3},{3,2},{4,5},{5,4},{6,7},{7,6},{8,9},{9,8},{10,11... | collective-permute-start | bytes 6291464 | tf_op jit(solution)/shard_map/ppermute | solution.py:489
  575.1 23.3 %collective-permute-start.79 = (f32[1,4,2,64]{3,2,1,0:T(2,128)S(1)}, f32[1,4,2,64]{3,2,1,0:T(2,128)S(1)}, u32[]{:S(2)}, u32[]{:S(2)}) collective-permute-start(f32[1,4,2,64]{3,2,1,0:T(2,128)S(1)} %constant_dynamic-slice_fusion.4), channel_id=1, source_target_pairs={{0,1},{1,0},{2,3},{3,2},{4,5},{5,4},{6,7},{7,6},{8,9},{9,8},{10,11... | collective-permute-start | bytes 6152 | tf_op jit(solution)/shard_map/ppermute | solution.py:489
  575.4 23.0 %collective-permute-start.75 = (bf16[64,2048]{1,0:T(8,128)(2,1)S(1)}, bf16[64,2048]{1,0:T(8,128)(2,1)S(1)}, u32[]{:S(2)}, u32[]{:S(2)}) collective-permute-start(bf16[64,2048]{1,0:T(8,128)(2,1)S(1)} %fusion.52), channel_id=1, source_target_pairs={{0,2},{1,3},{2,0},{3,1},{4,6},{5,7},{6,4},{7,5},{8,10},{9,11},{10,... | collective-permute-start | bytes 786440 | tf_op jit(solution)/shard_map/ppermute | solution.py:489
  576.0 22.4 %collective-permute-start.76 = (bf16[64,2048]{1,0:T(8,128)(2,1)S(1)}, bf16[64,2048]{1,0:T(8,128)(2,1)S(1)}, u32[]{:S(2)}, u32[]{:S(2)}) collective-permute-start(bf16[64,2048]{1,0:T(8,128)(2,1)S(1)} %fusion.53), channel_id=1, source_target_pairs={{0,4},{1,5},{2,6},{3,7},{4,0},{5,1},{6,2},{7,3},{8,12},{9,13},{10,... | collective-permute-start | bytes 786440 | tf_op jit(solution)/shard_map/ppermute | solution.py:489
  606.3 22.5 %collective-permute-start.87 = (bf16[128,2048]{1,0:T(8,128)(2,1)}, bf16[128,2048]{1,0:T(8,128)(2,1)}, u32[]{:S(2)}, u32[]{:S(2)}) collective-permute-start(bf16[128,2048]{1,0:T(8,128)(2,1)} %pad_maximum_fusion.7), channel_id=1, source_target_pairs={{0,16},{8,24},{16,0},{24,8},{1,17},{9,25},{17,1},{25,9},{2,18},{10... | collective-permute-start | bytes 1572872 | tf_op jit(solution)/shard_map/ppermute | solution.py:489
  (178 other events, 1371.6 us)
Sparse Core Ops, SparseCore 0:
  16.0 27.3 all-gather.7
  67.4 61.9 all-gather.9
  131.3 35.3 all-gather.11
  168.4 45.3 all-gather.13
  218.4 36.8 all-gather.15
  257.1 36.7 all-gather.17
  394.0 46.2 all-gather.19
  500.1 42.3 reduce-scatter.4
  545.5 43.1 reduce-scatter.2
